TPU v7x, 32 devices: a whole 2x2x4 slice. The times are simulated.
32 devices in a mesh: dp: 4 (over y, x), depth: 2 (over core), mp: 4 (over z).
Axes of the slice: x: 2, y: 2, z: 4, core: 2. Of those that a mesh axis runs over, the one named last changes fastest.
Arguments:
- tokens: bfloat16 [4096, 2048], P(('dp', 'depth')), may hold values from -6 to 6
- cotangent: bfloat16 [4096, 2048], P(('dp', 'depth')), may hold values from -6 to 6
- lengths: int32 [4, 2, 4], P('dp'), may hold values from 0 to 512, as said below
- bucket_loop_index: int32 [4, 2], P('dp'), may hold values from 0 to 1, as said below
- query_weight: bfloat16 [2048, 2048], P(('dp', 'depth'), 'mp'), may hold values from -0.125 to 0.125
- key_value_weight: bfloat16 [2048, 512], P(('dp', 'depth'), 'mp'), may hold values from -0.125 to 0.125
- output_weight: bfloat16 [2048, 2048], P('mp', ('dp', 'depth')), may hold values from -0.5 to 0.5
- gate_up_weight: bfloat16 [2, 2048, 16384], P(None, ('dp', 'depth'), 'mp'), may hold values from -0.125 to 0.125
- down_weight: bfloat16 [16384, 2048], P('mp', ('dp', 'depth')), may hold values from -0.046875 to 0.046875
- gains: bfloat16 [2, 2048], P(None, ('dp', 'depth')), may hold values from 0.5 to 1.5
- adapter_input_down: bfloat16 [2, 5, 2048, 256], P('depth', None, 'dp'), may hold values from -0.125 to 0.125
- adapter_query_up: bfloat16 [2, 256, 2048], P('depth', 'dp', 'mp'), may hold values from -0.375 to 0.375
- adapter_key_value: bfloat16 [2, 256, 512], P('depth', 'dp', 'mp'), may hold values from -0.375 to 0.375
- adapter_output_down: bfloat16 [2, 256, 2048], P('depth', 'dp', 'mp'), may hold values from -0.5 to 0.5
- adapter_hidden_down: bfloat16 [2, 256, 16384], P('depth', 'dp', 'mp'), may hold values from -0.046875 to 0.046875
- adapter_model_up: bfloat16 [2, 2, 256, 2048], P('depth', None, 'dp'), may hold values from -0.375 to 0.375
- adapter_gate_up: bfloat16 [2, 2, 256, 16384], P('depth', None, 'dp', 'mp'), may hold values from -0.375 to 0.375
Outputs:
- mixed_rows: bfloat16 [4096, 2048], P(('dp', 'depth'))
- grad_tokens: bfloat16 [4096, 2048], P(('dp', 'depth'))
- grad_w_query: float32 [2048, 2048], P(('dp', 'depth'), 'mp')
- grad_w_keyval: float32 [2048, 512], P(('dp', 'depth'), 'mp')
- grad_w_output: float32 [2048, 2048], P('mp', ('dp', 'depth'))
- grad_w_gateup: float32 [2, 2048, 16384], P(None, ('dp', 'depth'), 'mp')
- grad_w_down: float32 [16384, 2048], P('mp', ('dp', 'depth'))
- grad_gains: float32 [2, 2048], P(None, ('dp', 'depth'))
- grad_lora_in: float32 [2, 5, 2048, 256], P('depth', None, 'dp')
- grad_lora_query: float32 [2, 256, 2048], P('depth', 'dp', 'mp')
- grad_lora_keyval: float32 [2, 256, 512], P('depth', 'dp', 'mp')
- grad_lora_out: float32 [2, 256, 2048], P('depth', 'dp', 'mp')
- grad_lora_hidden: float32 [2, 256, 16384], P('depth', 'dp', 'mp')
- grad_lora_model: float32 [2, 2, 256, 2048], P('depth', None, 'dp')
- grad_lora_gateup: float32 [2, 2, 256, 16384], P('depth', None, 'dp', 'mp')
Inputs may be any that keep to these rules, and one draw needn't show every extreme that they name: The 4 entries of a bucket are the lengths of the sequences packed into it, in order; 0 marks an unused slot and every used length is at least 64; they sum to at most 512 and to at least half of it; in every draw some bucket holds a single sequence of 512 rows. `bucket_loop_index`: the 2 buckets of one dp index belong to different loops; in some dp index the bucket of depth 0 is of loop 1, and in another of loop 0.
All inputs are finite; a program needn't handle non-finite values.
Results may differ from a plain program's by a relative error of at most 0.025.
Values may be sent and summed in bfloat16 or wider, within the bound.
No kernel may reach another device: no remote copies, remote signals or barrier semaphores. Data moves between devices by JAX's collectives and lax.ppermute only.
A program may use at most 256 MiB of HBM per device.

v0:
```python
import jax
import jax.numpy as jnp
from jax import lax
from jax.sharding import PartitionSpec as P

HEAD_SIZE = 256


EPS = 1e-06
THETA = 10000.0
NEGATIVE = -1e30


def from_partner(block, axis, bit):
    count = lax.axis_size(axis)
    route = []
    for low in range(count):
        high = low | 1 << bit
        if high != low and high < count:
            route += [(low, high), (high, low)]
    return lax.ppermute(block, axis, route)


def product(left_op, right_op, left_dim, right_dim):
    return lax.dot_general(
        left_op,
        right_op,
        (((left_dim,), (right_dim,)), ((), ())),
        preferred_element_type=jnp.float32,
    )


def layout(seq_lens, row_count):
    seq_ends = jnp.cumsum(seq_lens)
    places = jnp.arange(row_count, dtype=jnp.int32)
    passed = (places[:, None] >= seq_ends[None, :]).astype(jnp.int32)
    segment = jnp.sum(passed, axis=1)
    starts = jnp.sum(passed * seq_lens[None, :], axis=1)
    valid_rows = (places < seq_ends[-1]).astype(jnp.float32)
    within = (places - starts).astype(jnp.float32)
    return (places, segment, within, valid_rows)


def rotary(within, head_width):
    half_width = head_width // 2
    frequency = THETA ** (-2.0 * jnp.arange(half_width, dtype=jnp.float32) / head_width)
    angles = within[:, None] * frequency[None, :]
    return (jnp.cos(angles), jnp.sin(angles))


def rotate(vector, cosine, sine_part):
    half_width = vector.shape[-1] // 2
    former = vector[..., :half_width]
    latter = vector[..., half_width:]
    return jnp.concatenate(
        [former * cosine - latter * sine_part, latter * cosine + former * sine_part], axis=-1
    )


def rotate_back(vector, cosine, sine_part):
    half_width = vector.shape[-1] // 2
    former = vector[..., :half_width]
    latter = vector[..., half_width:]
    return jnp.concatenate(
        [former * cosine + latter * sine_part, latter * cosine - former * sine_part], axis=-1
    )


def rms_forward(values, gain_row):
    inverse = lax.rsqrt(jnp.mean(values * values, axis=-1, keepdims=True) + EPS)
    return (values * inverse * gain_row, inverse)


def rms_backward(values, inverse, gain_row, grad_norm):
    weighted = grad_norm * gain_row
    grad_values = inverse * weighted - values * inverse**3 * jnp.mean(
        weighted * values, axis=-1, keepdims=True
    )
    grad_gain = jnp.sum(grad_norm * values * inverse, axis=0)
    return (grad_values, grad_gain)


def gelu_tanh(values):
    return jax.nn.gelu(values, approximate=True)


def block_mask(places, segment):
    return (segment[:, None] == segment[None, :]) & (places[None, :] <= places[:, None])


def attend(query_rows, key_rows, value_rows, places, segment, factor):
    row_count = query_rows.shape[0]
    block_rows = min(512, row_count)

    def one_block(block_id):
        allowed = block_mask(places, segment)
        scores = (
            jnp.einsum("qhd,kd->hqk", query_rows, key_rows, preferred_element_type=jnp.float32)
            * factor
        )
        scores = jnp.where(allowed[None], scores, NEGATIVE)
        row_peak = jnp.max(scores, axis=-1, keepdims=True)
        powers = jnp.exp(scores - row_peak)
        row_total = jnp.sum(powers, axis=-1, keepdims=True)
        attn_weights = (powers / row_total).astype(jnp.bfloat16)
        block_out = jnp.einsum(
            "hqk,kd->qhd", attn_weights, value_rows, preferred_element_type=jnp.float32
        )
        return (block_out, (row_peak + jnp.log(row_total))[..., 0])

    outputs, logsum = lax.map(one_block, jnp.arange(row_count // block_rows))
    return (outputs.reshape(query_rows.shape), logsum)


def attend_back(query_rows, key_rows, value_rows, places, segment, factor, logsum, grad_att):
    row_count = query_rows.shape[0]
    block_rows = min(512, row_count)

    def one_block(carry, block_id):
        grad_keys, grad_values = carry
        allowed = block_mask(places, segment)
        scores = (
            jnp.einsum("qhd,kd->hqk", query_rows, key_rows, preferred_element_type=jnp.float32)
            * factor
        )
        scores = jnp.where(allowed[None], scores, NEGATIVE)
        attn_probs = jnp.exp(scores - logsum[block_id][..., None])
        attn_weights = attn_probs.astype(jnp.bfloat16)
        grad_probs = jnp.einsum(
            "qhd,kd->hqk", grad_att, value_rows, preferred_element_type=jnp.float32
        )
        grad_values = grad_values + jnp.einsum(
            "hqk,qhd->kd", attn_weights, grad_att, preferred_element_type=jnp.float32
        )
        centre = jnp.sum(grad_probs * attn_probs, axis=-1, keepdims=True)
        grad_scores = (attn_probs * (grad_probs - centre)).astype(jnp.bfloat16)
        grad_query = (
            jnp.einsum("hqk,kd->qhd", grad_scores, key_rows, preferred_element_type=jnp.float32)
            * factor
        )
        grad_keys = (
            grad_keys
            + jnp.einsum("hqk,qhd->kd", grad_scores, query_rows, preferred_element_type=jnp.float32)
            * factor
        )
        return ((grad_keys, grad_values), grad_query)

    zero_rows = jnp.zeros(key_rows.shape, jnp.float32)
    (grad_keys, grad_values), grad_query = lax.scan(
        one_block, (zero_rows, zero_rows), jnp.arange(row_count // block_rows)
    )
    return (grad_query.reshape(query_rows.shape), grad_keys, grad_values)


def layer_pass(tok_rows, grad_rows, seq_lens, base_weights, loop_adapters, mp_index):
    query_weight, key_value_weight, output_weight, gate_up_weight, down_weight, gains = base_weights
    (
        adapter_input,
        query_lifted,
        key_value_lifted,
        output_down_adapter,
        hidden_down_adapter,
        model_lifted,
        gate_up_lifted,
    ) = loop_adapters
    row_count = tok_rows.shape[0]
    heads_here = query_weight.shape[1] // HEAD_SIZE
    kv_width = key_value_weight.shape[1]
    places, segment, within, valid_rows = layout(seq_lens, row_count)
    cosine, sine_part = rotary(within, HEAD_SIZE)
    head_cos = cosine[:, None, :]
    head_sin = sine_part[:, None, :]
    factor = HEAD_SIZE ** (-0.5)
    gain_one = gains[0].astype(jnp.float32)
    gain_two = gains[1].astype(jnp.float32)
    source = tok_rows.astype(jnp.float32)
    norm_one, inverse_one = rms_forward(source, gain_one)
    normalized_rows = norm_one.astype(jnp.bfloat16)
    rank_query_key_value = jnp.einsum(
        "bd,kdr->kbr", normalized_rows, adapter_input[:3], preferred_element_type=jnp.float32
    ).astype(jnp.bfloat16)
    query_raw = jnp.dot(
        normalized_rows, query_weight, preferred_element_type=jnp.float32
    ) + jnp.dot(rank_query_key_value[0], query_lifted, preferred_element_type=jnp.float32)
    query_rows = rotate(
        query_raw.reshape(row_count, heads_here, HEAD_SIZE), head_cos, head_sin
    ).astype(jnp.bfloat16)
    is_key = mp_index * kv_width < HEAD_SIZE
    rank_pick = jnp.where(is_key, rank_query_key_value[1], rank_query_key_value[2])
    joint_part = (
        jnp.dot(normalized_rows, key_value_weight, preferred_element_type=jnp.float32)
        + jnp.dot(rank_pick, key_value_lifted, preferred_element_type=jnp.float32)
    ).astype(jnp.bfloat16)
    joint_key_value = lax.all_gather(joint_part, "mp", axis=1, tiled=True)
    key_rows = rotate(joint_key_value[:, :HEAD_SIZE].astype(jnp.float32), cosine, sine_part).astype(
        jnp.bfloat16
    )
    value_rows = joint_key_value[:, HEAD_SIZE:]
    attended, logsum = attend(query_rows, key_rows, value_rows, places, segment, factor)
    flat_heads = attended.reshape(row_count, heads_here * HEAD_SIZE).astype(jnp.bfloat16)
    branch_part = jnp.dot(flat_heads, output_weight, preferred_element_type=jnp.float32)
    rank_part = product(flat_heads, output_down_adapter, 1, 1)
    branch_sum, rank_sum = (
        lax.psum(branch_part.astype(jnp.bfloat16), "mp").astype(jnp.float32),
        lax.psum(rank_part.astype(jnp.bfloat16), "mp").astype(jnp.float32),
    )
    rank_out = rank_sum.astype(jnp.bfloat16)
    hidden_state = (
        source + branch_sum + jnp.dot(rank_out, model_lifted[0], preferred_element_type=jnp.float32)
    )
    norm_two, inverse_two = rms_forward(hidden_state, gain_two)
    normed_two = norm_two.astype(jnp.bfloat16)
    rank_gu = jnp.einsum(
        "bd,kdr->kbr", normed_two, adapter_input[3:], preferred_element_type=jnp.float32
    ).astype(jnp.bfloat16)
    gate_rows = jnp.dot(
        normed_two, gate_up_weight[0], preferred_element_type=jnp.float32
    ) + jnp.dot(rank_gu[0], gate_up_lifted[0], preferred_element_type=jnp.float32)
    up_rows = jnp.dot(normed_two, gate_up_weight[1], preferred_element_type=jnp.float32) + jnp.dot(
        rank_gu[1], gate_up_lifted[1], preferred_element_type=jnp.float32
    )
    active, gelu_pull = jax.vjp(gelu_tanh, gate_rows)
    gated_rows = (active * up_rows).astype(jnp.bfloat16)
    ffn_part = jnp.dot(gated_rows, down_weight, preferred_element_type=jnp.float32)
    rank_down_part = product(gated_rows, hidden_down_adapter, 1, 1)
    ffn_sum, rank_down_sum = (
        lax.psum(ffn_part.astype(jnp.bfloat16), "mp").astype(jnp.float32),
        lax.psum(rank_down_part.astype(jnp.bfloat16), "mp").astype(jnp.float32),
    )
    rank_down = rank_down_sum.astype(jnp.bfloat16)
    output = (
        hidden_state
        + ffn_sum
        + jnp.dot(rank_down, model_lifted[1], preferred_element_type=jnp.float32)
    )
    result_rows = output.astype(jnp.bfloat16)
    grad_out = grad_rows.astype(jnp.float32) * valid_rows[:, None]
    grad_ffn = grad_out.astype(jnp.bfloat16)
    grad_rank_down = product(grad_ffn, model_lifted[1], 1, 1).astype(jnp.bfloat16)
    grad_gated = product(grad_ffn, down_weight, 1, 1) + jnp.dot(
        grad_rank_down, hidden_down_adapter, preferred_element_type=jnp.float32
    )
    grad_down_hidden = product(grad_rank_down, gated_rows, 0, 0)
    grad_w_down = product(gated_rows, grad_ffn, 0, 0)
    grad_up_down = product(rank_down, grad_ffn, 0, 0)
    grad_gate = gelu_pull(grad_gated * up_rows)[0].astype(jnp.bfloat16)
    grad_upper = (grad_gated * active).astype(jnp.bfloat16)
    grad_w_gateup = jnp.stack(
        [product(normed_two, grad_gate, 0, 0), product(normed_two, grad_upper, 0, 0)]
    )
    grad_up_gateup = jnp.stack(
        [product(rank_gu[0], grad_gate, 0, 0), product(rank_gu[1], grad_upper, 0, 0)]
    )
    grad_norm_part = product(grad_gate, gate_up_weight[0], 1, 1) + product(
        grad_upper, gate_up_weight[1], 1, 1
    )
    grad_rank_part = jnp.stack(
        [product(grad_gate, gate_up_lifted[0], 1, 1), product(grad_upper, gate_up_lifted[1], 1, 1)]
    )
    grad_norm_two, grad_rank_gu = (
        lax.psum(grad_norm_part.astype(jnp.bfloat16), "mp").astype(jnp.float32),
        lax.psum(grad_rank_part.astype(jnp.bfloat16), "mp").astype(jnp.float32),
    )
    grad_rank_gu = grad_rank_gu.astype(jnp.bfloat16)
    grad_adapt_gu = jnp.einsum(
        "bd,kbr->kdr", normed_two, grad_rank_gu, preferred_element_type=jnp.float32
    )
    grad_norm_two = grad_norm_two + jnp.einsum(
        "kbr,kdr->bd", grad_rank_gu, adapter_input[3:], preferred_element_type=jnp.float32
    )
    grad_hidden, grad_gain_two = rms_backward(hidden_state, inverse_two, gain_two, grad_norm_two)
    grad_hidden = grad_hidden + grad_out
    grad_branch = grad_hidden.astype(jnp.bfloat16)
    grad_rank_out = product(grad_branch, model_lifted[0], 1, 1).astype(jnp.bfloat16)
    grad_flat = product(grad_branch, output_weight, 1, 1) + jnp.dot(
        grad_rank_out, output_down_adapter, preferred_element_type=jnp.float32
    )
    grad_down_out = product(grad_rank_out, flat_heads, 0, 0)
    grad_w_output = product(flat_heads, grad_branch, 0, 0)
    grad_up_out = product(rank_out, grad_branch, 0, 0)
    grad_att = grad_flat.astype(jnp.bfloat16).reshape(row_count, heads_here, HEAD_SIZE)
    grad_query, grad_keys, grad_values = attend_back(
        query_rows, key_rows, value_rows, places, segment, factor, logsum, grad_att
    )
    grad_query = (
        rotate_back(grad_query, head_cos, head_sin)
        .reshape(row_count, heads_here * HEAD_SIZE)
        .astype(jnp.bfloat16)
    )
    grad_joint_all = jnp.concatenate(
        [rotate_back(grad_keys, cosine, sine_part), grad_values], axis=1
    )
    grad_joint = lax.psum_scatter(
        grad_joint_all.astype(jnp.bfloat16), "mp", scatter_dimension=1, tiled=True
    )
    grad_w_query = product(normalized_rows, grad_query, 0, 0)
    grad_up_query = product(rank_query_key_value[0], grad_query, 0, 0)
    grad_w_keyval = product(normalized_rows, grad_joint, 0, 0)
    grad_up_keyval = product(rank_pick, grad_joint, 0, 0)
    grad_pick = product(grad_joint, key_value_lifted, 1, 1)
    zero_rank = jnp.zeros_like(grad_pick)
    grad_rank_part = jnp.stack(
        [
            product(grad_query, query_lifted, 1, 1),
            jnp.where(is_key, grad_pick, zero_rank),
            jnp.where(is_key, zero_rank, grad_pick),
        ]
    )
    grad_norm_part = product(grad_query, query_weight, 1, 1) + product(
        grad_joint, key_value_weight, 1, 1
    )
    grad_norm_one, grad_rank_qkv = (
        lax.psum(grad_norm_part.astype(jnp.bfloat16), "mp").astype(jnp.float32),
        lax.psum(grad_rank_part.astype(jnp.bfloat16), "mp").astype(jnp.float32),
    )
    grad_rank_qkv = grad_rank_qkv.astype(jnp.bfloat16)
    grad_adapt_qkv = jnp.einsum(
        "bd,kbr->kdr", normalized_rows, grad_rank_qkv, preferred_element_type=jnp.float32
    )
    grad_norm_one = grad_norm_one + jnp.einsum(
        "kbr,kdr->bd", grad_rank_qkv, adapter_input[:3], preferred_element_type=jnp.float32
    )
    grad_source, grad_gain_one = rms_backward(source, inverse_one, gain_one, grad_norm_one)
    grad_input = (grad_source + grad_hidden).astype(jnp.bfloat16)
    base_grads = (
        grad_w_query,
        grad_w_keyval,
        grad_w_output,
        grad_w_gateup,
        grad_w_down,
        jnp.stack([grad_gain_one, grad_gain_two]),
    )
    adapt_grads = (
        jnp.concatenate([grad_adapt_qkv, grad_adapt_gu], axis=0),
        grad_up_query,
        grad_up_keyval,
        grad_down_out,
        grad_down_hidden,
        jnp.stack([grad_up_out, grad_up_down]),
        grad_up_gateup,
    )
    return (result_rows, grad_input, base_grads, adapt_grads)


def local(
    tokens,
    cotangent,
    lengths,
    bucket_loop_index,
    query_weight,
    key_value_weight,
    output_weight,
    gate_up_weight,
    down_weight,
    gains,
    adapter_input_down,
    adapter_query_up,
    adapter_key_value,
    adapter_output_down,
    adapter_hidden_down,
    adapter_model_up,
    adapter_gate_up,
):
    base_weights = (
        lax.all_gather(query_weight, ("dp", "depth"), axis=0, tiled=True),
        lax.all_gather(key_value_weight, ("dp", "depth"), axis=0, tiled=True),
        lax.all_gather(output_weight, ("dp", "depth"), axis=1, tiled=True),
        lax.all_gather(gate_up_weight, ("dp", "depth"), axis=1, tiled=True),
        lax.all_gather(down_weight, ("dp", "depth"), axis=1, tiled=True),
        lax.all_gather(gains, ("dp", "depth"), axis=1, tiled=True),
    )
    adapters_all = (
        lax.all_gather(adapter_input_down, "dp", axis=2, tiled=True),
        lax.all_gather(adapter_query_up, "dp", axis=1, tiled=True),
        lax.all_gather(adapter_key_value, "dp", axis=1, tiled=True),
        lax.all_gather(adapter_output_down, "dp", axis=1, tiled=True),
        lax.all_gather(adapter_hidden_down, "dp", axis=1, tiled=True),
        lax.all_gather(adapter_model_up, "dp", axis=2, tiled=True),
        lax.all_gather(adapter_gate_up, "dp", axis=2, tiled=True),
    )
    loop_adapters = tuple((adapter_table[0] for adapter_table in adapters_all))
    depth_id = lax.axis_index("depth")
    mp_index = lax.axis_index("mp")
    keep_own = bucket_loop_index[0, depth_id] == depth_id
    partner = from_partner((tokens, cotangent), "depth", 0)
    tok_rows = jnp.where(keep_own, tokens, partner[0])
    grad_rows = jnp.where(keep_own, cotangent, partner[1])
    slot_id = jnp.where(keep_own, depth_id, 1 - depth_id)
    seq_lens = lengths[0, slot_id]
    result_rows, grad_input, base_grads, adapt_grads = layer_pass(
        tok_rows, grad_rows, seq_lens, base_weights, loop_adapters, mp_index
    )
    returned = from_partner((result_rows, grad_input), "depth", 0)
    mixed_rows = jnp.where(keep_own, result_rows, returned[0])
    grad_tokens = jnp.where(keep_own, grad_input, returned[1])
    group_sums = (
        lax.psum_scatter(
            base_grads[0].astype(jnp.bfloat16), "dp", scatter_dimension=0, tiled=True
        ).astype(jnp.float32),
        lax.psum_scatter(
            base_grads[1].astype(jnp.bfloat16), "dp", scatter_dimension=0, tiled=True
        ).astype(jnp.float32),
        lax.psum_scatter(
            base_grads[2].astype(jnp.bfloat16), "dp", scatter_dimension=1, tiled=True
        ).astype(jnp.float32),
        lax.psum_scatter(
            base_grads[3].astype(jnp.bfloat16), "dp", scatter_dimension=1, tiled=True
        ).astype(jnp.float32),
        lax.psum_scatter(
            base_grads[4].astype(jnp.bfloat16), "dp", scatter_dimension=1, tiled=True
        ).astype(jnp.float32),
        lax.psum_scatter(
            base_grads[5].astype(jnp.bfloat16), "dp", scatter_dimension=1, tiled=True
        ).astype(jnp.float32),
    )
    weight_grads = (
        lax.psum_scatter(
            group_sums[0].astype(jnp.bfloat16), "depth", scatter_dimension=0, tiled=True
        ).astype(jnp.float32),
        lax.psum_scatter(
            group_sums[1].astype(jnp.bfloat16), "depth", scatter_dimension=0, tiled=True
        ).astype(jnp.float32),
        lax.psum_scatter(
            group_sums[2].astype(jnp.bfloat16), "depth", scatter_dimension=1, tiled=True
        ).astype(jnp.float32),
        lax.psum_scatter(
            group_sums[3].astype(jnp.bfloat16), "depth", scatter_dimension=1, tiled=True
        ).astype(jnp.float32),
        lax.psum_scatter(
            group_sums[4].astype(jnp.bfloat16), "depth", scatter_dimension=1, tiled=True
        ).astype(jnp.float32),
        lax.psum_scatter(
            group_sums[5].astype(jnp.bfloat16), "depth", scatter_dimension=1, tiled=True
        ).astype(jnp.float32),
    )
    adapter_grads = (
        lax.psum_scatter(
            adapt_grads[0][None].astype(jnp.bfloat16), "dp", scatter_dimension=2, tiled=True
        ).astype(jnp.float32),
        lax.psum_scatter(
            adapt_grads[1][None].astype(jnp.bfloat16), "dp", scatter_dimension=1, tiled=True
        ).astype(jnp.float32),
        lax.psum_scatter(
            adapt_grads[2][None].astype(jnp.bfloat16), "dp", scatter_dimension=1, tiled=True
        ).astype(jnp.float32),
        lax.psum_scatter(
            adapt_grads[3][None].astype(jnp.bfloat16), "dp", scatter_dimension=1, tiled=True
        ).astype(jnp.float32),
        lax.psum_scatter(
            adapt_grads[4][None].astype(jnp.bfloat16), "dp", scatter_dimension=1, tiled=True
        ).astype(jnp.float32),
        lax.psum_scatter(
            adapt_grads[5][None].astype(jnp.bfloat16), "dp", scatter_dimension=2, tiled=True
        ).astype(jnp.float32),
        lax.psum_scatter(
            adapt_grads[6][None].astype(jnp.bfloat16), "dp", scatter_dimension=2, tiled=True
        ).astype(jnp.float32),
    )
    return (mixed_rows, grad_tokens) + tuple(weight_grads) + tuple(adapter_grads)


def solution(mesh):
    return jax.shard_map(
        local,
        mesh=mesh,
        in_specs=(
            P(("dp", "depth"), None),
            P(("dp", "depth"), None),
            P("dp", None, None),
            P("dp", None),
            P(("dp", "depth"), "mp"),
            P(("dp", "depth"), "mp"),
            P("mp", ("dp", "depth")),
            P(None, ("dp", "depth"), "mp"),
            P("mp", ("dp", "depth")),
            P(None, ("dp", "depth")),
            P("depth", None, "dp", None),
            P("depth", "dp", "mp"),
            P("depth", "dp", "mp"),
            P("depth", "dp", "mp"),
            P("depth", "dp", "mp"),
            P("depth", None, "dp", None),
            P("depth", None, "dp", "mp"),
        ),
        out_specs=(
            P(("dp", "depth"), None),
            P(("dp", "depth"), None),
            P(("dp", "depth"), "mp"),
            P(("dp", "depth"), "mp"),
            P("mp", ("dp", "depth")),
            P(None, ("dp", "depth"), "mp"),
            P("mp", ("dp", "depth")),
            P(None, ("dp", "depth")),
            P("depth", None, "dp", None),
            P("depth", "dp", "mp"),
            P("depth", "dp", "mp"),
            P("depth", "dp", "mp"),
            P("depth", "dp", "mp"),
            P("depth", None, "dp", None),
            P("depth", None, "dp", "mp"),
        ),
        check_vma=False,
    )
```

profile of v0, /device:TPU:0, one launch (start us, length us, event | category | flops | bytes accessed | tf_op | source)
XLA Modules:
  0.0 1977.7 jit_solution(13108572549614486945)
XLA Ops:
  84.7 23.8 %all-gather.11.cloned.1.call-done = bf16[2048,512]{1,0:T(8,128)(2,1)} async-done(((bf16[256,512]{1,0:T(8,128)(2,1)}), bf16[2048,512]{1,0:T(8,128)(2,1)}) %all-gather.11.cloned.1.call-update) | async-done | bytes 2097168 | tf_op jit(solution)/shard_map/all_gather | solution.py:365
  119.4 15.3 all_gather.46
  156.1 19.7 all-gather.15.cloned.1.call-done
  178.4 34.4 %all-gather.23.cloned.1.call-done = bf16[1,256,4096]{2,1,0:T(8,128)(2,1)} async-done(((bf16[1,64,4096]{2,1,0:T(8,128)(2,1)}), bf16[1,256,4096]{2,1,0:T(8,128)(2,1)}) %all-gather.23.cloned.1.call-update) | async-done | bytes 2097168 | tf_op jit(solution)/shard_map/all_gather | solution.py:377
  219.6 92.7 %all-reduce.11.cloned.1.call-done = (bf16[512,2048]{1,0:T(8,128)(2,1)}, bf16[512,256]{1,0:T(8,128)(2,1)}) async-done(((bf16[512,2048]{1,0:T(8,128)(2,1)}, bf16[512,256]{1,0:T(8,128)(2,1)}), (bf16[512,2048]{1,0:T(8,128)(2,1)}, bf16[512,256]{1,0:T(8,128)(2,1)})) %all-reduce.11.cloned.1.call-update) | async-done | bytes 2359312 | tf_op jit(solution)/shard_map/psum | solution.py:204
  321.7 152.3 %all-gather.17.cloned.1.call-done = bf16[2,2048,4096]{2,1,0:T(8,128)(2,1)} async-done(((bf16[2,256,4096]{2,1,0:T(8,128)(2,1)}), bf16[2,2048,4096]{2,1,0:T(8,128)(2,1)}) %all-gather.17.cloned.1.call-update) | async-done | bytes 33554448 | tf_op jit(solution)/shard_map/all_gather | solution.py:368
  488.5 40.1 %all-gather.19.cloned.1.call-done = bf16[1,2,256,4096]{3,2,1,0:T(8,128)(2,1)} async-done(((bf16[1,2,64,4096]{3,2,1,0:T(8,128)(2,1)}), bf16[1,2,256,4096]{3,2,1,0:T(8,128)(2,1)}) %all-gather.19.cloned.1.call-update) | async-done | bytes 4194320 | tf_op jit(solution)/shard_map/all_gather | solution.py:379
  554.7 68.9 %all-gather.21.cloned.1.call-done = bf16[4096,2048]{1,0:T(8,128)(2,1)} async-done(((bf16[4096,256]{1,0:T(8,128)(2,1)}), bf16[4096,2048]{1,0:T(8,128)(2,1)}) %all-gather.21.cloned.1.call-update) | async-done | bytes 16777232 | tf_op jit(solution)/shard_map/all_gather | solution.py:369
  623.6 26.2 %multiply_convert_fusion.1 = (bf16[512,4096]{1,0:T(8,128)(2,1)}, bf16[512,4096]{1,0:T(8,128)(2,1)}, bf16[512,4096]{1,0:T(8,128)(2,1)}) fusion(f32[512,4096]{1,0:T(8,128)} %convolution_add_fusion.1, f32[512,4096]{1,0:T(8,128)} %convolution_add_fusion.2, f32[512,4096]{1,0:T(8,128)} %fusion.34, bf16[512,2048]{1,0:T(8,128)(2,1)S(1)} %copy-done.13, ...), kind=kOutput, calls=%fused_computation.26 | convolution fusion | flops 8646557696 | bytes 56623104 | tf_op jit(solution)/shard_map/dot_general | solution.py:25
  704.1 85.9 %all-reduce.9.cloned.1.call-done = (bf16[2,512,256]{2,1,0:T(8,128)(2,1)}, bf16[512,2048]{1,0:T(8,128)(2,1)}) async-done(((bf16[2,512,256]{2,1,0:T(8,128)(2,1)}, bf16[512,2048]{1,0:T(8,128)(2,1)}), (bf16[2,512,256]{2,1,0:T(8,128)(2,1)}, bf16[512,2048]{1,0:T(8,128)(2,1)})) %all-reduce.9.cloned.1.call-update) | async-done | bytes 2621456 | tf_op jit(solution)/shard_map/psum | solution.py:262
  847.5 176.4 %all-reduce.7.cloned.1.call-done = (bf16[3,512,256]{2,1,0:T(8,128)(2,1)}, bf16[512,2048]{1,0:T(8,128)(2,1)}, bf16[512,256]{1,0:T(8,128)(2,1)}, bf16[512,2048]{1,0:T(8,128)(2,1)}) async-done(((bf16[3,512,256]{2,1,0:T(8,128)(2,1)}, bf16[512,2048]{1,0:T(8,128)(2,1)}, bf16[512,256]{1,0:T(8,128)(2,1)}, bf16[512,2048]{1,0:T(8,128)(2,1)}), (bf16[3,512,256]{2,1,0:T(8,128)(2,1)}, bf16[512,2048]{1,0:T(8,128)(2,1)}, ...) | async-done | bytes 5242896 | tf_op jit(solution)/shard_map/psum | solution.py:314
  1075.8 22.9 %pad_maximum_fusion = bf16[2,2048,4096]{2,1,0:T(8,128)(2,1)} fusion(bf16[1,2048,4096]{2,1,0:T(8,128)(2,1)} %convert_bitcast_fusion, bf16[1,2048,4096]{2,1,0:T(8,128)(2,1)} %convert_bitcast_fusion.1), kind=kLoop, calls=%fused_computation | loop fusion | flops 16777216 | bytes 67108864 | tf_op jit(solution)/shard_map/stack | solution.py:248
  1110.5 17.9 reduce-scatter.27.cloned.1.call-done
  1140.6 16.2 reduce-scatter.61.cloned.1.call-done
  1167.7 145.8 %reduce-scatter.43.cloned.1.call-done = bf16[4096,512]{1,0:T(8,128)(2,1)} async-done(((bf16[4096,2048]{1,0:T(8,128)(2,1)}), bf16[4096,512]{1,0:T(8,128)(2,1)}) %reduce-scatter.43.cloned.1.call-update) | async-done | bytes 4194320 | tf_op jit(solution)/shard_map/reduce_scatter | solution.py:409
  1313.7 291.4 %reduce-scatter.39.cloned.1.call-done = bf16[2,512,4096]{2,1,0:T(8,128)(2,1)} async-done(((bf16[2,2048,4096]{2,1,0:T(8,128)(2,1)}), bf16[2,512,4096]{2,1,0:T(8,128)(2,1)}) %reduce-scatter.39.cloned.1.call-update) | async-done | bytes 8388624 | tf_op jit(solution)/shard_map/reduce_scatter | solution.py:406
  1613.2 19.0 reduce-scatter.53.cloned.1.call-done
  1633.6 25.2 %reduce-scatter.49.cloned.1.call-done = bf16[1,64,512]{2,1,0:T(8,128)(2,1)} async-done(((bf16[1,256,512]{2,1,0:T(8,128)(2,1)}), bf16[1,64,512]{2,1,0:T(8,128)(2,1)}) %reduce-scatter.49.cloned.1.call-update) | async-done | bytes 65552 | tf_op jit(solution)/shard_map/reduce_scatter | solution.py:440
  1660.3 25.7 %reduce-scatter.51.cloned.1.call-done = bf16[1,64,128]{2,1,0:T(8,128)(2,1)} async-done(((bf16[1,256,128]{2,1,0:T(8,128)(2,1)}), bf16[1,64,128]{2,1,0:T(8,128)(2,1)}) %reduce-scatter.51.cloned.1.call-update) | async-done | bytes 16400 | tf_op jit(solution)/shard_map/reduce_scatter | solution.py:443
  1687.4 37.4 %reduce-scatter.55.cloned.1.call-done = bf16[1,64,4096]{2,1,0:T(8,128)(2,1)} async-done(((bf16[1,256,4096]{2,1,0:T(8,128)(2,1)}), bf16[1,64,4096]{2,1,0:T(8,128)(2,1)}) %reduce-scatter.55.cloned.1.call-update) | async-done | bytes 524304 | tf_op jit(solution)/shard_map/reduce_scatter | solution.py:449
  1759.2 55.2 %reduce-scatter.59.cloned.1.call-done = bf16[1,2,64,4096]{3,2,1,0:T(8,128)(2,1)} async-done(((bf16[1,2,256,4096]{3,2,1,0:T(8,128)(2,1)}), bf16[1,2,64,4096]{3,2,1,0:T(8,128)(2,1)}) %reduce-scatter.59.cloned.1.call-update) | async-done | bytes 1048592 | tf_op jit(solution)/shard_map/reduce_scatter | solution.py:455
  1830.2 33.7 %reduce-scatter.57.cloned.1.call-done = bf16[1,2,64,2048]{3,2,1,0:T(8,128)(2,1)} async-done(((bf16[1,2,256,2048]{3,2,1,0:T(8,128)(2,1)}), bf16[1,2,64,2048]{3,2,1,0:T(8,128)(2,1)}) %reduce-scatter.57.cloned.1.call-update) | async-done | bytes 524304 | tf_op jit(solution)/shard_map/reduce_scatter | solution.py:452
  1866.0 63.2 %reduce-scatter.47.cloned.1.call-done = bf16[1,5,512,256]{2,3,1,0:T(8,128)(2,1)} async-done(((bf16[1,5,2048,256]{2,3,1,0:T(8,128)(2,1)}), bf16[1,5,512,256]{2,3,1,0:T(8,128)(2,1)}) %reduce-scatter.47.cloned.1.call-update) | async-done | bytes 1310736 | tf_op jit(solution)/shard_map/reduce_scatter | solution.py:437
  1947.4 16.5 reduce-scatter.41.cloned.1.call-done
  (360 shorter events, 455.5 us)
Async XLA Ops:
  10.6 301.6 %all-reduce.11.cloned.1.call-start = ((), (), s32[]{:S(2)}) async-start(), calls=%async_computation.50 | async-start | bytes 4718592 | tf_op jit(solution)/shard_map/psum | solution.py:204
  144.0 330.0 %all-gather.17.cloned.1.call-start = ((), (), s32[]{:S(2)}) async-start(), calls=%async_computation.24 | async-start | bytes 37748736 | tf_op jit(solution)/shard_map/all_gather | solution.py:368
  144.7 383.8 %all-gather.19.cloned.1.call-start = ((), (), s32[]{:S(2)}) async-start(), calls=%async_computation.25 | async-start | bytes 5242880 | tf_op jit(solution)/shard_map/all_gather | solution.py:379
  145.5 478.1 %all-gather.21.cloned.1.call-start = ((), (), s32[]{:S(2)}) async-start(), calls=%async_computation.26 | async-start | bytes 18874368 | tf_op jit(solution)/shard_map/all_gather | solution.py:369
  146.2 643.8 %all-reduce.9.cloned.1.call-start = ((), (), s32[]{:S(2)}) async-start(), calls=%async_computation.49 | async-start | bytes 5242880 | tf_op jit(solution)/shard_map/psum | solution.py:262
  835.5 273.7 %reduce-scatter.31.cloned.1.call-start = ((), (), s32[]{:S(2)}) async-start(), calls=%async_computation.31 | async-start | bytes 655360 | tf_op jit(solution)/shard_map/reduce_scatter | solution.py:400
  839.0 270.9 %reduce-scatter.35.cloned.1.call-start = ((), (), s32[]{:S(2)}) async-start(), calls=%async_computation.33 | async-start | bytes 2621440 | tf_op jit(solution)/shard_map/reduce_scatter | solution.py:403
  843.9 284.6 %reduce-scatter.27.cloned.1.call-start = ((), (), s32[]{:S(2)}) async-start(), calls=%async_computation.29 | async-start | bytes 2621440 | tf_op jit(solution)/shard_map/reduce_scatter | solution.py:397
  846.8 309.9 %reduce-scatter.61.cloned.1.call-start = ((), (), s32[]{:S(2)}) async-start(), calls=%async_computation.46 | async-start | bytes 655360
  1032.8 280.6 %reduce-scatter.43.cloned.1.call-start = ((), (), s32[]{:S(2)}) async-start(), calls=%async_computation.37 | async-start | bytes 20971520 | tf_op jit(solution)/shard_map/reduce_scatter | solution.py:409
  1047.8 557.2 %reduce-scatter.39.cloned.1.call-start = ((), (), s32[]{:S(2)}) async-start(), calls=%async_computation.35 | async-start | bytes 41943040 | tf_op jit(solution)/shard_map/reduce_scatter | solution.py:406
  1098.8 533.3 %reduce-scatter.53.cloned.1.call-start = ((), (), s32[]{:S(2)}) async-start(), calls=%async_computation.42 | async-start | bytes 327680 | tf_op jit(solution)/shard_map/reduce_scatter | solution.py:446
  1099.9 558.9 %reduce-scatter.49.cloned.1.call-start = ((), (), s32[]{:S(2)}) async-start(), calls=%async_computation.40 | async-start | bytes 327680 | tf_op jit(solution)/shard_map/reduce_scatter | solution.py:440
  1102.0 584.1 %reduce-scatter.51.cloned.1.call-start = ((), (), s32[]{:S(2)}) async-start(), calls=%async_computation.41 | async-start | bytes 81920 | tf_op jit(solution)/shard_map/reduce_scatter | solution.py:443
  1104.0 620.8 %reduce-scatter.55.cloned.1.call-start = ((), (), s32[]{:S(2)}) async-start(), calls=%async_computation.43 | async-start | bytes 2621440 | tf_op jit(solution)/shard_map/reduce_scatter | solution.py:449
  1109.2 625.5 %reduce-scatter.33.cloned.1.call-start = ((), (), s32[]{:S(2)}) async-start(), calls=%async_computation.32 | async-start | bytes 196608 | tf_op jit(solution)/shard_map/reduce_scatter | solution.py:420
  1109.9 636.1 %reduce-scatter.37.cloned.1.call-start = ((), (), s32[]{:S(2)}) async-start(), calls=%async_computation.34 | async-start | bytes 786432 | tf_op jit(solution)/shard_map/reduce_scatter | solution.py:423
  1110.5 646.9 %reduce-scatter.29.cloned.1.call-start = ((), (), s32[]{:S(2)}) async-start(), calls=%async_computation.30 | async-start | bytes 786432 | tf_op jit(solution)/shard_map/reduce_scatter | solution.py:417
  1128.4 685.9 %reduce-scatter.59.cloned.1.call-start = ((), (), s32[]{:S(2)}) async-start(), calls=%async_computation.45 | async-start | bytes 5242880 | tf_op jit(solution)/shard_map/reduce_scatter | solution.py:455
  1136.2 687.7 %reduce-scatter.63.cloned.1.call-start = ((), (), s32[]{:S(2)}) async-start(), calls=%async_computation.47 | async-start | bytes 196608
  1156.8 707.1 %reduce-scatter.57.cloned.1.call-start = ((), (), s32[]{:S(2)}) async-start(), calls=%async_computation.44 | async-start | bytes 2621440 | tf_op jit(solution)/shard_map/reduce_scatter | solution.py:452
  1159.6 769.6 %reduce-scatter.47.cloned.1.call-start = ((), (), s32[]{:S(2)}) async-start(), calls=%async_computation.39 | async-start | bytes 6553600 | tf_op jit(solution)/shard_map/reduce_scatter | solution.py:437
  1167.6 775.9 %reduce-scatter.45.cloned.1.call-start = ((), (), s32[]{:S(2)}) async-start(), calls=%async_computation.38 | async-start | bytes 6291456 | tf_op jit(solution)/shard_map/reduce_scatter | solution.py:429
  1313.5 650.5 %reduce-scatter.41.cloned.1.call-start = ((), (), s32[]{:S(2)}) async-start(), calls=%async_computation.36 | async-start | bytes 12582912 | tf_op jit(solution)/shard_map/reduce_scatter | solution.py:426
  (92 other events, 3759.9 us)
Sparse Core Ops, SparseCore 0:
  9.9 68.8 all-gather.8
  80.7 27.8 all-gather.10
  110.5 28.1 all-gather.12
  140.4 35.3 all-gather.14
  177.5 35.2 all-gather.22
  216.2 95.9 all-reduce.10
  314.1 159.8 all-gather.16
  475.8 52.6 all-gather.18
  530.5 93.1 all-gather.20
  685.5 104.4 all-reduce.8
  835.7 188.1 all-reduce.6
  1027.2 23.6 reduce-scatter.30
  1054.6 35.1 reduce-scatter.34
  1093.2 35.1 reduce-scatter.26
  1131.9 24.7 reduce-scatter.60
  1159.6 153.7 reduce-scatter.42
  1316.4 288.6 reduce-scatter.38
  1608.0 24.0 reduce-scatter.52
  1634.7 24.0 reduce-scatter.48
  1662.3 23.6 reduce-scatter.50
  1689.6 35.1 reduce-scatter.54
  1760.5 53.8 reduce-scatter.58
  1827.5 36.3 reduce-scatter.56
  1867.7 61.4 reduce-scatter.46
  (7 shorter events, 83.6 us)
where the time goes:
time: 1990 us; the launch traced here: 1980 us
  waiting for transfers between devices  1520 us (76%)
  matrix products  259 us (13%)
  other arithmetic  88.6 us (4%)
  blocking collectives  66.3 us (3%)
  local copies, waits for them, and re-layouts  21.7 us (1%)
    reduce_scatter x1, waiting for transfers between devices, local(): lax.psum_scatter(base_grads[3].astype(jnp.bfloat16), 'dp', scatter_dimens...  291 us
    psum x2, waiting for transfers between devices, layer_pass(): lax.psum(grad_rank_part.astype(jnp.bfloat16), 'mp').astype(jnp.float32)  262 us
    all_gather x1, waiting for transfers between devices, local(): lax.all_gather(gate_up_weight, ('dp', 'depth'), axis=1, tiled=True)  152 us
    dot_general x28, matrix products, product(): lax.dot_general(left_op, right_op, (((left_dim,), (right_dim,)), ((), ())...  152 us
    reduce_scatter x1, waiting for transfers between devices, local(): lax.psum_scatter(base_grads[4].astype(jnp.bfloat16), 'dp', scatter_dimens...  146 us
    psum x1, waiting for transfers between devices, layer_pass(): lax.psum(branch_part.astype(jnp.bfloat16), 'mp').astype(jnp.float32)  92.7 us
    all_gather x1, waiting for transfers between devices, local(): lax.all_gather(down_weight, ('dp', 'depth'), axis=1, tiled=True)  68.9 us
    reduce_scatter x1, waiting for transfers between devices, local(): lax.psum_scatter(adapt_grads[0][None].astype(jnp.bfloat16), 'dp', scatter...  63.2 us
  transfers between devices with their start and end apart: 35, of which 29 were waited for; matrix products, arithmetic and copies ran while one was open for 14% of the time, Pallas kernels for 0%

commit v1 on v0

v1 whole, which is shorter than its diff:
```python
import functools

import jax
import jax.numpy as jnp
from jax import lax
from jax.experimental import pallas as pl
from jax.experimental.pallas import tpu as pltpu
from jax.sharding import PartitionSpec as P

HEAD_SIZE = 256


EPS = 1e-06
THETA = 10000.0
NEGATIVE = -1e30


def product(left_op, right_op, left_dim, right_dim):
    return lax.dot_general(
        left_op,
        right_op,
        (((left_dim,), (right_dim,)), ((), ())),
        preferred_element_type=jnp.float32,
    )


def layout(seq_lens, row_count):
    seq_ends = jnp.cumsum(seq_lens)
    places = jnp.arange(row_count, dtype=jnp.int32)
    passed = (places[:, None] >= seq_ends[None, :]).astype(jnp.int32)
    segment = jnp.sum(passed, axis=1)
    starts = jnp.sum(passed * seq_lens[None, :], axis=1)
    valid_rows = (places < seq_ends[-1]).astype(jnp.float32)
    within = (places - starts).astype(jnp.float32)
    return (places, segment, within, valid_rows)


def rotary(within, head_width):
    half_width = head_width // 2
    frequency = THETA ** (-2.0 * jnp.arange(half_width, dtype=jnp.float32) / head_width)
    angles = within[:, None] * frequency[None, :]
    return (jnp.cos(angles), jnp.sin(angles))


def rotate(vector, cosine, sine_part):
    half_width = vector.shape[-1] // 2
    former = vector[..., :half_width]
    latter = vector[..., half_width:]
    return jnp.concatenate(
        [former * cosine - latter * sine_part, latter * cosine + former * sine_part], axis=-1
    )


def rotate_back(vector, cosine, sine_part):
    half_width = vector.shape[-1] // 2
    former = vector[..., :half_width]
    latter = vector[..., half_width:]
    return jnp.concatenate(
        [former * cosine + latter * sine_part, latter * cosine - former * sine_part], axis=-1
    )


def rms_forward(values, gain_row):
    inverse = lax.rsqrt(jnp.mean(values * values, axis=-1, keepdims=True) + EPS)
    return (values * inverse * gain_row, inverse)


def rms_backward(values, inverse, gain_row, grad_norm):
    weighted = grad_norm * gain_row
    grad_values = inverse * weighted - values * inverse**3 * jnp.mean(
        weighted * values, axis=-1, keepdims=True
    )
    grad_gain = jnp.sum(grad_norm * values * inverse, axis=0)
    return (grad_values, grad_gain)


def gelu_tanh(values):
    return jax.nn.gelu(values, approximate=True)


def block_mask(places, segment):
    return (segment[:, None] == segment[None, :]) & (places[None, :] <= places[:, None])


def attend(query_rows, key_rows, value_rows, places, segment, factor):
    row_count = query_rows.shape[0]
    block_rows = min(512, row_count)

    def one_block(block_id):
        allowed = block_mask(places, segment)
        scores = (
            jnp.einsum("qhd,kd->hqk", query_rows, key_rows, preferred_element_type=jnp.float32)
            * factor
        )
        scores = jnp.where(allowed[None], scores, NEGATIVE)
        row_peak = jnp.max(scores, axis=-1, keepdims=True)
        powers = jnp.exp(scores - row_peak)
        row_total = jnp.sum(powers, axis=-1, keepdims=True)
        attn_weights = (powers / row_total).astype(jnp.bfloat16)
        block_out = jnp.einsum(
            "hqk,kd->qhd", attn_weights, value_rows, preferred_element_type=jnp.float32
        )
        return (block_out, (row_peak + jnp.log(row_total))[..., 0])

    outputs, logsum = lax.map(one_block, jnp.arange(row_count // block_rows))
    return (outputs.reshape(query_rows.shape), logsum)


def attend_back(query_rows, key_rows, value_rows, places, segment, factor, logsum, grad_att):
    row_count = query_rows.shape[0]
    block_rows = min(512, row_count)

    def one_block(carry, block_id):
        grad_keys, grad_values = carry
        allowed = block_mask(places, segment)
        scores = (
            jnp.einsum("qhd,kd->hqk", query_rows, key_rows, preferred_element_type=jnp.float32)
            * factor
        )
        scores = jnp.where(allowed[None], scores, NEGATIVE)
        attn_probs = jnp.exp(scores - logsum[block_id][..., None])
        attn_weights = attn_probs.astype(jnp.bfloat16)
        grad_probs = jnp.einsum(
            "qhd,kd->hqk", grad_att, value_rows, preferred_element_type=jnp.float32
        )
        grad_values = grad_values + jnp.einsum(
            "hqk,qhd->kd", attn_weights, grad_att, preferred_element_type=jnp.float32
        )
        centre = jnp.sum(grad_probs * attn_probs, axis=-1, keepdims=True)
        grad_scores = (attn_probs * (grad_probs - centre)).astype(jnp.bfloat16)
        grad_query = (
            jnp.einsum("hqk,kd->qhd", grad_scores, key_rows, preferred_element_type=jnp.float32)
            * factor
        )
        grad_keys = (
            grad_keys
            + jnp.einsum("hqk,qhd->kd", grad_scores, query_rows, preferred_element_type=jnp.float32)
            * factor
        )
        return ((grad_keys, grad_values), grad_query)

    zero_rows = jnp.zeros(key_rows.shape, jnp.float32)
    (grad_keys, grad_values), grad_query = lax.scan(
        one_block, (zero_rows, zero_rows), jnp.arange(row_count // block_rows)
    )
    return (grad_query.reshape(query_rows.shape), grad_keys, grad_values)


CHUNKS = 4
GROUPS = 2
BF16 = jnp.bfloat16
F32 = jnp.float32


def trade(block, axis, mask):
    count = lax.axis_size(axis)
    return lax.ppermute(block, axis, [(i, i ^ mask) for i in range(count)])


def gather_dp(piece, *hold):
    count = lax.axis_size("dp")
    if count == 4:
        half = piece.shape[0] // 2
        from_one = trade(piece, "dp", 1)
        from_two = trade(piece, "dp", 2)
        far = jnp.concatenate(
            [
                trade(after(from_two[:half], *hold), "dp", 1),
                trade(after(from_one[half:], *hold), "dp", 2),
            ],
            axis=0,
        )
        return [piece, from_one, from_two, far]
    pieces, mask = [piece], 1
    while mask < count:
        pieces = pieces + [trade(held, "dp", mask) for held in pieces]
        mask *= 2
    return pieces


def gather_pair(one, two):
    count = lax.axis_size("dp")
    if count == 4:
        first_one, first_two = trade(one, "dp", 1), trade(one, "dp", 2)
        second_one, second_two = trade(two, "dp", 1), trade(two, "dp", 2)
        far = trade(first_two, "dp", 1), trade(second_one, "dp", 2)
        pieces = [(one, two), (first_one, second_one), (first_two, second_two), far]
        return pieces, far
    ones, twos = gather_dp(one), gather_dp(two)
    return list(zip(ones, twos)), (ones[-1], twos[-1])


def gather_near(bundle):
    count = lax.axis_size("dp")
    pieces, mask = [bundle], 1
    while mask < count:
        first = pieces if count != 4 else pieces[:1]
        pieces = pieces + [trade(held, "dp", mask) for held in first]
        mask *= 2
    return pieces


def gather_far(near, hold, height):
    chunks = [[((b, c), (b, CHUNKS + c)) for b in near] for c in range(CHUNKS)]
    if lax.axis_size("dp") == 4:
        size = CHUNKS // GROUPS
        for group in range(GROUPS):
            rows = (size * group * height, size * (group + 1) * height)
            one = lax.slice_in_dim(after(near[2], hold), *rows, axis=0)
            two = lax.slice_in_dim(
                after(near[1], hold), *[CHUNKS * height + r for r in rows], axis=0
            )
            one, two = trade(one, "dp", 1), trade(two, "dp", 2)
            for n in range(size):
                chunks[group * size + n].append(((one, n), (two, n)))
    return chunks


def scatter_dp(parts, *hold):
    count = lax.axis_size("dp")
    if hold:
        parts = [after(part, *hold) for part in parts]
    if count == 4:
        half = parts[3].shape[0] // 2
        near_one = trade(parts[3][:half], "dp", 1)
        near_two = trade(parts[3][half:], "dp", 2)
        for_two = jnp.concatenate([add_rounded(parts[2][:half], near_one), parts[2][half:]], axis=0)
        for_one = jnp.concatenate([parts[1][:half], add_rounded(parts[1][half:], near_two)], axis=0)
        got_one = trade(for_one, "dp", 1)
        got_two = trade(for_two, "dp", 2)
        return parts[0].astype(F32) + got_one.astype(F32) + got_two.astype(F32)
    mask = count // 2
    while mask:
        parts = [
            add_rounded(parts[p], trade(parts[p + mask], "dp", mask)) for p in range(mask)
        ]
        mask //= 2
    return parts[0].astype(F32)


def add_rounded(one, two):
    return (one.astype(F32) + two.astype(F32)).astype(BF16)


def relative(block, axis, index, count):
    width = block.shape[axis] // count
    mask = 1
    while mask < count:
        flipped = jnp.concatenate(
            [
                lax.slice_in_dim(block, (b ^ mask) * width, ((b ^ mask) + 1) * width, axis=axis)
                for b in range(count)
            ],
            axis=axis,
        )
        block = jnp.where((index & mask) > 0, flipped, block)
        mask *= 2
    return block


VMEM_LIMIT = 50 * 1024 * 1024
GELU_SCALE = 0.7978845608028654
BRIEF = pl.CostEstimate(flops=1, bytes_accessed=1, transcendentals=0)


def after(block, *earlier):
    return lax.optimization_barrier((block, *earlier))[0]


def whole_spec(shape):
    return pl.BlockSpec(shape, lambda *_: (0,) * len(shape), pipeline_mode=pl.Buffered(1))


def params():
    return pltpu.CompilerParams(vmem_limit_bytes=VMEM_LIMIT)


def nn(left_op, right_op):
    return product(left_op, right_op, 1, 0)


def nt(left_op, right_op):
    return product(left_op, right_op, 1, 1)


def late_split(height):
    return -(-height // 48) * 16


def pack_kernel(part, rank_part, rank, mp, *refs):
    query, key_value, output, gains, query_up, key_value_up, output_down = refs[:7]
    inputs, input_share, model_share, attn, one, late = refs[7:]
    heads = query.shape[1]
    one[...] = jnp.zeros_like(one)
    one[:part, :heads] = query[...]
    one[:part, heads:] = key_value[...]
    one[part : 2 * part, :heads] = output[...].T
    one[2 * part : 2 * part + 2, :part] = gains[...]
    first = 2 * part + 16
    one[first : first + rank_part, :heads] = query_up[0]
    one[first : first + rank_part, heads:] = key_value_up[0]
    one[first + rank_part :, :heads] = output_down[0]
    wide = inputs.shape[2]
    attn[wide:, :] = jnp.zeros_like(attn[wide:, :])
    for k in range(3):
        attn[:wide, k * rank : (k + 1) * rank] = inputs[0, k]
    row = 0
    for at in range(0, model_share.shape[3], rank):
        for k in range(2):
            late[row : row + rank_part, :] = model_share[0, k, :, at : at + rank]
            row += rank_part
    height = input_share.shape[2]
    for k in range(2):
        late[row : row + height, :] = input_share[0, 3 + k]
        row += height
    split = late_split(row)
    for k in range(3):
        rows = min(split, row - k * split)
        attn[wide : wide + rows, k * rank : (k + 1) * rank] = late[
            k * split : k * split + rows, :
        ]


def pack_pass(mp, arrays, mp_count, rank):
    query, key_value, output, gains, query_up, _, _, inputs, model_up = arrays
    part, rank_part = query.shape[0], query_up.shape[1]
    slice_width, columns = inputs.shape[2], model_up.shape[3] // mp_count
    rows = slice_width // mp_count
    late_rows = 2 * rank_part * (columns // rank) + 2 * rows
    shapes = [
        (slice_width + late_split(late_rows), 3 * rank),
        (2 * part + 16 + 2 * rank_part, query.shape[1] + key_value.shape[1]),
    ]

    def whole(shape):
        return pl.BlockSpec(shape, lambda s, mp: (0,) * len(shape))

    return pl.pallas_call(
        functools.partial(pack_kernel, part, rank_part, rank),
        grid_spec=pltpu.PrefetchScalarGridSpec(
            num_scalar_prefetch=1,
            grid=(1,),
            in_specs=[whole(a.shape) for a in arrays[:8]]
            + [
                pl.BlockSpec((1, 5, rows, rank), lambda s, mp: (0, 0, mp[0], 0)),
                pl.BlockSpec((1, 2, rank_part, columns), lambda s, mp: (0, 0, 0, mp[0])),
            ],
            out_specs=[whole(s) for s in shapes],
            scratch_shapes=[pltpu.VMEM((late_rows, rank), BF16)],
        ),
        out_shape=[jax.ShapeDtypeStruct(s, BF16) for s in shapes],
        compiler_params=params(),
        cost_estimate=BRIEF,
        name="pack_pass",
    )(mp, *arrays[:7], inputs, inputs, model_up)


def unpack_kernel(count, part, rank_part, *refs):
    pieces, (shared, inputs, late, lifted, out_down) = refs[: 2 * count], refs[2 * count :]
    rows = shared.shape[0] // count
    wide, rank = 2 * part, late.shape[2]
    heads = out_down.shape[1]
    height = late.shape[1]
    split = late_split(height)
    for p in range(count):
        attn, one = pieces[2 * p : 2 * p + 2]
        shared[p * rows : (p + 1) * rows, :] = one[:rows, :]
        here = slice(p * rank_part, (p + 1) * rank_part)
        lifted[here, :] = one[rows : rows + rank_part, :]
        out_down[here, :] = one[rows + rank_part :, :heads]
        inputs[p * wide : (p + 1) * wide, :] = attn[:wide, :]
        for k in range(3):
            number = min(split, height - k * split)
            late[p, k * split : k * split + number, :] = attn[
                wide : wide + number, k * rank : (k + 1) * rank
            ]


def unpack_pass(pieces, part, rank_part, rank, rows, columns, heads):
    count = len(pieces)
    joint = pieces[0][1].shape[1]
    late_rows = 2 * rank_part * (columns // rank) + 2 * rows
    flat = [b for pair in pieces for b in pair]
    shapes = [
        (count * (2 * part + 16), joint),
        (count * 2 * part, 3 * rank),
        (count, late_rows, rank),
        (count * rank_part, joint),
        (count * rank_part, heads),
    ]
    return pl.pallas_call(
        functools.partial(unpack_kernel, count, part, rank_part),
        grid=(1,),
        in_specs=[whole_spec(b.shape) for b in flat],
        out_specs=[whole_spec(s) for s in shapes],
        out_shape=[jax.ShapeDtypeStruct(s, BF16) for s in shapes],
        compiler_params=params(),
        cost_estimate=BRIEF,
        name="unpack_pass",
    )(*flat)


def shared_kernel(count, part, core, own, other, joint, output, gains):
    rows = own.shape[0] // count
    heads = output.shape[1]
    gains[...] = jnp.zeros_like(gains)
    for e in range(2):

        @pl.when(core[0] == e)
        def _(e=e):
            for side, source in ((e, own), (1 - e, other)):
                for p in range(count):
                    here = slice((2 * p + side) * part, (2 * p + side + 1) * part)
                    first = p * rows
                    joint[here, :] = source[first : first + part, :]
                    output[here, :] = source[first + part : first + 2 * part, :heads]
                    gains[:2, here] = source[first + 2 * part : first + 2 * part + 2, :part]


def shared_pass(core, own, other, count, part, heads):
    shapes = [(count * 2 * part, own.shape[1]), (count * 2 * part, heads), (16, count * 2 * part)]
    return pl.pallas_call(
        functools.partial(shared_kernel, count, part),
        grid=(1,),
        in_specs=[pl.BlockSpec(memory_space=pltpu.SMEM)] + [whole_spec(own.shape)] * 2,
        out_specs=[whole_spec(s) for s in shapes],
        out_shape=[jax.ShapeDtypeStruct(s, BF16) for s in shapes],
        compiler_params=params(),
        cost_estimate=BRIEF,
        name="shared_pass",
    )(core, own, other)


def late_kernel(rank_part, rows, count, late, model, inputs):
    rank = late.shape[3]
    for p in range(count):
        for n in range(model.shape[2] // rank):
            for k in range(2):
                first = (2 * n + k) * rank_part
                model[k, p * rank_part : (p + 1) * rank_part, n * rank : (n + 1) * rank] = late[
                    0, p, first : first + rank_part, :
                ]
        first = 2 * rank_part * (model.shape[2] // rank)
        for k in range(2):
            inputs[p, 0, :, k * rank : (k + 1) * rank] = late[
                0, p, first + k * rows : first + (k + 1) * rows, :
            ]


def late_pass(late, rows, columns, rank_part):
    mp_count, count, height, rank = late.shape
    model, inputs = pl.pallas_call(
        functools.partial(late_kernel, rank_part, rows, count),
        grid=(mp_count,),
        in_specs=[pl.BlockSpec((1, count, height, rank), lambda z: (z, 0, 0, 0))],
        out_specs=[
            pl.BlockSpec((2, rank, columns), lambda z: (0, 0, z)),
            pl.BlockSpec((count, 1, rows, 2 * rank), lambda z: (0, z, 0, 0)),
        ],
        out_shape=[
            jax.ShapeDtypeStruct((2, rank, mp_count * columns), BF16),
            jax.ShapeDtypeStruct((count, mp_count, rows, 2 * rank), BF16),
        ],
        compiler_params=params(),
        cost_estimate=BRIEF,
        name="late_pass",
    )(late)
    return model, inputs.reshape(count * mp_count * rows, 2 * rank)


def ffn_blocks(arrays, chunk, side):
    gate_up, down, lora_gate_up, lora_hidden = arrays

    def column(s, core):
        return side(core[0]) * CHUNKS + s

    return [
        pl.BlockSpec((2, gate_up.shape[1], chunk), lambda s, core: (0, 0, column(s, core))),
        pl.BlockSpec((chunk, down.shape[1]), lambda s, core: (column(s, core), 0)),
        pl.BlockSpec(
            (1, 2, lora_gate_up.shape[2], chunk), lambda s, core: (0, 0, 0, column(s, core))
        ),
        pl.BlockSpec((1, lora_hidden.shape[1], chunk), lambda s, core: (0, 0, column(s, core))),
    ]


def ffn_rows(gate_up, down, lora_gate_up, lora_hidden):
    return [
        gate_up[0],
        gate_up[1],
        down[...].T,
        jnp.concatenate([lora_gate_up[0, 0], lora_gate_up[0, 1], lora_hidden[0]], axis=0),
    ]


def give_kernel(core, gate_up, down, lora_gate_up, lora_hidden, given):
    first = 0
    for block in ffn_rows(gate_up, down, lora_gate_up, lora_hidden):
        given[first : first + block.shape[0], :] = block
        first += block.shape[0]


def give_pass(core, arrays, chunk):
    part, rank_part = arrays[0].shape[1], arrays[3].shape[1]
    height = 3 * (part + rank_part)
    return pl.pallas_call(
        give_kernel,
        grid_spec=pltpu.PrefetchScalarGridSpec(
            num_scalar_prefetch=1,
            grid=(CHUNKS,),
            in_specs=ffn_blocks(arrays, chunk, lambda me: 1 - me),
            out_specs=pl.BlockSpec((height, chunk), lambda s, core: (s, 0)),
        ),
        out_shape=jax.ShapeDtypeStruct((CHUNKS * height, chunk), BF16),
        compiler_params=params(),
        cost_estimate=BRIEF,
        name="give_pass",
    )(core, *arrays)


def bundle_kernel(part, core, gate_up, down, lora_gate_up, lora_hidden, taken, bundle):
    own_first = core[0] == 0
    one, two = bundle.at[0], bundle.at[1]
    gate, upper, lower, lifted = ffn_rows(gate_up, down, lora_gate_up, lora_hidden)

    def pair(own, start):
        other = taken[start : start + part, :]
        return jnp.where(own_first, own, other), jnp.where(own_first, other, own)

    one[:part, :], one[part : 2 * part, :] = pair(gate, 0)
    two[:part, :], two[part : 2 * part, :] = pair(upper, part)
    one[2 * part : 3 * part, :], two[2 * part : 3 * part, :] = pair(lower, 2 * part)
    one[3 * part :, :] = lifted
    two[3 * part :, :] = taken[3 * part :, :]


def bundle_pass(core, arrays, taken, chunk):
    part = arrays[0].shape[1]
    height = taken.shape[0] // CHUNKS
    out = pl.pallas_call(
        functools.partial(bundle_kernel, part),
        grid_spec=pltpu.PrefetchScalarGridSpec(
            num_scalar_prefetch=1,
            grid=(CHUNKS,),
            in_specs=ffn_blocks(arrays, chunk, lambda me: me)
            + [pl.BlockSpec((height, chunk), lambda s, core: (s, 0))],
            out_specs=pl.BlockSpec((2, height, chunk), lambda s, core: (0, s, 0)),
        ),
        out_shape=jax.ShapeDtypeStruct((2, CHUNKS * height, chunk), BF16),
        compiler_params=params(),
        cost_estimate=BRIEF,
        name="bundle_pass",
    )(core, *arrays, taken)
    return out.reshape(2 * CHUNKS * height, chunk)


def gate_kernel(count, width, rank_part, has_base, *refs):
    blocks, refs = refs[:4], refs[4:]
    pieces = [(refs[2 * p], refs[2 * p + 1]) for p in range(count)]
    refs = refs[2 * count :]
    bases, refs = (refs[:2], refs[2:]) if has_base else ((), refs)
    gated_ref, gate_ref, upper_ref, *outs = refs[:5]
    adapters = refs[5]
    rows = blocks[0].shape[0]
    part = width // 2
    rank = count * rank_part
    model_width = count * width
    for b in range(2):
        for k in range(3):
            first = 3 * part + k * rank_part
            for p in range(count):
                adapters[3 * b + k, p * rank_part : (p + 1) * rank_part, :] = pieces[p][b][
                    first : first + rank_part, :
                ]
    for b in range(2):
        normed, grad = blocks[b], blocks[2 + b]
        span = slice(b * rows, (b + 1) * rows)
        gate = nn(normed[:, model_width : model_width + rank], adapters[3 * b])
        upper = nn(normed[:, model_width + rank :], adapters[3 * b + 1])
        grad_gated = nn(grad[:, model_width:], adapters[3 * b + 2])
        for p in range(count):
            columns = slice(p * width, (p + 1) * width)
            gate += nn(normed[:, columns], pieces[p][0][:width, :])
            upper += nn(normed[:, columns], pieces[p][1][:width, :])
            for e in range(2):
                columns = slice(p * width + e * part, p * width + (e + 1) * part)
                grad_gated += nn(grad[:, columns], pieces[p][e][width : width + part, :])
        square = gate * gate
        bent = jnp.tanh(GELU_SCALE * gate * (1.0 + 0.044715 * square))
        half = 0.5 * (1.0 + bent)
        active = gate * half
        slope = half + 0.5 * gate * (1.0 - bent * bent) * GELU_SCALE * (
            1.0 + 3.0 * 0.044715 * square
        )
        gated_ref[span, :] = (active * upper).astype(BF16)
        gate_ref[span, :] = (grad_gated * upper * slope).astype(BF16)
        upper_ref[span, :] = (grad_gated * active).astype(BF16)

    def put(b, first, value):
        columns = slice(first, first + value.shape[1])
        if bases:
            value = value + bases[b][:, columns].astype(F32)
        outs[b][:, columns] = value.astype(outs[b].dtype)

    for p in range(count):
        value = nt(gate_ref[...], pieces[p][0][:width, :]) + nt(
            upper_ref[...], pieces[p][1][:width, :]
        )
        for b in range(2):
            put(b, p * width, value[b * rows : (b + 1) * rows])
    for b in range(2):
        span = slice(b * rows, (b + 1) * rows)
        put(b, model_width, nt(gate_ref[span, :], adapters[3 * b]))
        put(b, model_width + rank, nt(upper_ref[span, :], adapters[3 * b + 1]))


def gate_pass(normed_pair, grad_pair, pieces, width, rank_part, bases, last):
    blocks = (*normed_pair, *grad_pair)
    rows, columns = blocks[0].shape
    both_rows = 2 * rows
    pairs = [block for pair in pieces for block in pair]
    height = 3 * (width // 2 + rank_part)
    chunk = pairs[0][0].shape[1]
    return pl.pallas_call(
        functools.partial(gate_kernel, len(pieces), width, rank_part, bool(bases)),
        grid=(1,),
        in_specs=[whole_spec(a.shape) for a in blocks]
        + [
            pl.BlockSpec(
                (height, chunk),
                functools.partial(lambda at, t: (at, 0), at),
                pipeline_mode=pl.Buffered(1),
            )
            for _, at in pairs
        ]
        + [whole_spec(a.shape) for a in bases],
        out_specs=[whole_spec((both_rows, chunk))] * 3 + [whole_spec((rows, columns))] * 2,
        out_shape=[jax.ShapeDtypeStruct((both_rows, chunk), BF16)] * 3
        + [
            jax.ShapeDtypeStruct((rows, columns), F32 if last else BF16),
            jax.ShapeDtypeStruct((rows, columns), BF16),
        ],
        scratch_shapes=[pltpu.VMEM((6, len(pieces) * rank_part, chunk), BF16)],
        compiler_params=params(),
        cost_estimate=BRIEF,
        name="gate_pass",
    )(*blocks, *[block for block, _ in pairs], *bases)


def down_kernel(count, rows, width, rank_part, chunks, *refs):
    acts, refs = refs[:chunks], refs[chunks:]
    outs, adapters = refs[-3:-1], refs[-1]
    part = width // 2
    pieces = [
        [refs[2 * (q * count + p) : 2 * (q * count + p) + 2] for p in range(count)]
        for q in range(chunks)
    ]
    for b in range(2):
        span = slice(b * rows, (b + 1) * rows)
        for p in range(count):
            for e in range(2):
                value = nt(acts[0][span, :], pieces[0][p][e][width : width + part, :])
                for q in range(1, chunks):
                    value += nt(acts[q][span, :], pieces[q][p][e][width : width + part, :])
                first = p * width + e * part
                outs[b][:, first : first + part] = value.astype(outs[b].dtype)
        value = 0.0
        first = 3 * part + 2 * rank_part
        for q in range(chunks):
            for p in range(count):
                adapters[p * rank_part : (p + 1) * rank_part, :] = pieces[q][p][b][
                    first : first + rank_part, :
                ]
            value += nt(acts[q][span, :], adapters[...])
        outs[b][:, count * width :] = value.astype(outs[b].dtype)


def down_pass(acts, chunks, width, rank_part):
    count = len(chunks[0])
    both_rows, chunk = acts[0].shape
    rows = both_rows // 2
    columns = count * (width + rank_part)
    height = 3 * (width // 2 + rank_part)
    pairs = [block for pieces in chunks for pair in pieces for block in pair]
    shapes = [
        jax.ShapeDtypeStruct((rows, columns), F32),
        jax.ShapeDtypeStruct((rows, columns), BF16),
    ]
    return pl.pallas_call(
        functools.partial(down_kernel, count, rows, width, rank_part, len(chunks)),
        grid=(1,),
        in_specs=[whole_spec(a.shape) for a in acts]
        + [
            pl.BlockSpec(
                (height, chunk),
                functools.partial(lambda at, t: (at, 0), at),
                pipeline_mode=pl.Buffered(1),
            )
            for _, at in pairs
        ],
        out_specs=[whole_spec(s.shape) for s in shapes],
        out_shape=shapes,
        scratch_shapes=[pltpu.VMEM((count * rank_part, chunk), BF16)],
        compiler_params=params(),
        cost_estimate=BRIEF,
        name="down_pass",
    )(*acts, *[block for block, _ in pairs])


def sum_kernel(own, other, total):
    total[...] = (own[...].astype(F32) + other[...].astype(F32)).astype(BF16)


def sum_pass(own, other):
    rows, columns = own.shape
    tile = pl.BlockSpec((rows // 4, columns), lambda t: (t, 0))
    return pl.pallas_call(
        sum_kernel,
        grid=(4,),
        in_specs=[tile, tile],
        out_specs=tile,
        out_shape=jax.ShapeDtypeStruct((rows, columns), BF16),
        compiler_params=params(),
        cost_estimate=BRIEF,
        name="sum_pass",
    )(own, other)


def turn_kernel(own, other, turned):
    rows = own.shape[0]
    turned[:, :rows] = own[...].T
    turned[:, rows:] = other[...].T


def turn_pass(own, other):
    rows, columns = own.shape
    tile = 256
    source = pl.BlockSpec((rows, tile), lambda t: (0, t))
    return pl.pallas_call(
        turn_kernel,
        grid=(columns // tile,),
        in_specs=[source, source],
        out_specs=pl.BlockSpec((tile, 2 * rows), lambda t: (t, 0)),
        out_shape=jax.ShapeDtypeStruct((columns, 2 * rows), own.dtype),
        compiler_params=params(),
        cost_estimate=BRIEF,
        name="turn_pass",
    )(own, other)


def weight_kernel(part, rank_part, sides, adds, aliased, core, *refs):
    gate, upper, gated = refs[:3]
    refs = refs[3:]
    rows = gate.shape[0] // 2
    outs = refs[-len(sides) :]
    for side, number, out in zip(sides, adds, outs):
        normed, grad, *ranks = refs[:5]
        added = refs[5 : 5 + number]
        refs = refs[5 + number :]

        def store(start, value):
            here = slice(start, start + value.shape[0])
            for other in added:
                value = value + other[here, :].astype(F32)
            out[here, :] = value.astype(out.dtype)

        for n, (columns, act) in enumerate(((normed, gate), (normed, upper), (grad, gated))):
            store(n * part, nn(columns[...], act[...]))
        span = slice(side * rows, (side + 1) * rows)
        for n, act in enumerate((gate, upper, gated)):
            store(3 * part + n * rank_part, nn(ranks[n][:, span], act[span, :]))


def weight_pass(core, normed_t, grad_t, width, rank_part, acts, at, count, items, held=()):
    both_rows = normed_t.shape[1]
    chunk = acts[0].shape[1]
    part = width // 2
    height = 3 * (part + rank_part)
    tile = min(256, chunk)
    model_blocks = (2 * grad_t.shape[0] - normed_t.shape[0]) // rank_part
    rank_blocks = (normed_t.shape[0] - grad_t.shape[0]) // rank_part

    def rows_of(index, side):
        return pl.BlockSpec(
            (part, both_rows),
            lambda t, core: (2 * index + (core[0] ^ side), 0),
            pipeline_mode=pl.Buffered(1),
        )

    def ranks_of(block):
        return pl.BlockSpec(
            (rank_part, both_rows), lambda t, core: (block, 0), pipeline_mode=pl.Buffered(1)
        )

    tiled = pl.BlockSpec((height, tile), lambda t, core: (at, t))
    inputs = list(acts)
    specs = [pl.BlockSpec((both_rows, tile), lambda t, core: (0, t)) for _ in acts]
    for index, side, added, _ in items:
        inputs += [normed_t, grad_t, normed_t, normed_t, grad_t, *[block for block, _ in added]]
        specs += [rows_of(index, side)] * 2
        specs += [ranks_of(model_blocks + n * rank_blocks + index) for n in (0, 1, 0)]
        specs += [
            pl.BlockSpec((height, tile), functools.partial(lambda n, t, core: (n, t), n))
            for _, n in added
        ]
    aliases = {1 + len(inputs) + n: n for n in range(len(held))}
    return pl.pallas_call(
        functools.partial(
            weight_kernel,
            part,
            rank_part,
            tuple(item[1] for item in items),
            tuple(len(item[2]) for item in items),
            len(held),
        ),
        grid_spec=pltpu.PrefetchScalarGridSpec(
            num_scalar_prefetch=1,
            grid=(chunk // tile,),
            in_specs=specs + [pl.BlockSpec(memory_space=pl.ANY) for _ in held],
            out_specs=[tiled] * len(items),
        ),
        out_shape=[jax.ShapeDtypeStruct((count * height, chunk), item[3]) for item in items],
        input_output_aliases=aliases,
        compiler_params=params(),
        cost_estimate=BRIEF,
        name="weight_pass",
    )(core, *inputs, *held)


def finish_kernel(part, rank_part, groups, core, *refs):
    gate_up, down, lora_gate_up, lora_hidden = refs[-4:]
    for n, source in enumerate(refs[:-4]):
        here = pl.program_id(0) == n // groups
        if groups > 1:
            here &= pl.program_id(1) // (CHUNKS // groups) == n % groups

        @pl.when(here)
        def _(source=source):
            def rows(start, height):
                return source[start : start + height, :].astype(F32)

            gate_up[0] = rows(0, part)
            gate_up[1] = rows(part, part)
            down[...] = rows(2 * part, part).T
            lora_gate_up[0, 0] = rows(3 * part, rank_part)
            lora_gate_up[0, 1] = rows(3 * part + rank_part, rank_part)
            lora_hidden[0] = rows(3 * part + 2 * rank_part, rank_part)


def finish_pass(core, mine, other, part, rank_part, hidden):
    chunk = mine[0].shape[1]
    groups = len(mine)
    size = CHUNKS // groups
    height = mine[0].shape[0] // size

    def source(side, group):
        def index(s, q, core):
            inside = jnp.clip(q - group * size, 0, size - 1)
            return (jnp.where(s == side, inside, (size - 1) * (1 - side)), 0)

        return pl.BlockSpec((height, chunk), index)

    def column(s, q, core):
        return (core[0] ^ s) * CHUNKS + q

    shapes = [
        jax.ShapeDtypeStruct(s, F32)
        for s in (
            (2, part, hidden),
            (hidden, part),
            (1, 2, rank_part, hidden),
            (1, rank_part, hidden),
        )
    ]
    grid_spec = pltpu.PrefetchScalarGridSpec(
        num_scalar_prefetch=1,
        grid=(2, CHUNKS),
        in_specs=[source(side, group) for side in range(2) for group in range(groups)],
        out_specs=[
            pl.BlockSpec((2, part, chunk), lambda s, q, core: (0, 0, column(s, q, core))),
            pl.BlockSpec((chunk, part), lambda s, q, core: (column(s, q, core), 0)),
            pl.BlockSpec(
                (1, 2, rank_part, chunk), lambda s, q, core: (0, 0, 0, column(s, q, core))
            ),
            pl.BlockSpec((1, rank_part, chunk), lambda s, q, core: (0, 0, column(s, q, core))),
        ],
    )
    return pl.pallas_call(
        functools.partial(finish_kernel, part, rank_part, groups),
        grid_spec=grid_spec,
        out_shape=shapes,
        compiler_params=params(),
        cost_estimate=BRIEF,
        name="finish_pass",
    )(core, *mine, *other)


def dot(left_op, right_op):
    return jnp.dot(left_op, right_op, preferred_element_type=F32)


def pad_rows(block, rows, width):
    return jnp.pad(block, ((0, rows - block.shape[0]), (0, width - block.shape[1])))


def local(
    tokens,
    cotangent,
    lengths,
    bucket_loop_index,
    query_weight,
    key_value_weight,
    output_weight,
    gate_up_weight,
    down_weight,
    gains,
    adapter_input_down,
    adapter_query_up,
    adapter_key_value,
    adapter_output_down,
    adapter_hidden_down,
    adapter_model_up,
    adapter_gate_up,
):
    dp_count = lax.axis_size("dp")
    dp_id = lax.axis_index("dp")
    depth_id = lax.axis_index("depth")
    mp_index = lax.axis_index("mp")
    first_core = depth_id == 0
    row_count, model_width = tokens.shape
    slice_width = model_width // dp_count
    part_width = slice_width // 2
    heads_width = query_weight.shape[1]
    heads_here = heads_width // HEAD_SIZE
    kv_width = key_value_weight.shape[1]
    joint_width = heads_width + kv_width
    rank_part = adapter_query_up.shape[1]
    rank = rank_part * dp_count
    hidden = down_weight.shape[0]
    half_hidden = hidden // 2
    chunk = half_hidden // CHUNKS

    def partner(block):
        return trade(block, "depth", 1)

    def in_core_order(own, other):
        return jnp.where(first_core, own, other), jnp.where(first_core, other, own)

    keep_own = bucket_loop_index[0, depth_id] == depth_id
    tok_swap, grad_swap = partner(tokens), partner(cotangent)
    slot_id = jnp.where(keep_own, depth_id, 1 - depth_id)
    seq_lens = lengths[0, slot_id]
    places, segment, within, valid_rows = layout(seq_lens, row_count)
    cosine, sine_part = rotary(within, HEAD_SIZE)
    head_cos = cosine[:, None, :]
    head_sin = sine_part[:, None, :]
    factor = HEAD_SIZE ** (-0.5)
    tok_rows = relative(jnp.where(keep_own, tokens, tok_swap), 1, dp_id, dp_count)
    source = tok_rows.astype(F32)
    grad_rows = relative(jnp.where(keep_own, cotangent, grad_swap), 1, dp_id, dp_count)
    grad_out = grad_rows.astype(F32) * valid_rows[:, None]
    grad_ffn = grad_out.astype(BF16)

    mp_count = lax.axis_size("mp")
    share_rows = slice_width // mp_count
    share_columns = model_width // mp_count
    core = depth_id[None].astype(jnp.int32)
    ffn_arrays = (gate_up_weight, down_weight, adapter_gate_up, adapter_hidden_down)
    taken = partner(give_pass(core, ffn_arrays, chunk))
    bundles = pack_pass(
        mp_index[None].astype(jnp.int32),
        (query_weight, key_value_weight, output_weight, gains)
        + (adapter_query_up, adapter_key_value, adapter_output_down)
        + (adapter_input_down, adapter_model_up),
        mp_count,
        rank,
    )
    bundle = bundle_pass(core, ffn_arrays, taken, chunk)
    pieces, hold = gather_pair(*bundles)
    shared_own, input_attn, late, joint_lifted, out_down = unpack_pass(
        pieces, part_width, rank_part, rank, share_rows, share_columns, heads_width
    )
    joint_weight, out_weight, gains_all = shared_pass(
        core, shared_own, partner(shared_own), dp_count, part_width, heads_width
    )
    gains_all = gains_all[:2].astype(F32)
    gain_one, gain_two = gains_all[0], gains_all[1]
    model_all, input_ffn = late_pass(
        lax.all_gather(late, "mp", axis=0, tiled=False),
        share_rows,
        share_columns,
        rank_part,
    )
    model_all = relative(model_all, 2, dp_id, dp_count)
    model_lifted = [model_all[0], model_all[1]]

    near = gather_near(after(bundle, *hold))
    height = 3 * (part_width + rank_part)

    norm_one, inverse_one = rms_forward(source, gain_one)
    normalized_rows = norm_one.astype(BF16)
    ranks = jnp.arange(rank, dtype=jnp.int32)
    rank_swap = ((ranks[:, None] ^ (dp_id * rank_part)) == ranks[None, :]).astype(BF16)

    def swap_ranks(block):
        return dot(block, rank_swap).astype(BF16)

    rank_rows = dot(normalized_rows, input_attn).astype(BF16)
    rank_query, rank_key, rank_value = [
        swap_ranks(rank_rows[:, k * rank : (k + 1) * rank]) for k in range(3)
    ]
    is_key = mp_index * kv_width < HEAD_SIZE
    rank_pick = jnp.where(is_key, rank_key, rank_value)
    joint_raw = dot(normalized_rows, joint_weight)
    query_lifted = joint_lifted[:, :heads_width]
    key_value_lifted = joint_lifted[:, heads_width:]
    joint_part = (joint_raw[:, heads_width:] + dot(rank_pick, key_value_lifted)).astype(BF16)
    joint_key_value = lax.all_gather(joint_part, "mp", axis=1, tiled=True)
    query_raw = joint_raw[:, :heads_width] + dot(rank_query, query_lifted)
    query_rows = rotate(
        query_raw.reshape(row_count, heads_here, HEAD_SIZE), head_cos, head_sin
    ).astype(BF16)
    key_rows = rotate(joint_key_value[:, :HEAD_SIZE].astype(F32), cosine, sine_part).astype(BF16)
    value_rows = joint_key_value[:, HEAD_SIZE:]
    attended, logsum = attend(query_rows, key_rows, value_rows, places, segment, factor)
    flat_heads = attended.reshape(row_count, heads_width).astype(BF16)
    chunks = gather_far(near, flat_heads, height)
    branch_part = product(flat_heads, out_weight, 1, 1)
    rank_out_part = product(flat_heads, out_down, 1, 1)
    branch_sum, rank_out = lax.psum(
        (branch_part.astype(BF16), rank_out_part.astype(BF16)), "mp"
    )
    hidden_state = source + branch_sum.astype(F32) + dot(rank_out, model_lifted[0])

    norm_two, inverse_two = rms_forward(hidden_state, gain_two)
    normed_two = norm_two.astype(BF16)
    rank_gu_abs = dot(normed_two, input_ffn).astype(BF16)
    rank_gate = swap_ranks(rank_gu_abs[:, :rank])
    rank_up = swap_ranks(rank_gu_abs[:, rank:])
    grad_rank_down = product(grad_ffn, model_lifted[1], 1, 1).astype(BF16)

    normed_own = jnp.concatenate([normed_two, rank_gate, rank_up], axis=1)
    grad_own = jnp.concatenate([grad_ffn, grad_rank_down], axis=1)
    grad_pair = (grad_own, partner(grad_own))
    grad_t = turn_pass(*grad_pair)
    normed_pair = (after(normed_own, grad_t), partner(normed_own))

    acts, sums = [], ()
    for c in range(CHUNKS):
        *act, own_sum, other_sum = gate_pass(
            normed_pair, grad_pair, chunks[c], slice_width, rank_part, sums, c == CHUNKS - 1
        )
        acts.append(act)
        sums = (own_sum, other_sum)
    normed_t = turn_pass(after(normed_own, sums[1]), normed_pair[1])
    grad_norm_ready = sum_pass(sums[0], partner(sums[1]))
    grad_norm_sum = lax.psum(grad_norm_ready, "mp")

    groups = [range(0, CHUNKS // 2), range(CHUNKS // 2, CHUNKS)]

    def weight_share(items, group, hold):
        held = ()
        for n, c in enumerate(group):
            gated, grad_gate, grad_upper = acts[c]
            if hold is not None:
                grad_gate = after(grad_gate, hold)
            held = weight_pass(
                core,
                normed_t,
                grad_t,
                slice_width,
                rank_part,
                (grad_gate, grad_upper, gated),
                n,
                len(group),
                items(n) if callable(items) else items,
                held,
            )
        return held

    far, last_sent = (), []
    if dp_count == 4:
        far = weight_share([(3, 0, (), BF16), (3, 1, (), BF16)], range(CHUNKS), grad_norm_ready)
        near_one, near_two = trade(far[0], "dp", 1), trade(far[1], "dp", 2)
        blocks = weight_share([(1, 0, (), BF16), (2, 1, (), BF16)], range(CHUNKS), grad_norm_ready)
        first_sent = (trade(blocks[0], "dp", 1), trade(blocks[1], "dp", 2))
        for group in groups:
            blocks = weight_share(
                lambda n, at=group.start: [
                    (1, 1, ((near_two, at + n),), BF16),
                    (2, 0, ((near_one, at + n),), BF16),
                ],
                group,
                grad_norm_ready,
            )
            last_sent.append((trade(blocks[0], "dp", 1), trade(blocks[1], "dp", 2)))

    grad_norm_two = grad_norm_sum[:, :model_width]
    grad_gate_rank = grad_norm_sum[:, model_width : model_width + rank]
    grad_up_rank = grad_norm_sum[:, model_width + rank :]

    acts_down = [after(a[0], *far) for a in acts]
    ffn_own, ffn_given = down_pass(acts_down, chunks, slice_width, rank_part)
    ffn_all = after(sum_pass(ffn_own, partner(ffn_given)), grad_norm_sum)
    half_rows = row_count // 2
    ffn_first, rank_down = lax.psum(
        (ffn_all[:half_rows, :model_width], ffn_all[:, model_width:]), "mp"
    )

    grad_rank_gu = jnp.concatenate([swap_ranks(grad_gate_rank), swap_ranks(grad_up_rank)], axis=1)
    grad_input_ffn = product(normed_two, grad_rank_gu, 0, 0).astype(BF16)
    grad_norm_two = grad_norm_two.astype(F32) + product(grad_rank_gu, input_ffn, 1, 1)
    grad_hidden, grad_gain_two = rms_backward(hidden_state, inverse_two, gain_two, grad_norm_two)
    grad_hidden = grad_hidden + grad_out
    grad_branch = grad_hidden.astype(BF16)

    grad_rank_out = product(grad_branch, model_lifted[0], 1, 1).astype(BF16)
    grad_flat = dot(grad_branch, out_weight) + dot(grad_rank_out, out_down)
    grad_out_down = product(grad_rank_out, flat_heads, 0, 0).astype(BF16)
    grad_w_out = product(grad_branch, flat_heads, 0, 0).astype(BF16)
    grad_att = grad_flat.astype(BF16).reshape(row_count, heads_here, HEAD_SIZE)
    grad_query, grad_keys, grad_values = attend_back(
        query_rows, key_rows, value_rows, places, segment, factor, logsum, grad_att
    )
    grad_query = (
        rotate_back(grad_query, head_cos, head_sin).reshape(row_count, heads_width).astype(BF16)
    )
    grad_joint_all = jnp.concatenate(
        [rotate_back(grad_keys, cosine, sine_part), grad_values], axis=1
    )
    grad_joint_all = grad_joint_all.astype(BF16)
    grad_kv = lax.psum_scatter(
        grad_joint_all, "mp", scatter_dimension=1, tiled=True
    )
    grad_joint = jnp.concatenate([grad_query, grad_kv], axis=1)
    grad_pick = product(grad_kv, key_value_lifted, 1, 1)
    zero_rank = jnp.zeros_like(grad_pick)
    grad_rank_part = [
        product(grad_query, query_lifted, 1, 1),
        jnp.where(is_key, grad_pick, zero_rank),
        jnp.where(is_key, zero_rank, grad_pick),
    ]
    grad_norm_part = product(grad_joint, joint_weight, 1, 1)
    grad_norm_part = jnp.concatenate([grad_norm_part, *grad_rank_part], axis=1).astype(BF16)
    grad_norm_part = after(grad_norm_part, ffn_first)
    if dp_count == 4:
        grad_norm_part = after(grad_norm_part, *first_sent)
    grad_norm_one = lax.psum(grad_norm_part, "mp")
    grad_rank_qkv = [
        grad_norm_one[:, model_width + k * rank : model_width + (k + 1) * rank] for k in range(3)
    ]
    grad_norm_one = grad_norm_one[:, :model_width]
    ffn_last = lax.psum(after(ffn_all[half_rows:, :model_width], grad_norm_one), "mp")
    ffn_sum = jnp.concatenate([ffn_first, ffn_last], axis=0)
    output = hidden_state + ffn_sum.astype(F32) + dot(rank_down, model_lifted[1])
    result_rows = relative(output.astype(BF16), 1, dp_id, dp_count)
    grad_rank_qkv = jnp.concatenate([swap_ranks(g) for g in grad_rank_qkv], axis=1)
    grad_input_attn = product(normalized_rows, grad_rank_qkv, 0, 0).astype(BF16)
    grad_norm_one = grad_norm_one.astype(F32) + product(grad_rank_qkv, input_attn, 1, 1)
    grad_source, grad_gain_one = rms_backward(source, inverse_one, gain_one, grad_norm_one)
    grad_input = relative((grad_source + grad_hidden).astype(BF16), 1, dp_id, dp_count)

    def by_dp(block):
        return block.reshape(dp_count, block.shape[0] // dp_count, block.shape[1])

    def over_cores(block):
        halves = block.reshape(dp_count, 2, part_width, block.shape[1])
        mine = lax.dynamic_index_in_dim(halves, depth_id, 1, keepdims=False)
        theirs = lax.dynamic_index_in_dim(halves, 1 - depth_id, 1, keepdims=False)
        return add_rounded(mine, partner(theirs))

    grad_w_joint = over_cores(product(normalized_rows, grad_joint, 0, 0).astype(BF16))
    grad_lifted = by_dp(
        jnp.concatenate(
            [product(rank_query, grad_query, 0, 0), product(rank_pick, grad_kv, 0, 0)], axis=1
        ).astype(BF16)
    )
    joint_own = scatter_dp(
        [jnp.concatenate([grad_w_joint[p], grad_lifted[p]], axis=0) for p in range(dp_count)],
        grad_norm_part,
    )
    grad_w_out = over_cores(grad_w_out)
    grad_out_down = by_dp(grad_out_down)
    out_own = scatter_dp(
        [jnp.concatenate([grad_w_out[p], grad_out_down[p]], axis=0) for p in range(dp_count)],
        grad_norm_part,
    )
    grad_model = [
        by_dp(relative(product(rank_out, grad_branch, 0, 0).astype(BF16), 1, dp_id, dp_count)),
        by_dp(relative(product(rank_down, grad_ffn, 0, 0).astype(BF16), 1, dp_id, dp_count)),
    ]
    model_own = scatter_dp(
        [jnp.concatenate([g[p] for g in grad_model], axis=0) for p in range(dp_count)],
        grad_norm_part,
    )
    grad_input_ffn = by_dp(grad_input_ffn)
    ffn_in_own = scatter_dp([grad_input_ffn[p] for p in range(dp_count)], grad_norm_part)
    gain_grads = jnp.stack([grad_gain_one, grad_gain_two])
    gain_grads = gain_grads + partner(gain_grads)
    gain_grads = gain_grads.reshape(2, dp_count, 2, part_width)
    gain_grads = lax.dynamic_index_in_dim(gain_grads, depth_id, 2, keepdims=False).astype(BF16)
    grad_input_attn = by_dp(grad_input_attn)
    attn_in_own = scatter_dp(
        [
            jnp.concatenate(
                [grad_input_attn[p], pad_rows(gain_grads[:, p], 16, 3 * rank)], axis=0
            )
            for p in range(dp_count)
        ]
    )
    grad_w_gains = attn_in_own[slice_width : slice_width + 2, :part_width]
    input_own = jnp.concatenate([attn_in_own[:slice_width], ffn_in_own], axis=1)
    grad_lora_in = jnp.stack([input_own[:, k * rank : (k + 1) * rank] for k in range(5)])[None]

    if dp_count == 4:
        mine, theirs = [], []
        for group, (last_one, last_two) in zip(groups, last_sent):
            own_blocks = weight_share(
                lambda n, at=group.start, got=(last_one, last_two): [
                    (0, 0, ((first_sent[0], at + n), (got[1], n)), F32),
                    (0, 1, ((first_sent[1], at + n), (got[0], n)), BF16),
                ],
                group,
                grad_norm_part,
            )
            mine.append(own_blocks[0])
            theirs.append(partner(own_blocks[1]))
    else:
        blocks = [
            weight_share([(p, 0, (), BF16), (p, 1, (), BF16)], range(CHUNKS), None)
            for p in range(dp_count)
        ]
        mine = [scatter_dp([b[0] for b in blocks])]
        theirs = [partner(scatter_dp([b[1] for b in blocks]).astype(BF16))]
    grad_w_gateup, grad_w_down, grad_lora_gateup, grad_lora_hidden = finish_pass(
        core, mine, theirs, part_width, rank_part, hidden
    )

    mixed_rows = jnp.where(keep_own, result_rows, partner(result_rows))
    grad_tokens = jnp.where(keep_own, grad_input, partner(grad_input))
    return (
        mixed_rows,
        grad_tokens,
        joint_own[:part_width, :heads_width],
        joint_own[:part_width, heads_width:],
        out_own[:part_width].T,
        grad_w_gateup,
        grad_w_down,
        grad_w_gains,
        grad_lora_in,
        joint_own[part_width:, :heads_width][None],
        joint_own[part_width:, heads_width:][None],
        out_own[part_width:][None],
        grad_lora_hidden,
        model_own.reshape(1, 2, rank_part, model_width),
        grad_lora_gateup,
    )


def solution(mesh):
    return jax.shard_map(
        local,
        mesh=mesh,
        in_specs=(
            P(("dp", "depth"), None),
            P(("dp", "depth"), None),
            P("dp", None, None),
            P("dp", None),
            P(("dp", "depth"), "mp"),
            P(("dp", "depth"), "mp"),
            P("mp", ("dp", "depth")),
            P(None, ("dp", "depth"), "mp"),
            P("mp", ("dp", "depth")),
            P(None, ("dp", "depth")),
            P("depth", None, "dp", None),
            P("depth", "dp", "mp"),
            P("depth", "dp", "mp"),
            P("depth", "dp", "mp"),
            P("depth", "dp", "mp"),
            P("depth", None, "dp", None),
            P("depth", None, "dp", "mp"),
        ),
        out_specs=(
            P(("dp", "depth"), None),
            P(("dp", "depth"), None),
            P(("dp", "depth"), "mp"),
            P(("dp", "depth"), "mp"),
            P("mp", ("dp", "depth")),
            P(None, ("dp", "depth"), "mp"),
            P("mp", ("dp", "depth")),
            P(None, ("dp", "depth")),
            P("depth", None, "dp", None),
            P("depth", "dp", "mp"),
            P("depth", "dp", "mp"),
            P("depth", "dp", "mp"),
            P("depth", "dp", "mp"),
            P("depth", None, "dp", None),
            P("depth", None, "dp", "mp"),
        ),
        check_vma=False,
    )
```

time: 1990 us -> 1030 us (0.52)
  waiting for transfers between devices: 1520 us -> 419 us
  Pallas kernels: 0 us -> 272 us
  matrix products: 259 us -> 66.5 us
  local copies, waits for them, and re-layouts: 21.7 us -> 103 us
  starting transfers between devices: 3.67 us -> 42.3 us
  blocking collectives: 66.3 us -> 27.7 us
  other arithmetic: 88.6 us -> 66.6 us
    reduce_scatter x18 -> x1, waiting for transfers between devices: 784 us -> 5.99 us  [local(): lax.psum_scatter(grad_joint_all, 'mp', scatter_dimension=1, tiled=True)]
    all_gather x8 -> x1, waiting for transfers between devices: 351 us -> 27.6 us  [local(): lax.all_gather(late, 'mp', axis=0, tiled=False)]
    pallas_call x0 -> x32, Pallas kernels: none -> 272 us  [the longest x4 93.8 us: gate_pass(): pl.pallas_call(functools.partial(gate_kernel, len(pieces), width, rank_pa...]
    ppermute x4 -> x55, waiting for transfers between devices: 3.11 us -> 237 us  [trade(): return lax.ppermute(block, axis, [(i, i ^ mask) for i in range(count)])]
    psum x3 -> x4, waiting for transfers between devices: 355 us -> 148 us  [the longest x1 88.1 us: local(): lax.psum((branch_part.astype(BF16), rank_out_part.astype(BF16)), 'mp')]
    dot_general x28 -> x18, matrix products: 152 us -> 42.9 us  [product(): lax.dot_general(left_op, right_op, (((left_dim,), (right_dim,)), ((), ())...]
    dot_general x20 -> x19, matrix products: 104 us -> 19 us  [dot(): return jnp.dot(left_op, right_op, preferred_element_type=F32)]
    ppermute x4 -> x55, starting transfers between devices: 1.01 us -> 42 us  [trade(): return lax.ppermute(block, axis, [(i, i ^ mask) for i in range(count)])]
  transfers between devices with their start and end apart: 35 -> 61, of which waited for: 29 -> 25; matrix products, arithmetic and copies ran while one was open for 14% -> 16% of each run, Pallas kernels for 0% -> 22%
where the time goes in v1:
time: 1030 us; the launch traced here: 1010 us
  waiting for transfers between devices  419 us (41%)
  Pallas kernels  272 us (26%)
  local copies, waits for them, and re-layouts  103 us (10%)
  other arithmetic  66.6 us (6%)
  matrix products  66.5 us (6%)
  starting transfers between devices  42.3 us (4%)
  blocking collectives  27.7 us (3%)
  between operations  17.7 us (2%)
    ppermute x55, waiting for transfers between devices, trade(): return lax.ppermute(block, axis, [(i, i ^ mask) for i in range(count)])  237 us
    pallas_call x4, Pallas kernels, gate_pass(): pl.pallas_call(functools.partial(gate_kernel, len(pieces), width, rank_pa...  93.8 us
    pallas_call x16, Pallas kernels, weight_pass(): pl.pallas_call(functools.partial(weight_kernel, part, rank_part, tuple((i...  93 us
    psum x1, waiting for transfers between devices, local(): lax.psum((branch_part.astype(BF16), rank_out_part.astype(BF16)), 'mp')  88.1 us
    unnamed x432, local copies, waits for them, and re-layouts  56.3 us
    psum x2, waiting for transfers between devices, local(): lax.psum((ffn_all[:half_rows, :model_width], ffn_all[:, model_width:]), '...  45.8 us
    dot_general x18, matrix products, product(): lax.dot_general(left_op, right_op, (((left_dim,), (right_dim,)), ((), ())...  42.9 us
    ppermute x55, starting transfers between devices, trade(): return lax.ppermute(block, axis, [(i, i ^ mask) for i in range(count)])  42 us
  transfers between devices with their start and end apart: 61, of which 25 were waited for; matrix products, arithmetic and copies ran while one was open for 16% of the time, Pallas kernels for 22%

profile of v1, /device:TPU:0, one launch (start us, length us, event | category | flops | bytes accessed | tf_op | source)
XLA Modules:
  0.0 1014.9 jit_solution(12395390128733805574)
XLA Ops:
  31.8 12.5 %collective-permute-done.3.refs_4_ = bf16[688,768]{1,0:T(8,128)(2,1)} collective-permute-done((bf16[688,768]{1,0:T(8,128)(2,1)}, bf16[688,768]{1,0:T(8,128)(2,1)}, u32[]{:S(2)}, u32[]{:S(2)}) %collective-permute-start.3) | collective-permute-done | bytes 1056800 | tf_op jit(solution)/shard_map/ppermute | solution.py:157
  47.9 17.4 %collective-permute-done.2.refs_3_ = bf16[656,640]{1,0:T(8,128)(2,1)} collective-permute-done((bf16[656,640]{1,0:T(8,128)(2,1)}, bf16[656,640]{1,0:T(8,128)(2,1)}, u32[]{:S(2)}, u32[]{:S(2)}) %collective-permute-start.2) | collective-permute-done | bytes 839712 | tf_op jit(solution)/shard_map/ppermute | solution.py:157
  69.3 17.8 %collective-permute-done.4.refs_5_ = bf16[656,640]{1,0:T(8,128)(2,1)S(1)} collective-permute-done((bf16[656,640]{1,0:T(8,128)(2,1)}, bf16[656,640]{1,0:T(8,128)(2,1)S(1)}, u32[]{:S(2)}, u32[]{:S(2)}) %collective-permute-start.4) | collective-permute-done | bytes 839712 | tf_op jit(solution)/shard_map/ppermute | solution.py:157
  87.1 14.1 %collective-permute-done.6.refs_7_ = bf16[656,640]{1,0:T(8,128)(2,1)S(1)} collective-permute-done((bf16[656,640]{1,0:T(8,128)(2,1)}, bf16[656,640]{1,0:T(8,128)(2,1)S(1)}, u32[]{:S(2)}, u32[]{:S(2)}) %collective-permute-start.6) | collective-permute-done | bytes 839712 | tf_op jit(solution)/shard_map/ppermute | solution.py:157
  135.6 27.7 %all_gather.9 = bf16[512,512]{1,0:T(8,128)(2,1)S(1)} all-gather(bf16[512,128]{1,0:T(8,128)(2,1)S(1)} %fusion.25), channel_id=1, replica_groups=mesh['dp'=4,'depth'=2,'mp'=4] {'mp'}, dimensions={1}, use_global_device_ids=true | all-gather | bytes 655360 | tf_op jit(solution)/shard_map/all_gather | solution.py:1018
  175.9 27.6 %all-gather.3.cloned.1.call-done = bf16[16,512,256]{2,1,0:T(8,128)(2,1)} async-done(((bf16[4,512,256]{2,1,0:T(8,128)(2,1)}), bf16[16,512,256]{2,1,0:T(8,128)(2,1)}) %all-gather.3.cloned.1.call-update) | async-done | bytes 4194320 | tf_op jit(solution)/shard_map/all_gather | solution.py:989
  213.5 88.1 %all-reduce.17.cloned.1.call-done = (bf16[512,256]{1,0:T(8,128)(2,1)}, bf16[512,2048]{1,0:T(8,128)(2,1)}) async-done(((bf16[512,256]{1,0:T(8,128)(2,1)}, bf16[512,2048]{1,0:T(8,128)(2,1)}), (bf16[512,256]{1,0:T(8,128)(2,1)}, bf16[512,2048]{1,0:T(8,128)(2,1)})) %all-reduce.17.cloned.1.call-update) | async-done | bytes 2359312 | tf_op jit(solution)/shard_map/psum | solution.py:1030
  325.6 8.4 turn_pass.2.refs_4_.refs_7_.refs_9_.refs_12_.refs_10_.refs_13_.refs_11_.refs_14_
  334.0 28.4 %collective-permute-done.14.refs_10_.refs_18_ = bf16[1920,512]{1,0:T(8,128)(2,1)} collective-permute-done((bf16[1920,512]{1,0:T(8,128)(2,1)}, bf16[1920,512]{1,0:T(8,128)(2,1)}, u32[]{:S(2)}, u32[]{:S(2)}) %collective-permute-start.14) | collective-permute-done | bytes 1966112 | tf_op jit(solution)/shard_map/ppermute | solution.py:157
  368.2 21.8 %gate_pass.4 = (bf16[1024,512]{1,0:T(8,128)(2,1)S(1)}, bf16[1024,512]{1,0:T(8,128)(2,1)S(1)}, bf16[1024,512]{1,0:T(8,128)(2,1)S(1)}, bf16[512,2560]{1,0:T(8,128)(2,1)}, bf16[512,2560]{1,0:T(8,128)(2,1)}) custom-call(bf16[512,2560]{1,0:T(8,128)(2,1)} %copy-done.2, bf16[512,2560]{1,0:T(8,128)(2,1)} %copy-done.81, ...), custom_call_target="tpu_custom_call" | custom-call | flops 1 | bytes 1 | tf_op jit(solution)/shard_map/gate_pass/pallas_call | solution.py:624
  392.9 23.7 %gate_pass.5 = (bf16[1024,512]{1,0:T(8,128)(2,1)S(1)}, bf16[1024,512]{1,0:T(8,128)(2,1)S(1)}, bf16[1024,512]{1,0:T(8,128)(2,1)S(1)}, bf16[512,2560]{1,0:T(8,128)(2,1)}, bf16[512,2560]{1,0:T(8,128)(2,1)}) custom-call(bf16[512,2560]{1,0:T(8,128)(2,1)} %copy-done.2, bf16[512,2560]{1,0:T(8,128)(2,1)} %copy-done.81, ...), custom_call_target="tpu_custom_call" | custom-call | flops 1 | bytes 1 | tf_op jit(solution)/shard_map/gate_pass/pallas_call | solution.py:624
  420.8 23.6 %gate_pass.6 = (bf16[1024,512]{1,0:T(8,128)(2,1)S(1)}, bf16[1024,512]{1,0:T(8,128)(2,1)S(1)}, bf16[1024,512]{1,0:T(8,128)(2,1)S(1)}, bf16[512,2560]{1,0:T(8,128)(2,1)}, bf16[512,2560]{1,0:T(8,128)(2,1)}) custom-call(bf16[512,2560]{1,0:T(8,128)(2,1)} %copy-done.2, bf16[512,2560]{1,0:T(8,128)(2,1)} %copy-done.81, ...), custom_call_target="tpu_custom_call" | custom-call | flops 1 | bytes 1 | tf_op jit(solution)/shard_map/gate_pass/pallas_call | solution.py:624
  447.4 24.6 %gate_pass.7 = (bf16[1024,512]{1,0:T(8,128)(2,1)S(1)}, bf16[1024,512]{1,0:T(8,128)(2,1)S(1)}, bf16[1024,512]{1,0:T(8,128)(2,1)S(1)}, f32[512,2560]{1,0:T(8,128)}, bf16[512,2560]{1,0:T(8,128)(2,1)}) custom-call(bf16[512,2560]{1,0:T(8,128)(2,1)} %copy-done.2, bf16[512,2560]{1,0:T(8,128)(2,1)} %copy-done.81, bf16[512,2304]{1,0:T(8,128)(2,1)} %pad_maximum_fusion.2.own.refs_2_, ...), custom_call_target="tpu_custom_call" | custom-call | flops 1 | bytes 1 | tf_op jit(solution)/shard_map/gate_pass/pallas_call | solution.py:624
  488.7 8.3 turn_pass.3.refs_3_.refs_5_.refs_6_.refs_8_.refs_10_.refs_11_.refs_9_.refs_12_.refs_13_
  519.1 21.8 %down_pass.1 = (f32[512,2304]{1,0:T(8,128)}, bf16[512,2304]{1,0:T(8,128)(2,1)}) custom-call(bf16[1024,512]{1,0:T(8,128)(2,1)S(1)} %copy-done.12, bf16[1024,512]{1,0:T(8,128)(2,1)S(1)} %copy-done.10, bf16[1024,512]{1,0:T(8,128)(2,1)S(1)} %copy-done.5, bf16[1024,512]{1,0:T(8,128)(2,1)} %copy-done.6, bf16[7680,512]{1,0:T(8,128)(2,1)} %bitcast.187, ...), custom_call_target="tpu_custom_call" | custom-call | flops 1 | bytes 1 | tf_op jit(solution)/shard_map/down_pass/pallas_call | solution.py:689
  574.9 14.5 %all-reduce.11.cloned.1.call-done = bf16[512,2560]{1,0:T(8,128)(2,1)} async-done(((bf16[512,2560]{1,0:T(8,128)(2,1)}), bf16[512,2560]{1,0:T(8,128)(2,1)}) %all-reduce.11.cloned.1.call-update) | async-done | bytes 2621456 | tf_op jit(solution)/shard_map/psum | solution.py:1057
  663.3 45.8 %all-reduce.13.cloned.1.call-done = bf16[256,2048]{1,0:T(8,128)(2,1)} async-done(((bf16[256,2048]{1,0:T(8,128)(2,1)}), bf16[256,2048]{1,0:T(8,128)(2,1)}) %all-reduce.13.cloned.1.call-update) | async-done | bytes 1048592 | tf_op jit(solution)/shard_map/psum | solution.py:1106
  760.2 28.1 %collective-permute-done.47 = bf16[256,512]{1,0:T(8,128)(2,1)S(1)} collective-permute-done((bf16[256,512]{1,0:T(8,128)(2,1)S(1)}, bf16[256,512]{1,0:T(8,128)(2,1)S(1)}, u32[]{:S(2)}, u32[]{:S(2)}) %collective-permute-start.47) | collective-permute-done | bytes 262176 | tf_op jit(solution)/shard_map/ppermute | solution.py:157
  808.1 26.2 %collective-permute-done.37.refs_16_ = bf16[1920,512]{1,0:T(8,128)(2,1)} collective-permute-done((bf16[1920,512]{1,0:T(8,128)(2,1)}, bf16[1920,512]{1,0:T(8,128)(2,1)}, u32[]{:S(2)}, u32[]{:S(2)}) %collective-permute-start.37) | collective-permute-done | bytes 1966112 | tf_op jit(solution)/shard_map/ppermute | solution.py:157
  848.0 28.5 %collective-permute-done.39.refs_16_ = bf16[1920,512]{1,0:T(8,128)(2,1)} collective-permute-done((bf16[1920,512]{1,0:T(8,128)(2,1)}, bf16[1920,512]{1,0:T(8,128)(2,1)}, u32[]{:S(2)}, u32[]{:S(2)}) %collective-permute-start.39) | collective-permute-done | bytes 1966112 | tf_op jit(solution)/shard_map/ppermute | solution.py:157
  899.5 8.7 collective-permute-done.28
  911.6 10.4 %finish_pass.1 = (f32[2,256,4096]{2,1,0:T(8,128)}, f32[4096,256]{1,0:T(8,128)}, f32[1,2,64,4096]{3,2,1,0:T(8,128)}, f32[1,64,4096]{2,1,0:T(8,128)}) custom-call(s32[1]{0:T(128)} %bitcast.1.core, f32[1920,512]{1,0:T(8,128)} %get-tuple-element.262.refs_0_, f32[1920,512]{1,0:T(8,128)} %get-tuple-element.271.refs_1_, ...), custom_call_target="tpu_custom_call" | custom-call | flops 1 | bytes 1 | tf_op jit(solution)/shard_map/finish_pass/pallas_call | solution.py:888
  959.2 7.4 collective-permute-done.53
  986.5 13.1 %collective-permute-done.46 = bf16[528,768]{1,0:T(8,128)(2,1)S(1)} collective-permute-done((bf16[528,768]{1,0:T(8,128)(2,1)S(1)}, bf16[528,768]{1,0:T(8,128)(2,1)S(1)}, u32[]{:S(2)}, u32[]{:S(2)}) %collective-permute-start.46) | collective-permute-done | bytes 811040 | tf_op jit(solution)/shard_map/ppermute | solution.py:157
  (766 shorter events, 448.6 us)
Async XLA Ops:
  7.2 196.2 %all-gather.3.cloned.1.call-start = ((), (), s32[]{:S(2)}) async-start(), calls=%async_computation.4 | async-start | bytes 5242880 | tf_op jit(solution)/shard_map/all_gather | solution.py:989
  20.7 66.4 %collective-permute-start.1 = (bf16[688,768]{1,0:T(8,128)(2,1)}, bf16[688,768]{1,0:T(8,128)(2,1)}, u32[]{:S(2)}, u32[]{:S(2)}) collective-permute-start(bf16[688,768]{1,0:T(8,128)(2,1)} %get-tuple-element.179.refs_0_), channel_id=1, source_target_pairs={{0,8},{8,0},{16,24},{24,16},{1,9},{9,1},{17,25},{25,17},{2,10},{10... | collective-permute-start | bytes 3170312 | tf_op jit(solution)/shard_map/ppermute | solution.py:157
  44.4 73.8 %collective-permute-start.11 = (bf16[3840,512]{1,0:T(8,128)(2,1)}, bf16[3840,512]{1,0:T(8,128)(2,1)}, u32[]{:S(2)}, u32[]{:S(2)}) collective-permute-start(bf16[3840,512]{1,0:T(8,128)(2,1)} %give_pass.1), channel_id=1, source_target_pairs={{0,4},{4,0},{1,5},{5,1},{2,6},{6,2},{3,7},{7,3},{8,12},{12,8},{9,1... | collective-permute-start | bytes 11796488 | tf_op jit(solution)/shard_map/ppermute | solution.py:157
  114.0 187.6 %all-reduce.17.cloned.1.call-start = ((), (), s32[]{:S(2)}) async-start(), calls=%async_computation.6 | async-start | bytes 4718592 | tf_op jit(solution)/shard_map/psum | solution.py:1030
  124.9 192.9 %collective-permute-start.12 = (bf16[7680,512]{1,0:T(8,128)(2,1)}, bf16[7680,512]{1,0:T(8,128)(2,1)}, u32[]{:S(2)}, u32[]{:S(2)}) collective-permute-start(bf16[7680,512]{1,0:T(8,128)(2,1)} %bitcast.177), channel_id=1, source_target_pairs={{0,8},{8,0},{16,24},{24,16},{1,9},{9,1},{17,25},{25,17},{2,10},{10... | collective-permute-start | bytes 23592968 | tf_op jit(solution)/shard_map/ppermute | solution.py:157
  126.4 184.7 %collective-permute-start.13 = (bf16[7680,512]{1,0:T(8,128)(2,1)}, bf16[7680,512]{1,0:T(8,128)(2,1)}, u32[]{:S(2)}, u32[]{:S(2)}) collective-permute-start(bf16[7680,512]{1,0:T(8,128)(2,1)} %bitcast.178), channel_id=1, source_target_pairs={{0,16},{8,24},{16,0},{24,8},{1,17},{9,25},{17,1},{25,9},{2,18},{10... | collective-permute-start | bytes 23592968 | tf_op jit(solution)/shard_map/ppermute | solution.py:157
  175.8 413.6 %all-reduce.11.cloned.1.call-start = ((), (), s32[]{:S(2)}) async-start(), calls=%async_computation.1 | async-start | bytes 5242880 | tf_op jit(solution)/shard_map/psum | solution.py:1057
  213.5 110.6 %collective-permute-start.9 = (bf16[512,2304]{1,0:T(8,128)(2,1)}, bf16[512,2304]{1,0:T(8,128)(2,1)S(1)}, u32[]{:S(2)}, u32[]{:S(2)}) collective-permute-start(bf16[512,2304]{1,0:T(8,128)(2,1)} %pad_maximum_fusion.2.own.refs_2_), channel_id=1, source_target_pairs={{0,4},{4,0},{1,5},{5,1},{2,6},{6,2},{3,7},{7,3},{8,12},{12,8},{9,1... | collective-permute-start | bytes 7077896 | tf_op jit(solution)/shard_map/ppermute | solution.py:157
  323.5 96.0 %collective-permute-start.16 = (bf16[1920,512]{1,0:T(8,128)(2,1)}, bf16[1920,512]{1,0:T(8,128)(2,1)S(1)}, u32[]{:S(2)}, u32[]{:S(2)}) collective-permute-start(bf16[1920,512]{1,0:T(8,128)(2,1)} %get-tuple-element.365), channel_id=1, source_target_pairs={{0,8},{8,0},{16,24},{24,16},{1,9},{9,1},{17,25},{25,17},{2,10},{10... | collective-permute-start | bytes 5898248 | tf_op jit(solution)/shard_map/ppermute | solution.py:157
  324.1 95.5 %collective-permute-start.17 = (bf16[1920,512]{1,0:T(8,128)(2,1)}, bf16[1920,512]{1,0:T(8,128)(2,1)}, u32[]{:S(2)}, u32[]{:S(2)}) collective-permute-start(bf16[1920,512]{1,0:T(8,128)(2,1)} %get-tuple-element.363), channel_id=1, source_target_pairs={{0,16},{8,24},{16,0},{24,8},{1,17},{9,25},{17,1},{25,9},{2,18},{10... | collective-permute-start | bytes 5898248 | tf_op jit(solution)/shard_map/ppermute | solution.py:157
  487.0 169.1 %reduce-scatter.2.cloned.1.call-start = ((), (), s32[]{:S(2)}) async-start(), calls=%async_computation.3 | async-start | bytes 655360 | tf_op jit(solution)/shard_map/reduce_scatter | solution.py:1132
  549.5 175.9 %collective-permute-start.34 = (bf16[3840,512]{1,0:T(8,128)(2,1)}, bf16[3840,512]{1,0:T(8,128)(2,1)}, u32[]{:S(2)}, u32[]{:S(2)}) collective-permute-start(bf16[3840,512]{1,0:T(8,128)(2,1)} %get-tuple-element.227), channel_id=1, source_target_pairs={{0,16},{8,24},{16,0},{24,8},{1,17},{9,25},{17,1},{25,9},{2,18},{10... | collective-permute-start | bytes 11796488 | tf_op jit(solution)/shard_map/ppermute | solution.py:157
  551.0 174.4 %collective-permute-start.35 = (bf16[3840,512]{1,0:T(8,128)(2,1)}, bf16[3840,512]{1,0:T(8,128)(2,1)}, u32[]{:S(2)}, u32[]{:S(2)}) collective-permute-start(bf16[3840,512]{1,0:T(8,128)(2,1)} %get-tuple-element.226), channel_id=1, source_target_pairs={{0,8},{8,0},{16,24},{24,16},{1,9},{9,1},{17,25},{25,17},{2,10},{10... | collective-permute-start | bytes 11796488 | tf_op jit(solution)/shard_map/ppermute | solution.py:157
  567.8 154.7 %collective-permute-start.20 = (bf16[3840,512]{1,0:T(8,128)(2,1)}, bf16[3840,512]{1,0:T(8,128)(2,1)}, u32[]{:S(2)}, u32[]{:S(2)}) collective-permute-start(bf16[3840,512]{1,0:T(8,128)(2,1)} %get-tuple-element.242), channel_id=1, source_target_pairs={{0,8},{8,0},{16,24},{24,16},{1,9},{9,1},{17,25},{25,17},{2,10},{10... | collective-permute-start | bytes 11796488 | tf_op jit(solution)/shard_map/ppermute | solution.py:157
  569.3 153.2 %collective-permute-start.21 = (bf16[3840,512]{1,0:T(8,128)(2,1)}, bf16[3840,512]{1,0:T(8,128)(2,1)}, u32[]{:S(2)}, u32[]{:S(2)}) collective-permute-start(bf16[3840,512]{1,0:T(8,128)(2,1)} %get-tuple-element.243), channel_id=1, source_target_pairs={{0,16},{8,24},{16,0},{24,8},{1,17},{9,25},{17,1},{25,9},{2,18},{10... | collective-permute-start | bytes 11796488 | tf_op jit(solution)/shard_map/ppermute | solution.py:157
  635.3 73.8 %all-reduce.13.cloned.1.call-start = ((), (), s32[]{:S(2)}) async-start(), calls=%async_computation.2 | async-start | bytes 2097152 | tf_op jit(solution)/shard_map/psum | solution.py:1106
  637.8 78.2 %collective-permute-start.29 = (bf16[4,256,512]{2,1,0:T(8,128)(2,1)}, bf16[4,256,512]{2,1,0:T(8,128)(2,1)}, u32[]{:S(2)}, u32[]{:S(2)}) collective-permute-start(bf16[4,256,512]{2,1,0:T(8,128)(2,1)} %dynamic-slice_bitcast_fusion.1), channel_id=1, source_target_pairs={{0,4},{4,0},{1,5},{5,1},{2,6},{6,2},{3,7},{7,3},{8,12},{12,8},{9,1... | collective-permute-start | bytes 3145736 | tf_op jit(solution)/shard_map/ppermute | solution.py:157
  644.7 277.3 %all-reduce.15.cloned.1.call-start = ((), (), s32[]{:S(2)}) async-start(), calls=%async_computation.5 | async-start | bytes 8388608 | tf_op jit(solution)/shard_map/psum | solution.py:1106
  716.0 86.1 %collective-permute-start.24 = (bf16[4,256,640]{2,1,0:T(8,128)(2,1)}, bf16[4,256,640]{2,1,0:T(8,128)(2,1)}, u32[]{:S(2)}, u32[]{:S(2)}) collective-permute-start(bf16[4,256,640]{2,1,0:T(8,128)(2,1)} %dynamic-slice_bitcast_fusion), channel_id=1, source_target_pairs={{0,4},{4,0},{1,5},{5,1},{2,6},{6,2},{3,7},{7,3},{8,12},{12,8},{9,1... | collective-permute-start | bytes 3932168 | tf_op jit(solution)/shard_map/ppermute | solution.py:157
  736.7 70.0 %collective-permute-start.36 = (bf16[1920,512]{1,0:T(8,128)(2,1)}, bf16[1920,512]{1,0:T(8,128)(2,1)}, u32[]{:S(2)}, u32[]{:S(2)}) collective-permute-start(bf16[1920,512]{1,0:T(8,128)(2,1)} %get-tuple-element.257), channel_id=1, source_target_pairs={{0,16},{8,24},{16,0},{24,8},{1,17},{9,25},{17,1},{25,9},{2,18},{10... | collective-permute-start | bytes 5898248 | tf_op jit(solution)/shard_map/ppermute | solution.py:157
  794.4 82.0 %collective-permute-start.39 = (bf16[1920,512]{1,0:T(8,128)(2,1)}, bf16[1920,512]{1,0:T(8,128)(2,1)}, u32[]{:S(2)}, u32[]{:S(2)}) collective-permute-start(bf16[1920,512]{1,0:T(8,128)(2,1)} %get-tuple-element.267), channel_id=1, source_target_pairs={{0,8},{8,0},{16,24},{24,16},{1,9},{9,1},{17,25},{25,17},{2,10},{10... | collective-permute-start | bytes 5898248 | tf_op jit(solution)/shard_map/ppermute | solution.py:157
  805.1 84.5 %collective-permute-start.27 = (bf16[160,640]{1,0:T(8,128)(2,1)S(1)}, bf16[160,640]{1,0:T(8,128)(2,1)S(1)}, u32[]{:S(2)}, u32[]{:S(2)}) collective-permute-start(bf16[160,640]{1,0:T(8,128)(2,1)S(1)} %get-tuple-element.452), channel_id=1, source_target_pairs={{0,8},{8,0},{16,24},{24,16},{1,9},{9,1},{17,25},{25,17},{2,10},{10... | collective-permute-start | bytes 614408 | tf_op jit(solution)/shard_map/ppermute | solution.py:157
  806.7 91.1 %collective-permute-start.50 = (bf16[512,512]{1,0:T(8,128)(2,1)S(1)}, bf16[512,512]{1,0:T(8,128)(2,1)S(1)}, u32[]{:S(2)}, u32[]{:S(2)}) collective-permute-start(bf16[512,512]{1,0:T(8,128)(2,1)S(1)} %copy-done.163), channel_id=1, source_target_pairs={{0,16},{8,24},{16,0},{24,8},{1,17},{9,25},{17,1},{25,9},{2,18},{10... | collective-permute-start | bytes 1572872 | tf_op jit(solution)/shard_map/ppermute | solution.py:157
  834.4 64.9 %collective-permute-start.48 = (bf16[512,512]{1,0:T(8,128)(2,1)S(1)}, bf16[512,512]{1,0:T(8,128)(2,1)S(1)}, u32[]{:S(2)}, u32[]{:S(2)}) collective-permute-start(bf16[512,512]{1,0:T(8,128)(2,1)S(1)} %copy-done.162), channel_id=1, source_target_pairs={{0,8},{8,0},{16,24},{24,16},{1,9},{9,1},{17,25},{25,17},{2,10},{10... | collective-permute-start | bytes 1572872 | tf_op jit(solution)/shard_map/ppermute | solution.py:157
  (254 other events, 3579.1 us)
Sparse Core Ops, SparseCore 0:
  114.1 89.3 all-gather.2
  207.0 94.4 all-reduce.16
  487.1 102.2 all-reduce.10
  635.4 20.6 reduce-scatter.1
  658.9 50.1 all-reduce.12
  740.3 154.2 all-reduce.14

commit v2 on v1

--- a/solution.py
+++ b/solution.py
@@ -80,70 +80,6 @@
 
 def block_mask(places, segment):
     return (segment[:, None] == segment[None, :]) & (places[None, :] <= places[:, None])
-
-
-def attend(query_rows, key_rows, value_rows, places, segment, factor):
-    row_count = query_rows.shape[0]
-    block_rows = min(512, row_count)
-
-    def one_block(block_id):
-        allowed = block_mask(places, segment)
-        scores = (
-            jnp.einsum("qhd,kd->hqk", query_rows, key_rows, preferred_element_type=jnp.float32)
-            * factor
-        )
-        scores = jnp.where(allowed[None], scores, NEGATIVE)
-        row_peak = jnp.max(scores, axis=-1, keepdims=True)
-        powers = jnp.exp(scores - row_peak)
-        row_total = jnp.sum(powers, axis=-1, keepdims=True)
-        attn_weights = (powers / row_total).astype(jnp.bfloat16)
-        block_out = jnp.einsum(
-            "hqk,kd->qhd", attn_weights, value_rows, preferred_element_type=jnp.float32
-        )
-        return (block_out, (row_peak + jnp.log(row_total))[..., 0])
-
-    outputs, logsum = lax.map(one_block, jnp.arange(row_count // block_rows))
-    return (outputs.reshape(query_rows.shape), logsum)
-
-
-def attend_back(query_rows, key_rows, value_rows, places, segment, factor, logsum, grad_att):
-    row_count = query_rows.shape[0]
-    block_rows = min(512, row_count)
-
-    def one_block(carry, block_id):
-        grad_keys, grad_values = carry
-        allowed = block_mask(places, segment)
-        scores = (
-            jnp.einsum("qhd,kd->hqk", query_rows, key_rows, preferred_element_type=jnp.float32)
-            * factor
-        )
-        scores = jnp.where(allowed[None], scores, NEGATIVE)
-        attn_probs = jnp.exp(scores - logsum[block_id][..., None])
-        attn_weights = attn_probs.astype(jnp.bfloat16)
-        grad_probs = jnp.einsum(
-            "qhd,kd->hqk", grad_att, value_rows, preferred_element_type=jnp.float32
-        )
-        grad_values = grad_values + jnp.einsum(
-            "hqk,qhd->kd", attn_weights, grad_att, preferred_element_type=jnp.float32
-        )
-        centre = jnp.sum(grad_probs * attn_probs, axis=-1, keepdims=True)
-        grad_scores = (attn_probs * (grad_probs - centre)).astype(jnp.bfloat16)
-        grad_query = (
-            jnp.einsum("hqk,kd->qhd", grad_scores, key_rows, preferred_element_type=jnp.float32)
-            * factor
-        )
-        grad_keys = (
-            grad_keys
-            + jnp.einsum("hqk,qhd->kd", grad_scores, query_rows, preferred_element_type=jnp.float32)
-            * factor
-        )
-        return ((grad_keys, grad_values), grad_query)
-
-    zero_rows = jnp.zeros(key_rows.shape, jnp.float32)
-    (grad_keys, grad_values), grad_query = lax.scan(
-        one_block, (zero_rows, zero_rows), jnp.arange(row_count // block_rows)
-    )
-    return (grad_query.reshape(query_rows.shape), grad_keys, grad_values)
 
 
 CHUNKS = 4
@@ -178,12 +114,12 @@
     return pieces
 
 
-def gather_pair(one, two):
+def gather_pair(one, two, early):
     count = lax.axis_size("dp")
     if count == 4:
         first_one, first_two = trade(one, "dp", 1), trade(one, "dp", 2)
         second_one, second_two = trade(two, "dp", 1), trade(two, "dp", 2)
-        far = trade(first_two, "dp", 1), trade(second_one, "dp", 2)
+        far = trade(after(first_two, early), "dp", 1), trade(second_one, "dp", 2)
         pieces = [(one, two), (first_one, second_one), (first_two, second_two), far]
         return pieces, far
     ones, twos = gather_dp(one), gather_dp(two)
@@ -260,6 +196,7 @@
 
 VMEM_LIMIT = 50 * 1024 * 1024
 GELU_SCALE = 0.7978845608028654
+LONG = pl.CostEstimate(flops=10**14, bytes_accessed=1, transcendentals=0)
 BRIEF = pl.CostEstimate(flops=1, bytes_accessed=1, transcendentals=0)
 
 
@@ -554,6 +491,285 @@
     return out.reshape(2 * CHUNKS * height, chunk)
 
 
+def simple_pass(kernel, name, inputs, shapes, scalars=None, cost=BRIEF):
+    specs = [whole_spec(a.shape) for a in inputs]
+    if scalars is not None:
+        inputs = (scalars, *inputs)
+        specs = [pl.BlockSpec(memory_space=pltpu.SMEM)] + specs
+    return pl.pallas_call(
+        kernel,
+        grid=(1,),
+        in_specs=specs,
+        out_specs=[whole_spec(shape) for shape, _ in shapes],
+        out_shape=[jax.ShapeDtypeStruct(shape, dtype) for shape, dtype in shapes],
+        compiler_params=params(),
+        cost_estimate=cost,
+        name=name,
+    )(*inputs)
+
+
+def tn(left_op, right_op):
+    return product(left_op, right_op, 0, 0)
+
+
+def rank_order(block, rank, shift):
+    row = lax.broadcasted_iota(jnp.int32, (rank, rank), 0)
+    column = lax.broadcasted_iota(jnp.int32, (rank, rank), 1)
+    swap = (jnp.bitwise_xor(row, shift) == column).astype(F32).astype(BF16)
+    parts = [
+        nn(block[:, at : at + rank], swap).astype(BF16)
+        for at in range(0, block.shape[1], rank)
+    ]
+    return jnp.concatenate(parts, axis=1)
+
+
+def inverse_rms(values):
+    return lax.rsqrt(jnp.mean(values * values, axis=-1, keepdims=True) + EPS)
+
+
+def project_kernel(place, rows, gains, inputs, joint, lifted, cosine, sine, *outs):
+    normed, ranks, query, joint_part = outs
+    heads = query.shape[1]
+    rank = inputs.shape[1] // 3
+    values = rows[...].astype(F32)
+    gain = gains[0:1, :].astype(F32)
+    normed[...] = (values * inverse_rms(values) * gain).astype(BF16)
+    ranks[...] = rank_order(nn(normed[...], inputs[...]).astype(BF16), rank, place[0])
+    raw = nn(normed[...], joint[...])
+    query_raw = raw[:, :heads] + nn(ranks[:, :rank], lifted[:, :heads])
+    for at in range(0, heads, HEAD_SIZE):
+        here = slice(at, at + HEAD_SIZE)
+        query[:, here] = rotate(query_raw[:, here], cosine[...], sine[...]).astype(BF16)
+    pick = jnp.where(place[1] == 1, ranks[:, rank : 2 * rank], ranks[:, 2 * rank :])
+    joint_part[...] = (raw[:, heads:] + nn(pick, lifted[:, heads:])).astype(BF16)
+
+
+def beside(blocks):
+    return jnp.concatenate([blocks[n] for n in range(blocks.shape[0])], axis=1)
+
+
+def head_probs(query, keys, rows_segment, columns_segment):
+    count = query.shape[0]
+    scores = nt(query, keys) * HEAD_SIZE ** (-0.5)
+    row = lax.broadcasted_iota(jnp.int32, (count, count), 0)
+    column = lax.broadcasted_iota(jnp.int32, (count, count), 1)
+    allowed = (rows_segment == columns_segment) & (column <= row)
+    scores = jnp.where(allowed, scores, NEGATIVE)
+    powers = jnp.exp(scores - jnp.max(scores, axis=-1, keepdims=True))
+    return powers / jnp.sum(powers, axis=-1, keepdims=True)
+
+
+def attend_kernel(query, joint, cosine, sine, row_seg, column_seg, output, down, *outs):
+    keys, flat, branch = outs
+    width = output.shape[0]
+    both = beside(joint)
+    keys[...] = rotate(both[:, :HEAD_SIZE].astype(F32), cosine[...], sine[...]).astype(BF16)
+    for at in range(0, flat.shape[1], HEAD_SIZE):
+        here = slice(at, at + HEAD_SIZE)
+        probs = head_probs(query[:, here], keys[...], row_seg[...], column_seg[...])
+        flat[:, here] = nn(probs.astype(BF16), both[:, HEAD_SIZE:]).astype(BF16)
+    branch[:, :width] = nt(flat[...], output[...]).astype(BF16)
+    branch[:, width:] = nt(flat[...], down[...]).astype(BF16)
+
+
+def second_kernel(place, rows, branch, model, gains, inputs, hidden, normed):
+    width = rows.shape[1]
+    rank = model.shape[1]
+    hidden[...] = (
+        rows[...].astype(F32)
+        + branch[:, :width].astype(F32)
+        + nn(branch[:, width:], model[0])
+    )
+    values = hidden[...]
+    gain = gains[1:2, :].astype(F32)
+    normed[:, :width] = (values * inverse_rms(values) * gain).astype(BF16)
+    normed[:, width:] = rank_order(
+        nn(normed[:, :width], inputs[...]).astype(BF16), rank, place[0]
+    )
+
+
+def early_kernel(block, early, late):
+    rows, columns = early.shape[0], block.shape[1]
+    early[:, :columns] = block[:rows, :]
+    early[:, columns:] = block[rows:, columns - (early.shape[1] - columns) :]
+    late[...] = block[rows:, : late.shape[1]]
+
+
+def grad_kernel(rows, model, grad):
+    width = rows.shape[1]
+    grad[:, :width] = rows[...]
+    grad[:, width:] = nt(rows[...], model[1]).astype(BF16)
+
+
+def norm_back(values, gain, grad_norm):
+    inverse = inverse_rms(values)
+    weighted = grad_norm * gain
+    grad_values = inverse * weighted - values * inverse**3 * jnp.mean(
+        weighted * values, axis=-1, keepdims=True
+    )
+    return grad_values, jnp.sum(grad_norm * values * inverse, axis=0, keepdims=True)
+
+
+def attend_back_kernel(place, summed, hidden, gains, inputs, grad_ffn, model, *refs):
+    output, down, query, keys, joint, cosine, sine, row_seg, column_seg = refs[:9]
+    grad_hidden, branch, rank_gu, rank_out, grad_query, grad_joint, grad_gain = refs[9:]
+    width = hidden.shape[1]
+    rank = down.shape[0]
+    factor = HEAD_SIZE ** (-0.5)
+    rank_gu[...] = rank_order(summed[:, width:], rank, place[0])
+    grad_norm = summed[:, :width].astype(F32) + nt(rank_gu[...], inputs[...])
+    values, gain_row = norm_back(hidden[...], gains[1:2, :].astype(F32), grad_norm)
+    grad_gain[...] = jnp.broadcast_to(gain_row, grad_gain.shape)
+    grad_hidden[...] = values + grad_ffn[...].astype(F32)
+    branch[...] = grad_hidden[...].astype(BF16)
+    rank_out[...] = nt(branch[...], model[0]).astype(BF16)
+    grad_flat = (nn(branch[...], output[...]) + nn(rank_out[...], down[...])).astype(BF16)
+    values_here = beside(joint)[:, HEAD_SIZE:]
+    grad_keys = grad_values = 0.0
+    for at in range(0, query.shape[1], HEAD_SIZE):
+        here = slice(at, at + HEAD_SIZE)
+        probs = head_probs(query[:, here], keys[...], row_seg[...], column_seg[...])
+        grad_probs = nt(grad_flat[:, here], values_here)
+        grad_values += tn(probs.astype(BF16), grad_flat[:, here])
+        centre = jnp.sum(grad_probs * probs, axis=-1, keepdims=True)
+        grad_scores = (probs * (grad_probs - centre)).astype(BF16)
+        turned = rotate_back(nn(grad_scores, keys[...]) * factor, cosine[...], sine[...])
+        grad_query[:, here] = turned.astype(BF16)
+        grad_keys += tn(grad_scores, query[:, here]) * factor
+    both = jnp.concatenate([rotate_back(grad_keys, cosine[...], sine[...]), grad_values], axis=1)
+    kv = grad_joint.shape[2]
+    for n in range(grad_joint.shape[0]):
+        grad_joint[n] = both[:, n * kv : (n + 1) * kv].astype(BF16)
+
+
+def project_back_kernel(place, grad_query, grad_kv, joint, lifted, out):
+    heads = grad_query.shape[1]
+    width, rank = joint.shape[0], lifted.shape[0]
+    out[:, :width] = (
+        nt(grad_query[...], joint[:, :heads]) + nt(grad_kv[...], joint[:, heads:])
+    ).astype(BF16)
+    pick = nt(grad_kv[...], lifted[:, heads:]).astype(BF16)
+    none = jnp.zeros_like(pick)
+    out[:, width : width + rank] = nt(grad_query[...], lifted[:, :heads]).astype(BF16)
+    out[:, width + rank : width + 2 * rank] = jnp.where(place[1] == 1, pick, none)
+    out[:, width + 2 * rank :] = jnp.where(place[1] == 1, none, pick)
+
+
+def first_back_kernel(place, summed, rows, gains, inputs, grad_hidden, *outs):
+    grad_rows, ranks, grad_gain = outs
+    width = rows.shape[1]
+    ranks[...] = rank_order(summed[:, width:], inputs.shape[1] // 3, place[0])
+    grad_norm = summed[:, :width].astype(F32) + nt(ranks[...], inputs[...])
+    values, gain_row = norm_back(rows[...].astype(F32), gains[0:1, :].astype(F32), grad_norm)
+    grad_gain[...] = jnp.broadcast_to(gain_row, grad_gain.shape)
+    grad_rows[...] = (values + grad_hidden[...]).astype(BF16)
+
+
+def folded(block, width):
+    blocks = [block[:, at : at + width] for at in range(0, block.shape[1], width)]
+    return blocks[0] if len(blocks) == 1 else jnp.concatenate(blocks, axis=0)
+
+
+def share_of(block, first, rows):
+    total = jnp.zeros((rows, block.shape[1]), block.dtype)
+    for at in range(0, block.shape[0], rows):
+        total = jnp.where(first == at, block[at : at + rows], total)
+    return total
+
+
+def shares_kernel(count, share_rows, share_columns, place, normed, grad_query, grad_kv, ranks, branch, flat, *refs):
+    rank_out, out_sum, second, rank_gu, down_sum, grad_ffn = refs[:6]
+    mine, theirs, *rest = refs[6:]
+    heads, kv = grad_query.shape[1], grad_kv.shape[1]
+    width = normed.shape[1]
+    rank = rank_out.shape[1]
+    part, rank_part = width // (2 * count), rank // count
+    own_first = place[2] == 0
+    pick = jnp.where(place[1] == 1, ranks[:, rank : 2 * rank], ranks[:, 2 * rank : 3 * rank])
+
+    def put(target, p, start, block):
+        target[p, start : start + block.shape[0], :] = block.astype(BF16)
+        return start + block.shape[0]
+
+    def put_rest(p, start, block):
+        rest[p][start : start + block.shape[0], :] = block.astype(BF16)
+        return start + block.shape[0]
+
+    lift_query = tn(ranks[:, :rank], grad_query[...])
+    lift_kv = tn(pick, grad_kv[...])
+    out_down = tn(rank_out[...], flat[...])
+    for p in range(count):
+        columns = slice(2 * p * part, 2 * (p + 1) * part)
+        here = slice(p * rank_part, (p + 1) * rank_part)
+        query = tn(normed[:, columns], grad_query[...])
+        joint = tn(normed[:, columns], grad_kv[...])
+        output = tn(branch[:, columns], flat[...])
+        quarter = part * kv // heads
+        for side, target in ((0, mine), (1, theirs)):
+            first = [jnp.where(own_first, b[:part], b[part:]) for b in (query, joint, output)]
+            other = [jnp.where(own_first, b[part:], b[:part]) for b in (query, joint, output)]
+            blocks = first if side == 0 else other
+            put(target, p, 0, blocks[0])
+            for n in range(part // quarter):
+                target[p, part : part + quarter, n * kv : (n + 1) * kv] = blocks[1][
+                    n * quarter : (n + 1) * quarter
+                ].astype(BF16)
+            put(target, p, part + quarter, blocks[2])
+        at = put_rest(p, 0, lift_query[here])
+        small = rank_part * kv // heads
+        for n in range(rank_part // small):
+            rest[p][at : at + small, n * kv : (n + 1) * kv] = lift_kv[
+                p * rank_part + n * small : p * rank_part + (n + 1) * small
+            ].astype(BF16)
+        at = put_rest(p, at + small, out_down[here])
+        here_columns = pl.multiple_of(place[4], 128)
+        for ranks_of, rows_of in ((out_sum, branch), (down_sum, grad_ffn)):
+            value = tn(ranks_of[:, here], rows_of[:, pl.ds(here_columns, share_columns)])
+            for block in range(0, share_columns, heads):
+                at = put_rest(p, at, value[:, block : block + heads])
+        if share_rows % 128 == 0:
+            first = pl.multiple_of(2 * p * part + place[5], 128)
+            value = tn(second[:, pl.ds(first, share_rows)], rank_gu[...])
+        else:
+            value = share_of(tn(second[:, columns], rank_gu[...]), place[5], share_rows)
+        for block in range(0, value.shape[1], heads):
+            at = put_rest(p, at, value[:, block : block + heads])
+
+
+def add_kernel(*refs):
+    total = 0.0
+    for ref in refs[:-1]:
+        total += ref[...].astype(F32).reshape(refs[-1].shape)
+    refs[-1][...] = total.astype(refs[-1].dtype)
+
+
+def add_pass(dtype, *blocks):
+    inputs, specs = [], []
+    for block in blocks:
+        if isinstance(block, tuple):
+            block, at = block
+            specs.append(
+                pl.BlockSpec(
+                    (1, *block.shape[1:]), functools.partial(lambda at, t: (at, 0, 0), at)
+                )
+            )
+            shape = block.shape[1:]
+        else:
+            specs.append(whole_spec(block.shape))
+            shape = block.shape
+        inputs.append(block)
+    return pl.pallas_call(
+        add_kernel,
+        grid=(1,),
+        in_specs=specs,
+        out_specs=whole_spec(shape),
+        out_shape=jax.ShapeDtypeStruct(shape, dtype),
+        compiler_params=params(),
+        cost_estimate=BRIEF,
+        name="add_pass",
+    )(*inputs)
+
+
 def gate_kernel(count, width, rank_part, has_base, *refs):
     blocks, refs = refs[:4], refs[4:]
     pieces = [(refs[2 * p], refs[2 * p + 1]) for p in range(count)]
@@ -561,6 +777,7 @@
     bases, refs = (refs[:2], refs[2:]) if has_base else ((), refs)
     gated_ref, gate_ref, upper_ref, *outs = refs[:5]
     adapters = refs[5]
+    start = pl.program_id(0) == 0
     rows = blocks[0].shape[0]
     part = width // 2
     rank = count * rank_part
@@ -598,8 +815,9 @@
 
     def put(b, first, value):
         columns = slice(first, first + value.shape[1])
-        if bases:
-            value = value + bases[b][:, columns].astype(F32)
+        before = outs[b][:, columns].astype(F32)
+        base = bases[b][:, columns].astype(F32) if bases else jnp.zeros_like(before)
+        value = value + jnp.where(start, base, before)
         outs[b][:, columns] = value.astype(outs[b].dtype)
 
     for p in range(count):
@@ -614,34 +832,31 @@
         put(b, model_width + rank, nt(upper_ref[span, :], adapters[3 * b + 1]))
 
 
-def gate_pass(normed_pair, grad_pair, pieces, width, rank_part, bases, last):
+def gate_pass(normed_pair, grad_pair, chunks, width, rank_part, bases, last):
     blocks = (*normed_pair, *grad_pair)
     rows, columns = blocks[0].shape
-    both_rows = 2 * rows
-    pairs = [block for pair in pieces for block in pair]
+    both_rows, size = 2 * rows, len(chunks)
+    pairs = [block for pair in chunks[0] for block in pair]
     height = 3 * (width // 2 + rank_part)
     chunk = pairs[0][0].shape[1]
+    tiled = pl.BlockSpec((both_rows, chunk), lambda t: (0, t))
     return pl.pallas_call(
-        functools.partial(gate_kernel, len(pieces), width, rank_part, bool(bases)),
-        grid=(1,),
+        functools.partial(gate_kernel, len(chunks[0]), width, rank_part, bool(bases)),
+        grid=(size,),
         in_specs=[whole_spec(a.shape) for a in blocks]
         + [
-            pl.BlockSpec(
-                (height, chunk),
-                functools.partial(lambda at, t: (at, 0), at),
-                pipeline_mode=pl.Buffered(1),
-            )
+            pl.BlockSpec((height, chunk), functools.partial(lambda at, t: (at + t, 0), at))
             for _, at in pairs
         ]
         + [whole_spec(a.shape) for a in bases],
-        out_specs=[whole_spec((both_rows, chunk))] * 3 + [whole_spec((rows, columns))] * 2,
-        out_shape=[jax.ShapeDtypeStruct((both_rows, chunk), BF16)] * 3
+        out_specs=[tiled] * 3 + [whole_spec((rows, columns))] * 2,
+        out_shape=[jax.ShapeDtypeStruct((both_rows, size * chunk), BF16)] * 3
         + [
             jax.ShapeDtypeStruct((rows, columns), F32 if last else BF16),
             jax.ShapeDtypeStruct((rows, columns), BF16),
         ],
-        scratch_shapes=[pltpu.VMEM((6, len(pieces) * rank_part, chunk), BF16)],
-        compiler_params=params(),
+        scratch_shapes=[pltpu.VMEM((6, len(chunks[0]) * rank_part, chunk), BF16)],
+        compiler_params=pltpu.CompilerParams(vmem_limit_bytes=60 * 1024 * 1024),
         cost_estimate=BRIEF,
         name="gate_pass",
     )(*blocks, *[block for block, _ in pairs], *bases)
@@ -677,7 +892,8 @@
 
 def down_pass(acts, chunks, width, rank_part):
     count = len(chunks[0])
-    both_rows, chunk = acts[0].shape
+    both_rows = acts[0][0].shape[0]
+    chunk = chunks[0][0][0][0].shape[1]
     rows = both_rows // 2
     columns = count * (width + rank_part)
     height = 3 * (width // 2 + rank_part)
@@ -689,7 +905,14 @@
     return pl.pallas_call(
         functools.partial(down_kernel, count, rows, width, rank_part, len(chunks)),
         grid=(1,),
-        in_specs=[whole_spec(a.shape) for a in acts]
+        in_specs=[
+            pl.BlockSpec(
+                (both_rows, chunk),
+                functools.partial(lambda n, t: (0, n), n),
+                pipeline_mode=pl.Buffered(1),
+            )
+            for _, n in acts
+        ]
         + [
             pl.BlockSpec(
                 (height, chunk),
@@ -704,26 +927,35 @@
         compiler_params=params(),
         cost_estimate=BRIEF,
         name="down_pass",
-    )(*acts, *[block for block, _ in pairs])
-
-
-def sum_kernel(own, other, total):
-    total[...] = (own[...].astype(F32) + other[...].astype(F32)).astype(BF16)
-
-
-def sum_pass(own, other):
-    rows, columns = own.shape
-    tile = pl.BlockSpec((rows // 4, columns), lambda t: (t, 0))
+    )(*[a for a, _ in acts], *[block for block, _ in pairs])
+
+
+def sum_kernel(*refs):
+    total = refs[0][...].astype(F32)
+    for other in refs[1:-1]:
+        total = total + other[...].astype(F32)
+    refs[-1][...] = total.astype(BF16)
+
+
+def sum_pass(*blocks):
+    blocks = [b if isinstance(b, tuple) else (b, 0) for b in blocks]
+    rows, columns = min((b.shape for b, _ in blocks), key=lambda shape: shape[0])
+    steps = 4
     return pl.pallas_call(
         sum_kernel,
-        grid=(4,),
-        in_specs=[tile, tile],
-        out_specs=tile,
+        grid=(steps,),
+        in_specs=[
+            pl.BlockSpec(
+                (rows // steps, columns), functools.partial(lambda at, t: (at * steps + t, 0), at)
+            )
+            for _, at in blocks
+        ],
+        out_specs=pl.BlockSpec((rows // steps, columns), lambda t: (t, 0)),
         out_shape=jax.ShapeDtypeStruct((rows, columns), BF16),
         compiler_params=params(),
         cost_estimate=BRIEF,
         name="sum_pass",
-    )(own, other)
+    )(*[b for b, _ in blocks])
 
 
 def turn_kernel(own, other, turned):
@@ -771,9 +1003,8 @@
             store(3 * part + n * rank_part, nn(ranks[n][:, span], act[span, :]))
 
 
-def weight_pass(core, normed_t, grad_t, width, rank_part, acts, at, count, items, held=()):
+def weight_pass(core, normed_t, grad_t, width, rank_part, acts, chunk, at, count, items, held=()):
     both_rows = normed_t.shape[1]
-    chunk = acts[0].shape[1]
     part = width // 2
     height = 3 * (part + rank_part)
     tile = min(256, chunk)
@@ -793,8 +1024,14 @@
         )
 
     tiled = pl.BlockSpec((height, tile), lambda t, core: (at, t))
-    inputs = list(acts)
-    specs = [pl.BlockSpec((both_rows, tile), lambda t, core: (0, t)) for _ in acts]
+    inputs = [a for a, _ in acts]
+    specs = [
+        pl.BlockSpec(
+            (both_rows, tile),
+            functools.partial(lambda n, t, core: (0, n * (chunk // tile) + t), n),
+        )
+        for _, n in acts
+    ]
     for index, side, added, _ in items:
         inputs += [normed_t, grad_t, normed_t, normed_t, grad_t, *[block for block, _ in added]]
         specs += [rows_of(index, side)] * 2
@@ -827,17 +1064,18 @@
     )(core, *inputs, *held)
 
 
-def finish_kernel(part, rank_part, groups, core, *refs):
+def finish_kernel(part, rank_part, core, *refs):
+    *mine, other = refs[:-4]
     gate_up, down, lora_gate_up, lora_hidden = refs[-4:]
-    for n, source in enumerate(refs[:-4]):
-        here = pl.program_id(0) == n // groups
-        if groups > 1:
-            here &= pl.program_id(1) // (CHUNKS // groups) == n % groups
-
-        @pl.when(here)
-        def _(source=source):
+    for side, sources in enumerate((mine, [other])):
+
+        @pl.when(pl.program_id(0) == side)
+        def _(sources=sources):
             def rows(start, height):
-                return source[start : start + height, :].astype(F32)
+                total = sources[0][start : start + height, :].astype(F32)
+                for source in sources[1:]:
+                    total = total + source[start : start + height, :].astype(F32)
+                return total
 
             gate_up[0] = rows(0, part)
             gate_up[1] = rows(part, part)
@@ -848,17 +1086,14 @@
 
 
 def finish_pass(core, mine, other, part, rank_part, hidden):
-    chunk = mine[0].shape[1]
-    groups = len(mine)
-    size = CHUNKS // groups
-    height = mine[0].shape[0] // size
-
-    def source(side, group):
-        def index(s, q, core):
-            inside = jnp.clip(q - group * size, 0, size - 1)
-            return (jnp.where(s == side, inside, (size - 1) * (1 - side)), 0)
-
-        return pl.BlockSpec((height, chunk), index)
+    chunk = other.shape[1]
+    height = other.shape[0] // CHUNKS
+
+    def source(side, first=0):
+        return pl.BlockSpec(
+            (height, chunk),
+            lambda s, q, core: (first + jnp.where(s == side, q, (CHUNKS - 1) * (1 - side)), 0),
+        )
 
     def column(s, q, core):
         return (core[0] ^ s) * CHUNKS + q
@@ -875,7 +1110,7 @@
     grid_spec = pltpu.PrefetchScalarGridSpec(
         num_scalar_prefetch=1,
         grid=(2, CHUNKS),
-        in_specs=[source(side, group) for side in range(2) for group in range(groups)],
+        in_specs=[source(0, first) for _, first in mine] + [source(1)],
         out_specs=[
             pl.BlockSpec((2, part, chunk), lambda s, q, core: (0, 0, column(s, q, core))),
             pl.BlockSpec((chunk, part), lambda s, q, core: (column(s, q, core), 0)),
@@ -886,13 +1121,13 @@
         ],
     )
     return pl.pallas_call(
-        functools.partial(finish_kernel, part, rank_part, groups),
+        functools.partial(finish_kernel, part, rank_part),
         grid_spec=grid_spec,
         out_shape=shapes,
         compiler_params=params(),
         cost_estimate=BRIEF,
         name="finish_pass",
-    )(core, *mine, *other)
+    )(core, *[block for block, _ in mine], other)
 
 
 def dot(left_op, right_op):
@@ -952,14 +1187,9 @@
     seq_lens = lengths[0, slot_id]
     places, segment, within, valid_rows = layout(seq_lens, row_count)
     cosine, sine_part = rotary(within, HEAD_SIZE)
-    head_cos = cosine[:, None, :]
-    head_sin = sine_part[:, None, :]
-    factor = HEAD_SIZE ** (-0.5)
     tok_rows = relative(jnp.where(keep_own, tokens, tok_swap), 1, dp_id, dp_count)
-    source = tok_rows.astype(F32)
     grad_rows = relative(jnp.where(keep_own, cotangent, grad_swap), 1, dp_id, dp_count)
-    grad_out = grad_rows.astype(F32) * valid_rows[:, None]
-    grad_ffn = grad_out.astype(BF16)
+    grad_ffn = (grad_rows.astype(F32) * valid_rows[:, None]).astype(BF16)
 
     mp_count = lax.axis_size("mp")
     share_rows = slice_width // mp_count
@@ -976,15 +1206,13 @@
         rank,
     )
     bundle = bundle_pass(core, ffn_arrays, taken, chunk)
-    pieces, hold = gather_pair(*bundles)
+    pieces, hold = gather_pair(*bundles, bundle)
     shared_own, input_attn, late, joint_lifted, out_down = unpack_pass(
         pieces, part_width, rank_part, rank, share_rows, share_columns, heads_width
     )
     joint_weight, out_weight, gains_all = shared_pass(
         core, shared_own, partner(shared_own), dp_count, part_width, heads_width
     )
-    gains_all = gains_all[:2].astype(F32)
-    gain_one, gain_two = gains_all[0], gains_all[1]
     model_all, input_ffn = late_pass(
         lax.all_gather(late, "mp", axis=0, tiled=False),
         share_rows,
@@ -992,78 +1220,83 @@
         rank_part,
     )
     model_all = relative(model_all, 2, dp_id, dp_count)
-    model_lifted = [model_all[0], model_all[1]]
 
     near = gather_near(after(bundle, *hold))
     height = 3 * (part_width + rank_part)
 
-    norm_one, inverse_one = rms_forward(source, gain_one)
-    normalized_rows = norm_one.astype(BF16)
-    ranks = jnp.arange(rank, dtype=jnp.int32)
-    rank_swap = ((ranks[:, None] ^ (dp_id * rank_part)) == ranks[None, :]).astype(BF16)
-
-    def swap_ranks(block):
-        return dot(block, rank_swap).astype(BF16)
-
-    rank_rows = dot(normalized_rows, input_attn).astype(BF16)
-    rank_query, rank_key, rank_value = [
-        swap_ranks(rank_rows[:, k * rank : (k + 1) * rank]) for k in range(3)
-    ]
     is_key = mp_index * kv_width < HEAD_SIZE
-    rank_pick = jnp.where(is_key, rank_key, rank_value)
-    joint_raw = dot(normalized_rows, joint_weight)
-    query_lifted = joint_lifted[:, :heads_width]
-    key_value_lifted = joint_lifted[:, heads_width:]
-    joint_part = (joint_raw[:, heads_width:] + dot(rank_pick, key_value_lifted)).astype(BF16)
-    joint_key_value = lax.all_gather(joint_part, "mp", axis=1, tiled=True)
-    query_raw = joint_raw[:, :heads_width] + dot(rank_query, query_lifted)
-    query_rows = rotate(
-        query_raw.reshape(row_count, heads_here, HEAD_SIZE), head_cos, head_sin
-    ).astype(BF16)
-    key_rows = rotate(joint_key_value[:, :HEAD_SIZE].astype(F32), cosine, sine_part).astype(BF16)
-    value_rows = joint_key_value[:, HEAD_SIZE:]
-    attended, logsum = attend(query_rows, key_rows, value_rows, places, segment, factor)
-    flat_heads = attended.reshape(row_count, heads_width).astype(BF16)
+    place = jnp.stack([dp_id * rank_part, is_key.astype(jnp.int32), depth_id, dp_id]
+        + [((mp_index * share_columns // slice_width) ^ dp_id) * slice_width + mp_index * share_columns % slice_width, mp_index * share_rows]).astype(jnp.int32)
+    row_segment, column_segment = segment[:, None], segment[None, :]
+    normalized_rows, rank_rows, query_rows, joint_part = simple_pass(
+        project_kernel,
+        "project_pass",
+        (tok_rows, gains_all, input_attn, joint_weight, joint_lifted, cosine, sine_part),
+        [
+            ((row_count, model_width), BF16),
+            ((row_count, 3 * rank), BF16),
+            ((row_count, heads_width), BF16),
+            ((row_count, kv_width), BF16),
+        ],
+        place,
+    )
+    joint_key_value = lax.all_gather(joint_part, "mp", axis=0, tiled=False)
+    key_rows, flat_heads, branch_part = simple_pass(
+        attend_kernel,
+        "attend_pass",
+        (query_rows, joint_key_value, cosine, sine_part, row_segment, column_segment)
+        + (out_weight, out_down),
+        [
+            ((row_count, HEAD_SIZE), BF16),
+            ((row_count, heads_width), BF16),
+            ((row_count, model_width + rank), BF16),
+        ],
+    )
     chunks = gather_far(near, flat_heads, height)
-    branch_part = product(flat_heads, out_weight, 1, 1)
-    rank_out_part = product(flat_heads, out_down, 1, 1)
-    branch_sum, rank_out = lax.psum(
-        (branch_part.astype(BF16), rank_out_part.astype(BF16)), "mp"
-    )
-    hidden_state = source + branch_sum.astype(F32) + dot(rank_out, model_lifted[0])
-
-    norm_two, inverse_two = rms_forward(hidden_state, gain_two)
-    normed_two = norm_two.astype(BF16)
-    rank_gu_abs = dot(normed_two, input_ffn).astype(BF16)
-    rank_gate = swap_ranks(rank_gu_abs[:, :rank])
-    rank_up = swap_ranks(rank_gu_abs[:, rank:])
-    grad_rank_down = product(grad_ffn, model_lifted[1], 1, 1).astype(BF16)
-
-    normed_own = jnp.concatenate([normed_two, rank_gate, rank_up], axis=1)
-    grad_own = jnp.concatenate([grad_ffn, grad_rank_down], axis=1)
+    branch_sum = lax.psum(branch_part, "mp")
+    rank_out = branch_sum[:, model_width:]
+
+    hidden_state, normed_own = simple_pass(
+        second_kernel,
+        "second_pass",
+        (tok_rows, branch_sum, model_all, gains_all, input_ffn),
+        [((row_count, model_width), F32), ((row_count, model_width + 2 * rank), BF16)],
+        place,
+    )
+    (grad_own,) = simple_pass(
+        grad_kernel,
+        "grad_pass",
+        (grad_ffn, model_all),
+        [((row_count, model_width + rank), BF16)],
+    )
     grad_pair = (grad_own, partner(grad_own))
     grad_t = turn_pass(*grad_pair)
     normed_pair = (after(normed_own, grad_t), partner(normed_own))
 
     acts, sums = [], ()
-    for c in range(CHUNKS):
+    size = CHUNKS // GROUPS
+    for group in range(GROUPS):
         *act, own_sum, other_sum = gate_pass(
-            normed_pair, grad_pair, chunks[c], slice_width, rank_part, sums, c == CHUNKS - 1
+            normed_pair,
+            grad_pair,
+            chunks[group * size : (group + 1) * size],
+            slice_width,
+            rank_part,
+            sums,
+            group == GROUPS - 1,
         )
-        acts.append(act)
+        acts += [[(a, n) for a in act] for n in range(size)]
         sums = (own_sum, other_sum)
     normed_t = turn_pass(after(normed_own, sums[1]), normed_pair[1])
     grad_norm_ready = sum_pass(sums[0], partner(sums[1]))
+    first_space = partner(grad_norm_ready[:16])
     grad_norm_sum = lax.psum(grad_norm_ready, "mp")
 
-    groups = [range(0, CHUNKS // 2), range(CHUNKS // 2, CHUNKS)]
-
-    def weight_share(items, group, hold):
-        held = ()
-        for n, c in enumerate(group):
+    def weight_share(items, hold, held=(), start=0, count=CHUNKS):
+        for c in range(CHUNKS):
             gated, grad_gate, grad_upper = acts[c]
             if hold is not None:
-                grad_gate = after(grad_gate, hold)
+                grad_gate = (after(grad_gate[0], hold), grad_gate[1])
             held = weight_pass(
                 core,
                 normed_t,
@@ -1071,135 +1304,191 @@
                 slice_width,
                 rank_part,
                 (grad_gate, grad_upper, gated),
-                n,
-                len(group),
-                items(n) if callable(items) else items,
+                chunk,
+                start + c,
+                count,
+                items,
                 held,
             )
         return held
 
-    far, last_sent = (), []
+    sends, held, last_sent = (), (), ()
     if dp_count == 4:
-        far = weight_share([(3, 0, (), BF16), (3, 1, (), BF16)], range(CHUNKS), grad_norm_ready)
-        near_one, near_two = trade(far[0], "dp", 1), trade(far[1], "dp", 2)
-        blocks = weight_share([(1, 0, (), BF16), (2, 1, (), BF16)], range(CHUNKS), grad_norm_ready)
-        first_sent = (trade(blocks[0], "dp", 1), trade(blocks[1], "dp", 2))
-        for group in groups:
-            blocks = weight_share(
-                lambda n, at=group.start: [
-                    (1, 1, ((near_two, at + n),), BF16),
-                    (2, 0, ((near_one, at + n),), BF16),
-                ],
-                group,
-                grad_norm_ready,
-            )
-            last_sent.append((trade(blocks[0], "dp", 1), trade(blocks[1], "dp", 2)))
-
-    grad_norm_two = grad_norm_sum[:, :model_width]
-    grad_gate_rank = grad_norm_sum[:, model_width : model_width + rank]
-    grad_up_rank = grad_norm_sum[:, model_width + rank :]
-
-    acts_down = [after(a[0], *far) for a in acts]
+        sends = weight_share(
+            [(3, 0, (), BF16), (3, 1, (), BF16)], first_space, count=2 * CHUNKS
+        )
+        sends = weight_share(
+            [(1, 0, (), BF16), (2, 1, (), BF16)], first_space, sends, CHUNKS, 2 * CHUNKS
+        )
+        near_one, near_two = trade(sends[0], "dp", 1), trade(sends[1], "dp", 2)
+        held = weight_share([(1, 1, (), BF16), (2, 0, (), BF16)], sends[0])
+
+    acts_down = [(after(a[0][0], first_space, *sends), a[0][1]) for a in acts]
     ffn_own, ffn_given = down_pass(acts_down, chunks, slice_width, rank_part)
-    ffn_all = after(sum_pass(ffn_own, partner(ffn_given)), grad_norm_sum)
+    ffn_ready = sum_pass(ffn_own, partner(ffn_given))
+    grad_norm_sum = after(grad_norm_sum, ffn_ready)
+    if dp_count == 4:
+        grad_norm_sum = after(grad_norm_sum, *held)
     half_rows = row_count // 2
-    ffn_first, rank_down = lax.psum(
-        (ffn_all[:half_rows, :model_width], ffn_all[:, model_width:]), "mp"
-    )
-
-    grad_rank_gu = jnp.concatenate([swap_ranks(grad_gate_rank), swap_ranks(grad_up_rank)], axis=1)
-    grad_input_ffn = product(normed_two, grad_rank_gu, 0, 0).astype(BF16)
-    grad_norm_two = grad_norm_two.astype(F32) + product(grad_rank_gu, input_ffn, 1, 1)
-    grad_hidden, grad_gain_two = rms_backward(hidden_state, inverse_two, gain_two, grad_norm_two)
-    grad_hidden = grad_hidden + grad_out
-    grad_branch = grad_hidden.astype(BF16)
-
-    grad_rank_out = product(grad_branch, model_lifted[0], 1, 1).astype(BF16)
-    grad_flat = dot(grad_branch, out_weight) + dot(grad_rank_out, out_down)
-    grad_out_down = product(grad_rank_out, flat_heads, 0, 0).astype(BF16)
-    grad_w_out = product(grad_branch, flat_heads, 0, 0).astype(BF16)
-    grad_att = grad_flat.astype(BF16).reshape(row_count, heads_here, HEAD_SIZE)
-    grad_query, grad_keys, grad_values = attend_back(
-        query_rows, key_rows, value_rows, places, segment, factor, logsum, grad_att
-    )
-    grad_query = (
-        rotate_back(grad_query, head_cos, head_sin).reshape(row_count, heads_width).astype(BF16)
-    )
-    grad_joint_all = jnp.concatenate(
-        [rotate_back(grad_keys, cosine, sine_part), grad_values], axis=1
-    )
-    grad_joint_all = grad_joint_all.astype(BF16)
-    grad_kv = lax.psum_scatter(
-        grad_joint_all, "mp", scatter_dimension=1, tiled=True
-    )
-    grad_joint = jnp.concatenate([grad_query, grad_kv], axis=1)
-    grad_pick = product(grad_kv, key_value_lifted, 1, 1)
-    zero_rank = jnp.zeros_like(grad_pick)
-    grad_rank_part = [
-        product(grad_query, query_lifted, 1, 1),
-        jnp.where(is_key, grad_pick, zero_rank),
-        jnp.where(is_key, zero_rank, grad_pick),
-    ]
-    grad_norm_part = product(grad_joint, joint_weight, 1, 1)
-    grad_norm_part = jnp.concatenate([grad_norm_part, *grad_rank_part], axis=1).astype(BF16)
-    grad_norm_part = after(grad_norm_part, ffn_first)
+    ffn_first, ffn_last = simple_pass(
+        early_kernel,
+        "early_pass",
+        (ffn_ready,),
+        [((half_rows, model_width + 2 * rank), BF16), ((half_rows, model_width), BF16)],
+    )
+    ffn_first = after(ffn_first, grad_norm_sum)
+    grad_norm_sum = after(grad_norm_sum, partner(ffn_first))
+    ffn_first = lax.psum(ffn_first, "mp")
+    rank_down = jnp.concatenate(
+        [ffn_first[:, model_width : model_width + rank], ffn_first[:, model_width + rank :]],
+        axis=0,
+    )
+
+    grad_hidden, grad_branch, grad_rank_gu, grad_rank_out, grad_query, grad_joint, gain_two = (
+        simple_pass(
+            attend_back_kernel,
+            "attend_back_pass",
+            (grad_norm_sum, hidden_state, gains_all, input_ffn, grad_ffn, model_all)
+            + (out_weight, out_down, query_rows, key_rows, joint_key_value)
+            + (cosine, sine_part, row_segment, column_segment),
+            [
+                ((row_count, model_width), F32),
+                ((row_count, model_width), BF16),
+                ((row_count, 2 * rank), BF16),
+                ((row_count, rank), BF16),
+                ((row_count, heads_width), BF16),
+                ((mp_count, row_count, kv_width), BF16),
+                ((8, model_width), F32),
+            ],
+            place,
+            LONG,
+        )
+    )
+    grad_kv = lax.psum_scatter(after(grad_joint, ffn_first), "mp", scatter_dimension=0, tiled=False)
     if dp_count == 4:
-        grad_norm_part = after(grad_norm_part, *first_sent)
-    grad_norm_one = lax.psum(grad_norm_part, "mp")
-    grad_rank_qkv = [
-        grad_norm_one[:, model_width + k * rank : model_width + (k + 1) * rank] for k in range(3)
-    ]
-    grad_norm_one = grad_norm_one[:, :model_width]
-    ffn_last = lax.psum(after(ffn_all[half_rows:, :model_width], grad_norm_one), "mp")
-    ffn_sum = jnp.concatenate([ffn_first, ffn_last], axis=0)
-    output = hidden_state + ffn_sum.astype(F32) + dot(rank_down, model_lifted[1])
+        near_one, near_two = after(near_one, grad_query), after(near_two, grad_query)
+        last_one = sum_pass(held[0], (near_two, 0))
+        last_two = sum_pass(held[1], (near_one, 0))
+        last_sent = (trade(last_one, "dp", 1), trade(last_two, "dp", 2))
+    (grad_norm_part,) = simple_pass(
+        project_back_kernel,
+        "project_back_pass",
+        (grad_query, grad_kv, joint_weight, joint_lifted),
+        [((row_count, model_width + 3 * rank), BF16)],
+        place,
+    )
+    ffn_last = after(ffn_last, ffn_first)
+    grad_norm_one, ffn_last = lax.psum((grad_norm_part, ffn_last), "mp")
+    grad_rows, grad_rank_qkv, gain_one = simple_pass(
+        first_back_kernel,
+        "first_back_pass",
+        (grad_norm_one, tok_rows, gains_all, input_attn, grad_hidden),
+        [
+            ((row_count, model_width), BF16),
+            ((row_count, 3 * rank), BF16),
+            ((8, model_width), F32),
+        ],
+        place,
+        LONG,
+    )
+    grad_input = relative(grad_rows, 1, dp_id, dp_count)
+
+    quarter = part_width * kv_width // heads_width
+    small = rank_part * kv_width // heads_width
+    blocks = share_columns // heads_width
+    mp_rows = 2 * blocks * rank_part + 2 * rank // heads_width * share_rows
+    rest_rows = 2 * rank_part + small + mp_rows
+    base_rows = 2 * part_width + quarter
+    shares, shares_given, *rest = simple_pass(
+        functools.partial(shares_kernel, dp_count, share_rows, share_columns),
+        "shares_pass",
+        (after(normalized_rows, grad_norm_part), grad_query, grad_kv, rank_rows, grad_branch, flat_heads)
+        + (grad_rank_out, rank_out, normed_own, grad_rank_gu, rank_down, grad_ffn),
+        [
+            ((dp_count, base_rows, heads_width), BF16),
+            ((dp_count, base_rows, heads_width), BF16),
+            *[((rest_rows, heads_width), BF16)] * dp_count,
+        ],
+        place,
+    )
+    own = ()
+    if dp_count == 4:
+        own = weight_share([(0, 0, (), BF16), (0, 1, (), BF16)], grad_norm_part)
+    shares_given = after(shares_given, *own)
+    if dp_count == 4:
+        mine = [(own[0], 0), (near_one, CHUNKS), (last_sent[1], 0)]
+        theirs = sum_pass(own[1], (near_two, 1), after(last_sent[0], last_sent[1]))
+        grad_rank_qkv = after(grad_rank_qkv, theirs)
+        theirs = partner(theirs)
+    else:
+        by_index = [
+            weight_share([(p, 0, (), BF16), (p, 1, (), BF16)], None)
+            for p in range(dp_count)
+        ]
+        mine = [(scatter_dp([b[0] for b in by_index]), 0)]
+        theirs = partner(scatter_dp([b[1] for b in by_index]).astype(BF16))
+    grad_w_gateup, grad_w_down, grad_lora_gateup, grad_lora_hidden = finish_pass(
+        core, mine, theirs, part_width, rank_part, hidden
+    )
+
+    ffn_sum = jnp.concatenate([ffn_first[:, :model_width], ffn_last], axis=0)
+    output = hidden_state + ffn_sum.astype(F32) + dot(rank_down, model_all[1])
     result_rows = relative(output.astype(BF16), 1, dp_id, dp_count)
-    grad_rank_qkv = jnp.concatenate([swap_ranks(g) for g in grad_rank_qkv], axis=1)
-    grad_input_attn = product(normalized_rows, grad_rank_qkv, 0, 0).astype(BF16)
-    grad_norm_one = grad_norm_one.astype(F32) + product(grad_rank_qkv, input_attn, 1, 1)
-    grad_source, grad_gain_one = rms_backward(source, inverse_one, gain_one, grad_norm_one)
-    grad_input = relative((grad_source + grad_hidden).astype(BF16), 1, dp_id, dp_count)
+    shares_got = after(partner(shares_given), grad_rank_qkv)
+
+    def shared(p, dtype, *more):
+        return add_pass(dtype, (shares, p), (shares_got, p), *more)
+
+    if dp_count == 4:
+        near_share = trade(shared(3, BF16), "dp", 1)
+        near_rest = after(trade(after(rest[3], *own), "dp", 2), grad_rank_qkv)
+        share_one, rest_two = trade(shared(1, BF16), "dp", 1), trade(after(rest[2], near_rest), "dp", 2)
+        share_two = trade(shared(2, BF16, near_share), "dp", 2)
+        rest_one = trade(add_pass(BF16, rest[1], near_rest), "dp", 1)
+        share_own = shared(0, F32, after(share_one, grad_w_down), share_two)
+        rest_own = add_pass(F32, rest[0], after(rest_one, grad_rank_qkv), rest_two)
+    else:
+        share_own = scatter_dp([shared(p, BF16) for p in range(dp_count)])
+        rest_own = scatter_dp([rest[p] for p in range(dp_count)])
+
+    share_own, rest_own = after(share_own, grad_rank_qkv), after(rest_own, grad_rank_qkv)
+
+    def unfolded(block, width, heights):
+        rows = heights
+        columns = [block[at : at + rows, :width] for at in range(0, block.shape[0], rows)]
+        return jnp.concatenate(columns, axis=1)
+
+    def side_by_side(block, width):
+        return jnp.concatenate(
+            [block[:, at : at + width] for at in range(0, heads_width, width)], axis=0
+        )
+
+    grad_w_query = share_own[:part_width]
+    grad_w_keyval = side_by_side(share_own[part_width : part_width + quarter], kv_width)
+    grad_w_output = share_own[part_width + quarter :].T
+    at = rank_part
+    grad_lora_query = rest_own[:at][None]
+    grad_lora_keyval = side_by_side(rest_own[at : at + small], kv_width)[None]
+    at += small
+    grad_lora_out = rest_own[at : at + rank_part][None]
+    at += rank_part
+    gathered = lax.all_gather(rest_own[at:].astype(BF16), "mp", axis=0, tiled=False).astype(F32)
+    model_own, at = [], 0
+    for _ in range(2):
+        block = gathered[:, at : at + blocks * rank_part].reshape(-1, heads_width)
+        model_own.append(unfolded(block, heads_width, rank_part))
+        at += blocks * rank_part
+    grad_lora_model = jnp.stack(model_own)[None]
+    ffn_in_own = jnp.concatenate(
+        [unfolded(gathered[z, at:], heads_width, share_rows) for z in range(mp_count)], axis=0
+    )
 
     def by_dp(block):
         return block.reshape(dp_count, block.shape[0] // dp_count, block.shape[1])
 
-    def over_cores(block):
-        halves = block.reshape(dp_count, 2, part_width, block.shape[1])
-        mine = lax.dynamic_index_in_dim(halves, depth_id, 1, keepdims=False)
-        theirs = lax.dynamic_index_in_dim(halves, 1 - depth_id, 1, keepdims=False)
-        return add_rounded(mine, partner(theirs))
-
-    grad_w_joint = over_cores(product(normalized_rows, grad_joint, 0, 0).astype(BF16))
-    grad_lifted = by_dp(
-        jnp.concatenate(
-            [product(rank_query, grad_query, 0, 0), product(rank_pick, grad_kv, 0, 0)], axis=1
-        ).astype(BF16)
-    )
-    joint_own = scatter_dp(
-        [jnp.concatenate([grad_w_joint[p], grad_lifted[p]], axis=0) for p in range(dp_count)],
-        grad_norm_part,
-    )
-    grad_w_out = over_cores(grad_w_out)
-    grad_out_down = by_dp(grad_out_down)
-    out_own = scatter_dp(
-        [jnp.concatenate([grad_w_out[p], grad_out_down[p]], axis=0) for p in range(dp_count)],
-        grad_norm_part,
-    )
-    grad_model = [
-        by_dp(relative(product(rank_out, grad_branch, 0, 0).astype(BF16), 1, dp_id, dp_count)),
-        by_dp(relative(product(rank_down, grad_ffn, 0, 0).astype(BF16), 1, dp_id, dp_count)),
-    ]
-    model_own = scatter_dp(
-        [jnp.concatenate([g[p] for g in grad_model], axis=0) for p in range(dp_count)],
-        grad_norm_part,
-    )
-    grad_input_ffn = by_dp(grad_input_ffn)
-    ffn_in_own = scatter_dp([grad_input_ffn[p] for p in range(dp_count)], grad_norm_part)
-    gain_grads = jnp.stack([grad_gain_one, grad_gain_two])
-    gain_grads = gain_grads + partner(gain_grads)
-    gain_grads = gain_grads.reshape(2, dp_count, 2, part_width)
-    gain_grads = lax.dynamic_index_in_dim(gain_grads, depth_id, 2, keepdims=False).astype(BF16)
-    grad_input_attn = by_dp(grad_input_attn)
+    gain_grads = jnp.stack([gain_one[0], gain_two[0]]).astype(BF16)
+    gain_grads = gain_grads.reshape(2, dp_count, slice_width)
+    grad_input_attn = by_dp(product(normalized_rows, grad_rank_qkv, 0, 0).astype(BF16))
     attn_in_own = scatter_dp(
         [
             jnp.concatenate(
@@ -1208,51 +1497,31 @@
             for p in range(dp_count)
         ]
     )
-    grad_w_gains = attn_in_own[slice_width : slice_width + 2, :part_width]
+    gain_grads = attn_in_own[slice_width : slice_width + 2, :slice_width]
+    gain_first, gain_second = gain_grads[:, :part_width], gain_grads[:, part_width:]
+    grad_w_gains = jnp.where(first_core, gain_first, gain_second) + partner(
+        jnp.where(first_core, gain_second, gain_first)
+    )
     input_own = jnp.concatenate([attn_in_own[:slice_width], ffn_in_own], axis=1)
     grad_lora_in = jnp.stack([input_own[:, k * rank : (k + 1) * rank] for k in range(5)])[None]
-
-    if dp_count == 4:
-        mine, theirs = [], []
-        for group, (last_one, last_two) in zip(groups, last_sent):
-            own_blocks = weight_share(
-                lambda n, at=group.start, got=(last_one, last_two): [
-                    (0, 0, ((first_sent[0], at + n), (got[1], n)), F32),
-                    (0, 1, ((first_sent[1], at + n), (got[0], n)), BF16),
-                ],
-                group,
-                grad_norm_part,
-            )
-            mine.append(own_blocks[0])
-            theirs.append(partner(own_blocks[1]))
-    else:
-        blocks = [
-            weight_share([(p, 0, (), BF16), (p, 1, (), BF16)], range(CHUNKS), None)
-            for p in range(dp_count)
-        ]
-        mine = [scatter_dp([b[0] for b in blocks])]
-        theirs = [partner(scatter_dp([b[1] for b in blocks]).astype(BF16))]
-    grad_w_gateup, grad_w_down, grad_lora_gateup, grad_lora_hidden = finish_pass(
-        core, mine, theirs, part_width, rank_part, hidden
-    )
 
     mixed_rows = jnp.where(keep_own, result_rows, partner(result_rows))
     grad_tokens = jnp.where(keep_own, grad_input, partner(grad_input))
     return (
         mixed_rows,
         grad_tokens,
-        joint_own[:part_width, :heads_width],
-        joint_own[:part_width, heads_width:],
-        out_own[:part_width].T,
+        grad_w_query,
+        grad_w_keyval,
+        grad_w_output,
         grad_w_gateup,
         grad_w_down,
         grad_w_gains,
         grad_lora_in,
-        joint_own[part_width:, :heads_width][None],
-        joint_own[part_width:, heads_width:][None],
-        out_own[part_width:][None],
+        grad_lora_query,
+        grad_lora_keyval,
+        grad_lora_out,
         grad_lora_hidden,
-        model_own.reshape(1, 2, rank_part, model_width),
+        grad_lora_model,
         grad_lora_gateup,
     )
 

time: 1030 us -> 917 us (0.89)
  Pallas kernels: 272 us -> 351 us
  matrix products: 66.5 us -> 2.58 us
  local copies, waits for them, and re-layouts: 103 us -> 62.5 us
  other arithmetic: 66.6 us -> 32.2 us
  waiting for transfers between devices: 419 us -> 387 us
    ppermute x55 -> x40, waiting for transfers between devices: 237 us -> 135 us  [trade(): return lax.ppermute(block, axis, [(i, i ^ mask) for i in range(count)])]
    pallas_call x7 -> x23, Pallas kernels: 112 us -> 193 us  [the longest x2 77.2 us: gate_pass(): pl.pallas_call(functools.partial(gate_kernel, len(chunks[0]), width, rank...]
    psum x3, waiting for transfers between devices: 134 us -> 205 us  [the longest x1 85.4 us: local(): branch_sum = lax.psum(branch_part, 'mp')]
    dot_general x18 -> x1, matrix products: 42.9 us -> 1.86 us  [product(): lax.dot_general(left_op, right_op, (((left_dim,), (right_dim,)), ((), ())...]
    dot_general x19 -> x1, matrix products: 19 us -> 0.72 us  [dot(): return jnp.dot(left_op, right_op, preferred_element_type=F32)]
    reduce_scatter x1, waiting for transfers between devices: 5.99 us -> 23.8 us  [local(): lax.psum_scatter(after(grad_joint, ffn_first), 'mp', scatter_dimension=0,...]
    psum x1, waiting for transfers between devices: 14.5 us -> 0.01 us  [local(): grad_norm_sum = lax.psum(grad_norm_ready, 'mp')]
    unnamed x432 -> x179, local copies, waits for them, and re-layouts: 56.3 us -> 42.5 us
  transfers between devices with their start and end apart: 61 -> 47, of which waited for: 25 -> 18; matrix products, arithmetic and copies ran while one was open for 16% -> 6% of each run, Pallas kernels for 22% -> 33%
where the time goes in v2:
time: 917 us; the launch traced here: 909 us
  waiting for transfers between devices  387 us (42%)
  Pallas kernels  351 us (38%)
  local copies, waits for them, and re-layouts  62.5 us (7%)
  starting transfers between devices  34.1 us (4%)
  other arithmetic  32.2 us (4%)
  blocking collectives  22.8 us (2%)
  between operations  16.4 us (2%)
    ppermute x40, waiting for transfers between devices, trade(): return lax.ppermute(block, axis, [(i, i ^ mask) for i in range(count)])  135 us
    pallas_call x16, Pallas kernels, weight_pass(): pl.pallas_call(functools.partial(weight_kernel, part, rank_part, tuple((i...  91.8 us
    psum x1, waiting for transfers between devices, local(): branch_sum = lax.psum(branch_part, 'mp')  85.4 us
    psum x1, waiting for transfers between devices, local(): grad_norm_one, ffn_last = lax.psum((grad_norm_part, ffn_last), 'mp')  82.7 us
    pallas_call x2, Pallas kernels, gate_pass(): pl.pallas_call(functools.partial(gate_kernel, len(chunks[0]), width, rank...  77.2 us
    pallas_call x9, Pallas kernels, simple_pass(): pl.pallas_call(kernel, grid=(1,), in_specs=specs, out_specs=[whole_spec(s...  66.3 us
    unnamed x179, local copies, waits for them, and re-layouts  42.5 us
    psum x1, waiting for transfers between devices, local(): ffn_first = lax.psum(ffn_first, 'mp')  37 us
  transfers between devices with their start and end apart: 47, of which 18 were waited for; matrix products, arithmetic and copies ran while one was open for 6% of the time, Pallas kernels for 33%

profile of v2, /device:TPU:0, one launch (start us, length us, event | category | flops | bytes accessed | tf_op | source)
XLA Modules:
  0.0 908.5 jit_solution(13674477972057843048)
XLA Ops:
  32.4 15.6 %collective-permute-done.3.refs_4_ = bf16[688,768]{1,0:T(8,128)(2,1)S(1)} collective-permute-done((bf16[688,768]{1,0:T(8,128)(2,1)S(1)}, bf16[688,768]{1,0:T(8,128)(2,1)S(1)}, u32[]{:S(2)}, u32[]{:S(2)}) %collective-permute-start.3) | collective-permute-done | bytes 1056800 | tf_op jit(solution)/shard_map/ppermute | solution.py:93
  51.7 19.6 %collective-permute-done.4.refs_5_ = bf16[656,640]{1,0:T(8,128)(2,1)S(1)} collective-permute-done((bf16[656,640]{1,0:T(8,128)(2,1)S(1)}, bf16[656,640]{1,0:T(8,128)(2,1)S(1)}, u32[]{:S(2)}, u32[]{:S(2)}) %collective-permute-start.4) | collective-permute-done | bytes 839712 | tf_op jit(solution)/shard_map/ppermute | solution.py:93
  71.3 16.5 %collective-permute-done.7.refs_7_ = bf16[656,640]{1,0:T(8,128)(2,1)S(1)} collective-permute-done((bf16[656,640]{1,0:T(8,128)(2,1)S(1)}, bf16[656,640]{1,0:T(8,128)(2,1)S(1)}, u32[]{:S(2)}, u32[]{:S(2)}) %collective-permute-start.7) | collective-permute-done | bytes 839712 | tf_op jit(solution)/shard_map/ppermute | solution.py:93
  121.5 10.2 %project_pass.1 = (bf16[512,2048]{1,0:T(8,128)(2,1)}, bf16[512,768]{1,0:T(8,128)(2,1)S(1)}, bf16[512,512]{1,0:T(8,128)(2,1)S(1)}, bf16[512,128]{1,0:T(8,128)(2,1)S(1)}) custom-call(s32[6]{0:T(128)S(1)} %stack.65.place, bf16[512,2048]{1,0:T(8,128)(2,1)} %maximum_select_fusion.1.rows, bf16[16,2048]{1,0:T(8,128)(2,1)S(1)} %get-tuple-element.139.gains, ...), custom_call_target="tpu_custom_call" | custom-call | flops 1 | bytes 1 | tf_op jit(solution)/shard_map/project_pass/pallas_call | solution.py:499
  132.6 22.8 %all-gather = bf16[2048,128]{1,0:T(8,128)(2,1)S(1)} all-gather(bf16[512,128]{1,0:T(8,128)(2,1)S(1)} %get-tuple-element.144), channel_id=2, replica_groups=mesh['dp'=4,'depth'=2,'mp'=4] {'mp'}, dimensions={0}, use_global_device_ids=true | all-gather | bytes 655360 | tf_op jit(solution)/shard_map/all_gather | solution.py:1243
  163.0 23.0 %all-gather.6.cloned.1.call-done = bf16[16,512,256]{2,1,0:T(8,128)(2,1)} async-done(((bf16[4,512,256]{2,1,0:T(8,128)(2,1)}), bf16[16,512,256]{2,1,0:T(8,128)(2,1)}) %all-gather.6.cloned.1.call-update) | async-done | bytes 4194320 | tf_op jit(solution)/shard_map/all_gather | solution.py:1217
  197.7 85.4 %all-reduce.10.cloned.1.call-done.branch = bf16[512,2304]{1,0:T(8,128)(2,1)} async-done(((bf16[512,2304]{1,0:T(8,128)(2,1)}), bf16[512,2304]{1,0:T(8,128)(2,1)}) %all-reduce.10.cloned.1.call-update) | async-done | bytes 2359312 | tf_op jit(solution)/shard_map/psum | solution.py:1256
  301.7 7.5 turn_pass.2.refs_4_.refs_7_.refs_9_.refs_12_
  309.2 30.3 %collective-permute-done.14.refs_10_.refs_18_ = bf16[1920,512]{1,0:T(8,128)(2,1)} collective-permute-done((bf16[1920,512]{1,0:T(8,128)(2,1)S(1)}, bf16[1920,512]{1,0:T(8,128)(2,1)}, u32[]{:S(2)}, u32[]{:S(2)}) %collective-permute-start.14) | collective-permute-done | bytes 1966112 | tf_op jit(solution)/shard_map/ppermute | solution.py:93
  344.7 37.5 %gate_pass.2 = (bf16[1024,1024]{1,0:T(8,128)(2,1)}, bf16[1024,1024]{1,0:T(8,128)(2,1)}, bf16[1024,1024]{1,0:T(8,128)(2,1)}, bf16[512,2560]{1,0:T(8,128)(2,1)}, bf16[512,2560]{1,0:T(8,128)(2,1)}) custom-call(bf16[512,2560]{1,0:T(8,128)(2,1)} %get-tuple-element.167.refs_0_.own.refs_2_, bf16[512,2560]{1,0:T(8,128)(2,1)} %copy-done.67, ...), custom_call_target="tpu_custom_call" | custom-call | flops 1 | bytes 1 | tf_op jit(solution)/shard_map/gate_pass/pallas_call | solution.py:843
  386.2 39.7 %gate_pass.3 = (bf16[1024,1024]{1,0:T(8,128)(2,1)}, bf16[1024,1024]{1,0:T(8,128)(2,1)}, bf16[1024,1024]{1,0:T(8,128)(2,1)}, f32[512,2560]{1,0:T(8,128)}, bf16[512,2560]{1,0:T(8,128)(2,1)}) custom-call(bf16[512,2560]{1,0:T(8,128)(2,1)} %get-tuple-element.167.refs_0_.own.refs_2_, bf16[512,2560]{1,0:T(8,128)(2,1)} %copy-done.67, ...), custom_call_target="tpu_custom_call" | custom-call | flops 1 | bytes 1 | tf_op jit(solution)/shard_map/gate_pass/pallas_call | solution.py:843
  441.5 8.4 turn_pass.3.refs_3_.refs_5_.refs_6_.refs_8_.refs_10_.refs_11_
  496.0 23.3 %down_pass.1 = (f32[512,2304]{1,0:T(8,128)}, bf16[512,2304]{1,0:T(8,128)(2,1)}) custom-call(bf16[1024,1024]{1,0:T(8,128)(2,1)} %get-tuple-element.187.refs_2_.refs_0_.refs_1_, bf16[1024,1024]{1,0:T(8,128)(2,1)} %get-tuple-element.187.refs_2_.refs_0_.refs_1_, bf16[1024,1024]{1,0:T(8,128)(2,1)} %get-tuple-element.188.refs_2_.refs_3_, ...), custom_call_target="tpu_custom_call" | custom-call | flops 1 | bytes 1 | tf_op jit(solution)/shard_map/down_pass/pallas_call | solution.py:905
  558.7 14.1 %attend_back_pass.1 = (f32[512,2048]{1,0:T(8,128)}, bf16[512,2048]{1,0:T(8,128)(2,1)}, bf16[512,512]{1,0:T(8,128)(2,1)S(1)}, bf16[512,256]{1,0:T(8,128)(2,1)S(1)...) custom-call(s32[6]{0:T(128)S(1)} %copy-done.59, ...), custom_call_target="tpu_custom_call" | custom-call | flops 100000000376832 | bytes 1 | tf_op jit(solution)/shard_map/attend_back_pass/pallas_call | solution.py:499
  575.8 37.0 %all-reduce.14.cloned.1.call-done = bf16[256,2560]{1,0:T(8,128)(2,1)} async-done(((bf16[256,2560]{1,0:T(8,128)(2,1)}), bf16[256,2560]{1,0:T(8,128)(2,1)}) %all-reduce.14.cloned.1.call-update) | async-done | bytes 1310736 | tf_op jit(solution)/shard_map/psum | solution.py:1341
  612.8 23.8 %reduce-scatter.2.cloned.1.call-done = bf16[1,512,128]{2,1,0:T(8,128)(2,1)} async-done(((bf16[4,512,128]{2,1,0:T(8,128)(2,1)}), bf16[1,512,128]{2,1,0:T(8,128)(2,1)}) %reduce-scatter.2.cloned.1.call-update) | async-done | bytes 131088 | tf_op jit(solution)/shard_map/reduce_scatter | solution.py:1367
  670.1 10.7 %shares_pass.1 = (bf16[4,576,512]{2,1,0:T(8,128)(2,1)}, bf16[4,576,512]{2,1,0:T(8,128)(2,1)}, bf16[400,512]{1,0:T(8,128)(2,1)S(1)}, bf16[400,512]{1,0:T(8,128)(2...) custom-call(s32[6]{0:T(128)S(1)} %copy-done.59, bf16[512,2048]{1,0:T(8,128)(2,1)} %get-tuple-element.214.normed, ...), custom_call_target="tpu_custom_call" | custom-call | flops 1 | bytes 1 | tf_op jit(solution)/shard_map/shares_pass/pallas_call | solution.py:499
  683.1 9.0 collective-permute-done.24.refs_1_
  706.2 82.7 %all-reduce.16.cloned.1.call-done = (bf16[256,2048]{1,0:T(8,128)(2,1)}, bf16[512,2816]{1,0:T(8,128)(2,1)}) async-done(((bf16[256,2048]{1,0:T(8,128)(2,1)}, bf16[512,2816]{1,0:T(8,128)(2,1)}), (bf16[256,2048]{1,0:T(8,128)(2,1)}, bf16[512,2816]{1,0:T(8,128)(2,1)})) %all-reduce.16.cloned.1.call-update) | async-done | bytes 3932176 | tf_op jit(solution)/shard_map/psum | solution.py:1381
  788.9 8.3 first_back_pass.1
  804.6 7.3 sum_pass.9
  849.1 7.8 collective-permute-done.30.refs_2_
  860.5 13.8 %collective-permute-done.33 = bf16[528,768]{1,0:T(8,128)(2,1)} collective-permute-done((bf16[528,768]{1,0:T(8,128)(2,1)}, bf16[528,768]{1,0:T(8,128)(2,1)}, u32[]{:S(2)}, u32[]{:S(2)}) %collective-permute-start.33) | collective-permute-done | bytes 811040 | tf_op jit(solution)/shard_map/ppermute | solution.py:93
  884.4 12.5 %finish_pass.1 = (f32[2,256,4096]{2,1,0:T(8,128)}, f32[4096,256]{1,0:T(8,128)}, f32[1,2,64,4096]{3,2,1,0:T(8,128)}, f32[1,64,4096]{2,1,0:T(8,128)}) custom-call(s32[1]{0:T(128)} %bitcast.3.core, bf16[3840,512]{1,0:T(8,128)(2,1)S(1)} %copy-done.5, bf16[7680,512]{1,0:T(8,128)(2,1)} %collective-permute-done.26.refs_1_, ...), custom_call_target="tpu_custom_call" | custom-call | flops 1 | bytes 1 | tf_op jit(solution)/shard_map/finish_pass/pallas_call | solution.py:1123
  (378 shorter events, 325.6 us)
Async XLA Ops:
  7.2 178.8 %all-gather.6.cloned.1.call-start = ((), (), s32[]{:S(2)}) async-start(), calls=%async_computation.5 | async-start | bytes 5242880 | tf_op jit(solution)/shard_map/all_gather | solution.py:1217
  25.4 45.9 %collective-permute-start.1 = (bf16[688,768]{1,0:T(8,128)(2,1)S(1)}, bf16[688,768]{1,0:T(8,128)(2,1)S(1)}, u32[]{:S(2)}, u32[]{:S(2)}) collective-permute-start(bf16[688,768]{1,0:T(8,128)(2,1)S(1)} %get-tuple-element.135.refs_0_), channel_id=1, source_target_pairs={{0,8},{8,0},{16,24},{24,16},{1,9},{9,1},{17,25},{25,17},{2,10},{10... | collective-permute-start | bytes 3170312 | tf_op jit(solution)/shard_map/ppermute | solution.py:93
  48.0 42.1 %collective-permute-start.6 = (bf16[688,768]{1,0:T(8,128)(2,1)S(1)}, bf16[688,768]{1,0:T(8,128)(2,1)S(1)}, u32[]{:S(2)}, u32[]{:S(2)}) collective-permute-start(bf16[688,768]{1,0:T(8,128)(2,1)S(1)} %collective-permute-done.3.refs_4_), channel_id=1, source_target_pairs={{0,8},{8,0},{16,24},{24,16},{1,9},{9,1},{17,25},{25,17},{2,10},{10... | collective-permute-start | bytes 3170312 | tf_op jit(solution)/shard_map/ppermute | solution.py:93
  51.7 51.0 %collective-permute-start = (bf16[512,2048]{1,0:T(8,128)(2,1)}, bf16[512,2048]{1,0:T(8,128)(2,1)}, u32[]{:S(2)}, u32[]{:S(2)}) collective-permute-start(bf16[512,2048]{1,0:T(8,128)(2,1)} %param.17), channel_id=1, source_target_pairs={{0,4},{4,0},{1,5},{5,1},{2,6},{6,2},{3,7},{7,3},{8,12},{12,8},{9,1... | collective-permute-start | bytes 6291464 | tf_op jit(solution)/shard_map/ppermute | solution.py:93
  96.4 186.7 %all-reduce.10.cloned.1.call-start = ((), (), s32[]{:S(2)}) async-start(), calls=%async_computation.1 | async-start | bytes 4718592 | tf_op jit(solution)/shard_map/psum | solution.py:1256
  98.6 191.4 %collective-permute-start.13 = (bf16[7680,512]{1,0:T(8,128)(2,1)}, bf16[7680,512]{1,0:T(8,128)(2,1)}, u32[]{:S(2)}, u32[]{:S(2)}) collective-permute-start(bf16[7680,512]{1,0:T(8,128)(2,1)} %bitcast.106), channel_id=1, source_target_pairs={{0,16},{8,24},{16,0},{24,8},{1,17},{9,25},{17,1},{25,9},{2,18},{10... | collective-permute-start | bytes 23592968 | tf_op jit(solution)/shard_map/ppermute | solution.py:93
  100.1 195.1 %collective-permute-start.12 = (bf16[7680,512]{1,0:T(8,128)(2,1)}, bf16[7680,512]{1,0:T(8,128)(2,1)}, u32[]{:S(2)}, u32[]{:S(2)}) collective-permute-start(bf16[7680,512]{1,0:T(8,128)(2,1)} %bitcast.107), channel_id=1, source_target_pairs={{0,8},{8,0},{16,24},{24,16},{1,9},{9,1},{17,25},{25,17},{2,10},{10... | collective-permute-start | bytes 23592968 | tf_op jit(solution)/shard_map/ppermute | solution.py:93
  197.7 103.4 %collective-permute-start.10 = (bf16[512,2304]{1,0:T(8,128)(2,1)}, bf16[512,2304]{1,0:T(8,128)(2,1)}, u32[]{:S(2)}, u32[]{:S(2)}) collective-permute-start(bf16[512,2304]{1,0:T(8,128)(2,1)} %grad_pass.1.own.refs_2_), channel_id=1, source_target_pairs={{0,4},{4,0},{1,5},{5,1},{2,6},{6,2},{3,7},{7,3},{8,12},{12,8},{9,1... | collective-permute-start | bytes 7077896 | tf_op jit(solution)/shard_map/ppermute | solution.py:93
  293.8 45.7 %collective-permute-start.14 = (bf16[1920,512]{1,0:T(8,128)(2,1)S(1)}, bf16[1920,512]{1,0:T(8,128)(2,1)}, u32[]{:S(2)}, u32[]{:S(2)}) collective-permute-start(bf16[1920,512]{1,0:T(8,128)(2,1)S(1)} %get-tuple-element.322), channel_id=1, source_target_pairs={{0,8},{8,0},{16,24},{24,16},{1,9},{9,1},{17,25},{25,17},{2,10},{10... | collective-permute-start | bytes 5898248 | tf_op jit(solution)/shard_map/ppermute | solution.py:93
  299.0 45.8 %collective-permute-start.15 = (bf16[1920,512]{1,0:T(8,128)(2,1)S(1)}, bf16[1920,512]{1,0:T(8,128)(2,1)}, u32[]{:S(2)}, u32[]{:S(2)}) collective-permute-start(bf16[1920,512]{1,0:T(8,128)(2,1)S(1)} %get-tuple-element.320), channel_id=1, source_target_pairs={{0,16},{8,24},{16,0},{24,8},{1,17},{9,25},{17,1},{25,9},{2,18},{10... | collective-permute-start | bytes 5898248 | tf_op jit(solution)/shard_map/ppermute | solution.py:93
  300.5 81.8 %collective-permute-start.16 = (bf16[1920,512]{1,0:T(8,128)(2,1)}, bf16[1920,512]{1,0:T(8,128)(2,1)}, u32[]{:S(2)}, u32[]{:S(2)}) collective-permute-start(bf16[1920,512]{1,0:T(8,128)(2,1)} %get-tuple-element.321), channel_id=1, source_target_pairs={{0,8},{8,0},{16,24},{24,16},{1,9},{9,1},{17,25},{25,17},{2,10},{10... | collective-permute-start | bytes 5898248 | tf_op jit(solution)/shard_map/ppermute | solution.py:93
  301.2 85.0 %collective-permute-start.17 = (bf16[1920,512]{1,0:T(8,128)(2,1)}, bf16[1920,512]{1,0:T(8,128)(2,1)}, u32[]{:S(2)}, u32[]{:S(2)}) collective-permute-start(bf16[1920,512]{1,0:T(8,128)(2,1)} %get-tuple-element.319), channel_id=1, source_target_pairs={{0,16},{8,24},{16,0},{24,8},{1,17},{9,25},{17,1},{25,9},{2,18},{10... | collective-permute-start | bytes 5898248 | tf_op jit(solution)/shard_map/ppermute | solution.py:93
  438.7 115.8 %all-reduce.12.cloned.1.call-start = ((), (), s32[]{:S(2)}) async-start(), calls=%async_computation.2 | async-start | bytes 5242880 | tf_op jit(solution)/shard_map/psum | solution.py:1293
  439.4 173.3 %all-reduce.14.cloned.1.call-start = ((), (), s32[]{:S(2)}) async-start(), calls=%async_computation.3 | async-start | bytes 2621440 | tf_op jit(solution)/shard_map/psum | solution.py:1341
  519.7 172.4 %collective-permute-start.24 = (bf16[7680,512]{1,0:T(8,128)(2,1)}, bf16[7680,512]{1,0:T(8,128)(2,1)}, u32[]{:S(2)}, u32[]{:S(2)}) collective-permute-start(bf16[7680,512]{1,0:T(8,128)(2,1)} %get-tuple-element.186), channel_id=1, source_target_pairs={{0,16},{8,24},{16,0},{24,8},{1,17},{9,25},{17,1},{25,9},{2,18},{10... | collective-permute-start | bytes 23592968 | tf_op jit(solution)/shard_map/ppermute | solution.py:93
  521.2 177.3 %collective-permute-start.26 = (bf16[7680,512]{1,0:T(8,128)(2,1)}, bf16[7680,512]{1,0:T(8,128)(2,1)}, u32[]{:S(2)}, u32[]{:S(2)}) collective-permute-start(bf16[7680,512]{1,0:T(8,128)(2,1)} %get-tuple-element.185), channel_id=1, source_target_pairs={{0,8},{8,0},{16,24},{24,16},{1,9},{9,1},{17,25},{25,17},{2,10},{10... | collective-permute-start | bytes 23592968 | tf_op jit(solution)/shard_map/ppermute | solution.py:93
  554.5 82.1 %reduce-scatter.2.cloned.1.call-start = ((), (), s32[]{:S(2)}) async-start(), calls=%async_computation.4 | async-start | bytes 655360 | tf_op jit(solution)/shard_map/reduce_scatter | solution.py:1367
  612.8 176.1 %all-reduce.16.cloned.1.call-start = ((), (), s32[]{:S(2)}) async-start(), calls=%async_computation.7 | async-start | bytes 7864320 | tf_op jit(solution)/shard_map/psum | solution.py:1381
  643.5 235.6 %all-gather.8.cloned.1.call-start = ((), (), s32[]{:S(2)}) async-start(), calls=%async_computation.6 | async-start | bytes 1310720 | tf_op jit(solution)/shard_map/all_gather | solution.py:1475
  681.5 139.0 %collective-permute-start.37 = (bf16[400,512]{1,0:T(8,128)(2,1)}, bf16[400,512]{1,0:T(8,128)(2,1)}, u32[]{:S(2)}, u32[]{:S(2)}) collective-permute-start(bf16[400,512]{1,0:T(8,128)(2,1)} %get-tuple-element.247), channel_id=1, source_target_pairs={{0,16},{8,24},{16,0},{24,8},{1,17},{9,25},{17,1},{25,9},{2,18},{10... | collective-permute-start | bytes 1228808 | tf_op jit(solution)/shard_map/ppermute | solution.py:93
  683.1 141.6 %collective-permute-start.23 = (bf16[4,576,512]{2,1,0:T(8,128)(2,1)}, bf16[4,576,512]{2,1,0:T(8,128)(2,1)}, u32[]{:S(2)}, u32[]{:S(2)}) collective-permute-start(bf16[4,576,512]{2,1,0:T(8,128)(2,1)} %get-tuple-element.231), channel_id=1, source_target_pairs={{0,4},{4,0},{1,5},{5,1},{2,6},{6,2},{3,7},{7,3},{8,12},{12,8},{9,1... | collective-permute-start | bytes 7077896 | tf_op jit(solution)/shard_map/ppermute | solution.py:93
  697.9 106.6 %collective-permute-start.25 = (bf16[3840,512]{1,0:T(8,128)(2,1)}, bf16[3840,512]{1,0:T(8,128)(2,1)}, u32[]{:S(2)}, u32[]{:S(2)}) collective-permute-start(bf16[3840,512]{1,0:T(8,128)(2,1)} %sum_pass.7), channel_id=1, source_target_pairs={{0,8},{8,0},{16,24},{24,16},{1,9},{9,1},{17,25},{25,17},{2,10},{10... | collective-permute-start | bytes 11796488 | tf_op jit(solution)/shard_map/ppermute | solution.py:93
  704.7 99.9 %collective-permute-start.27 = (bf16[3840,512]{1,0:T(8,128)(2,1)}, bf16[3840,512]{1,0:T(8,128)(2,1)}, u32[]{:S(2)}, u32[]{:S(2)}) collective-permute-start(bf16[3840,512]{1,0:T(8,128)(2,1)} %sum_pass.8), channel_id=1, source_target_pairs={{0,16},{8,24},{16,0},{24,8},{1,17},{9,25},{17,1},{25,9},{2,18},{10... | collective-permute-start | bytes 11796488 | tf_op jit(solution)/shard_map/ppermute | solution.py:93
  846.2 50.6 %collective-permute-start.28 = (bf16[576,512]{1,0:T(8,128)(2,1)}, bf16[576,512]{1,0:T(8,128)(2,1)}, u32[]{:S(2)}, u32[]{:S(2)}) collective-permute-start(bf16[576,512]{1,0:T(8,128)(2,1)} %add_pass.6), channel_id=1, source_target_pairs={{0,8},{8,0},{16,24},{24,16},{1,9},{9,1},{17,25},{25,17},{2,10},{10... | collective-permute-start | bytes 1769480 | tf_op jit(solution)/shard_map/ppermute | solution.py:93
  (111 other events, 1867.6 us)
Sparse Core Ops, SparseCore 0:
  96.5 89.4 all-gather.5
  188.9 94.1 all-reduce.9
  441.9 102.3 all-reduce.11
  554.6 58.0 all-reduce.13
  615.4 21.1 reduce-scatter.1
  643.6 145.2 all-reduce.15
  847.9 25.9 all-gather.7

commit v3 on v2

--- a/solution.py
+++ b/solution.py
@@ -114,14 +114,14 @@
     return pieces
 
 
-def gather_pair(one, two, early):
+def gather_pair(one, two, *early):
     count = lax.axis_size("dp")
     if count == 4:
         first_one, first_two = trade(one, "dp", 1), trade(one, "dp", 2)
         second_one, second_two = trade(two, "dp", 1), trade(two, "dp", 2)
-        far = trade(after(first_two, early), "dp", 1), trade(second_one, "dp", 2)
+        far = trade(after(first_two, *early), "dp", 1), trade(second_one, "dp", 2)
         pieces = [(one, two), (first_one, second_one), (first_two, second_two), far]
-        return pieces, far
+        return pieces, (first_two, second_one)
     ones, twos = gather_dp(one), gather_dp(two)
     return list(zip(ones, twos)), (ones[-1], twos[-1])
 
@@ -152,10 +152,8 @@
     return chunks
 
 
-def scatter_dp(parts, *hold):
+def scatter_dp(parts, *last):
     count = lax.axis_size("dp")
-    if hold:
-        parts = [after(part, *hold) for part in parts]
     if count == 4:
         half = parts[3].shape[0] // 2
         near_one = trade(parts[3][:half], "dp", 1)
@@ -163,7 +161,7 @@
         for_two = jnp.concatenate([add_rounded(parts[2][:half], near_one), parts[2][half:]], axis=0)
         for_one = jnp.concatenate([parts[1][:half], add_rounded(parts[1][half:], near_two)], axis=0)
         got_one = trade(for_one, "dp", 1)
-        got_two = trade(for_two, "dp", 2)
+        got_two = after(trade(for_two, "dp", 2), *last)
         return parts[0].astype(F32) + got_one.astype(F32) + got_two.astype(F32)
     mask = count // 2
     while mask:
@@ -1206,7 +1204,7 @@
         rank,
     )
     bundle = bundle_pass(core, ffn_arrays, taken, chunk)
-    pieces, hold = gather_pair(*bundles, bundle)
+    pieces, hold = gather_pair(*bundles, bundle, tok_rows, grad_ffn)
     shared_own, input_attn, late, joint_lifted, out_down = unpack_pass(
         pieces, part_width, rank_part, rank, share_rows, share_columns, heads_width
     )
@@ -1392,6 +1390,7 @@
         LONG,
     )
     grad_input = relative(grad_rows, 1, dp_id, dp_count)
+    grad_input_attn = product(normalized_rows, grad_rank_qkv, 0, 0).astype(BF16)
 
     quarter = part_width * kv_width // heads_width
     small = rank_part * kv_width // heads_width
@@ -1415,12 +1414,21 @@
     if dp_count == 4:
         own = weight_share([(0, 0, (), BF16), (0, 1, (), BF16)], grad_norm_part)
     shares_given = after(shares_given, *own)
+    shares_got = after(partner(shares_given), grad_input_attn)
+
+    def shared(p, dtype, *more):
+        return add_pass(dtype, (shares, p), (shares_got, p), *more)
+
+    far_share = shared(dp_count - 1, BF16)
     if dp_count == 4:
         mine = [(own[0], 0), (near_one, CHUNKS), (last_sent[1], 0)]
-        theirs = sum_pass(own[1], (near_two, 1), after(last_sent[0], last_sent[1]))
-        grad_rank_qkv = after(grad_rank_qkv, theirs)
+        theirs = sum_pass(
+            own[1], (near_two, 1), after(last_sent[0], last_sent[1], far_share)
+        )
+        summed = after(grad_rank_qkv, theirs)
         theirs = partner(theirs)
     else:
+        summed = grad_rank_qkv
         by_index = [
             weight_share([(p, 0, (), BF16), (p, 1, (), BF16)], None)
             for p in range(dp_count)
@@ -1434,15 +1442,13 @@
     ffn_sum = jnp.concatenate([ffn_first[:, :model_width], ffn_last], axis=0)
     output = hidden_state + ffn_sum.astype(F32) + dot(rank_down, model_all[1])
     result_rows = relative(output.astype(BF16), 1, dp_id, dp_count)
-    shares_got = after(partner(shares_given), grad_rank_qkv)
-
-    def shared(p, dtype, *more):
-        return add_pass(dtype, (shares, p), (shares_got, p), *more)
+    result_rows = after(result_rows, grad_w_down)
+    grad_input = after(grad_input, grad_w_down)
 
     if dp_count == 4:
-        near_share = trade(shared(3, BF16), "dp", 1)
-        near_rest = after(trade(after(rest[3], *own), "dp", 2), grad_rank_qkv)
-        share_one, rest_two = trade(shared(1, BF16), "dp", 1), trade(after(rest[2], near_rest), "dp", 2)
+        near_share = trade(far_share, "dp", 1)
+        near_rest = after(trade(after(rest[3], *own), "dp", 2), summed)
+        share_one, rest_two = trade(after(shared(1, BF16), summed), "dp", 1), trade(after(rest[2], near_rest), "dp", 2)
         share_two = trade(shared(2, BF16, near_share), "dp", 2)
         rest_one = trade(add_pass(BF16, rest[1], near_rest), "dp", 1)
         share_own = shared(0, F32, after(share_one, grad_w_down), share_two)
@@ -1488,14 +1494,15 @@
 
     gain_grads = jnp.stack([gain_one[0], gain_two[0]]).astype(BF16)
     gain_grads = gain_grads.reshape(2, dp_count, slice_width)
-    grad_input_attn = by_dp(product(normalized_rows, grad_rank_qkv, 0, 0).astype(BF16))
+    grad_input_attn = by_dp(grad_input_attn)
     attn_in_own = scatter_dp(
         [
             jnp.concatenate(
                 [grad_input_attn[p], pad_rows(gain_grads[:, p], 16, 3 * rank)], axis=0
             )
             for p in range(dp_count)
-        ]
+        ],
+        grad_w_down,
     )
     gain_grads = attn_in_own[slice_width : slice_width + 2, :slice_width]
     gain_first, gain_second = gain_grads[:, :part_width], gain_grads[:, part_width:]

time: 917 us -> 911 us (level)
  waiting for transfers between devices: 387 us -> 375 us
    ppermute x40, waiting for transfers between devices: 135 us -> 106 us  [trade(): return lax.ppermute(block, axis, [(i, i ^ mask) for i in range(count)])]
    all_gather x1, waiting for transfers between devices: 23 us -> 34.2 us  [local(): lax.all_gather(late, 'mp', axis=0, tiled=False)]
    unnamed x179 -> x173, local copies, waits for them, and re-layouts: 42.5 us -> 38.9 us
  transfers between devices with their start and end apart: 47 -> 47, of which waited for: 18 -> 18; matrix products, arithmetic and copies ran while one was open for 6% -> 7% of each run, Pallas kernels for 33% -> 34%
where the time goes in v3:
time: 911 us; the launch traced here: 903 us
  waiting for transfers between devices  375 us (41%)
  Pallas kernels  355 us (39%)
  local copies, waits for them, and re-layouts  59.7 us (7%)
  other arithmetic  39.4 us (4%)
  starting transfers between devices  29.5 us (3%)
  blocking collectives  23 us (3%)
  between operations  16.4 us (2%)
    ppermute x40, waiting for transfers between devices, trade(): return lax.ppermute(block, axis, [(i, i ^ mask) for i in range(count)])  106 us
    pallas_call x16, Pallas kernels, weight_pass(): pl.pallas_call(functools.partial(weight_kernel, part, rank_part, tuple((i...  92.1 us
    psum x1, waiting for transfers between devices, local(): branch_sum = lax.psum(branch_part, 'mp')  85.4 us
    psum x1, waiting for transfers between devices, local(): grad_norm_one, ffn_last = lax.psum((grad_norm_part, ffn_last), 'mp')  82.8 us
    pallas_call x2, Pallas kernels, gate_pass(): pl.pallas_call(functools.partial(gate_kernel, len(chunks[0]), width, rank...  77.2 us
    pallas_call x9, Pallas kernels, simple_pass(): pl.pallas_call(kernel, grid=(1,), in_specs=specs, out_specs=[whole_spec(s...  66.5 us
    unnamed x173, local copies, waits for them, and re-layouts  38.9 us
    psum x1, waiting for transfers between devices, local(): ffn_first = lax.psum(ffn_first, 'mp')  37 us
  transfers between devices with their start and end apart: 47, of which 18 were waited for; matrix products, arithmetic and copies ran while one was open for 7% of the time, Pallas kernels for 34%

profile of v3, /device:TPU:0, one launch (start us, length us, event | category | flops | bytes accessed | tf_op | source)
XLA Modules:
  0.0 902.7 jit_solution(13035166424725666506)
XLA Ops:
  41.7 6.5 bundle_pass.1
  50.2 15.1 %collective-permute-done.2.refs_3_ = bf16[656,640]{1,0:T(8,128)(2,1)} collective-permute-done((bf16[656,640]{1,0:T(8,128)(2,1)}, bf16[656,640]{1,0:T(8,128)(2,1)}, u32[]{:S(2)}, u32[]{:S(2)}) %collective-permute-start.2) | collective-permute-done | bytes 839712 | tf_op jit(solution)/shard_map/ppermute | solution.py:93
  71.4 17.3 %collective-permute-done.8.refs_7_ = bf16[656,640]{1,0:T(8,128)(2,1)S(1)} collective-permute-done((bf16[656,640]{1,0:T(8,128)(2,1)}, bf16[656,640]{1,0:T(8,128)(2,1)S(1)}, u32[]{:S(2)}, u32[]{:S(2)}) %collective-permute-start.8) | collective-permute-done | bytes 839712 | tf_op jit(solution)/shard_map/ppermute | solution.py:93
  108.3 10.2 %project_pass.1 = (bf16[512,2048]{1,0:T(8,128)(2,1)}, bf16[512,768]{1,0:T(8,128)(2,1)S(1)}, bf16[512,512]{1,0:T(8,128)(2,1)S(1)}, bf16[512,128]{1,0:T(8,128)(2,1)S(1)}) custom-call(s32[6]{0:T(128)S(1)} %stack.65.place, bf16[512,2048]{1,0:T(8,128)(2,1)} %maximum_select_fusion.1.rows, bf16[16,2048]{1,0:T(8,128)(2,1)S(1)} %get-tuple-element.143.gains, ...), custom_call_target="tpu_custom_call" | custom-call | flops 1 | bytes 1 | tf_op jit(solution)/shard_map/project_pass/pallas_call | solution.py:497
  119.3 23.0 %all-gather = bf16[2048,128]{1,0:T(8,128)(2,1)S(1)} all-gather(bf16[512,128]{1,0:T(8,128)(2,1)S(1)} %get-tuple-element.148), channel_id=2, replica_groups=mesh['dp'=4,'depth'=2,'mp'=4] {'mp'}, dimensions={0}, use_global_device_ids=true | all-gather | bytes 655360 | tf_op jit(solution)/shard_map/all_gather | solution.py:1241
  150.0 34.2 %all-gather.6.cloned.1.call-done = bf16[16,512,256]{2,1,0:T(8,128)(2,1)} async-done(((bf16[4,512,256]{2,1,0:T(8,128)(2,1)}), bf16[16,512,256]{2,1,0:T(8,128)(2,1)}) %all-gather.6.cloned.1.call-update) | async-done | bytes 4194320 | tf_op jit(solution)/shard_map/all_gather | solution.py:1215
  195.9 85.4 %all-reduce.10.cloned.1.call-done.branch = bf16[512,2304]{1,0:T(8,128)(2,1)} async-done(((bf16[512,2304]{1,0:T(8,128)(2,1)}), bf16[512,2304]{1,0:T(8,128)(2,1)}) %all-reduce.10.cloned.1.call-update) | async-done | bytes 2359312 | tf_op jit(solution)/shard_map/psum | solution.py:1254
  281.3 6.9 second_pass.1
  299.8 7.5 turn_pass.2.refs_4_.refs_7_.refs_9_.refs_12_
  307.3 30.3 %collective-permute-done.14.refs_10_.refs_18_ = bf16[1920,512]{1,0:T(8,128)(2,1)} collective-permute-done((bf16[1920,512]{1,0:T(8,128)(2,1)S(1)}, bf16[1920,512]{1,0:T(8,128)(2,1)}, u32[]{:S(2)}, u32[]{:S(2)}) %collective-permute-start.14) | collective-permute-done | bytes 1966112 | tf_op jit(solution)/shard_map/ppermute | solution.py:93
  344.4 37.5 %gate_pass.2 = (bf16[1024,1024]{1,0:T(8,128)(2,1)}, bf16[1024,1024]{1,0:T(8,128)(2,1)}, bf16[1024,1024]{1,0:T(8,128)(2,1)}, bf16[512,2560]{1,0:T(8,128)(2,1)}, bf16[512,2560]{1,0:T(8,128)(2,1)}) custom-call(bf16[512,2560]{1,0:T(8,128)(2,1)} %get-tuple-element.171.refs_0_.own.refs_2_, bf16[512,2560]{1,0:T(8,128)(2,1)} %copy-done.62, ...), custom_call_target="tpu_custom_call" | custom-call | flops 1 | bytes 1 | tf_op jit(solution)/shard_map/gate_pass/pallas_call | solution.py:841
  384.3 39.7 %gate_pass.3 = (bf16[1024,1024]{1,0:T(8,128)(2,1)}, bf16[1024,1024]{1,0:T(8,128)(2,1)}, bf16[1024,1024]{1,0:T(8,128)(2,1)}, f32[512,2560]{1,0:T(8,128)}, bf16[512,2560]{1,0:T(8,128)(2,1)}) custom-call(bf16[512,2560]{1,0:T(8,128)(2,1)} %get-tuple-element.171.refs_0_.own.refs_2_, bf16[512,2560]{1,0:T(8,128)(2,1)} %copy-done.62, ...), custom_call_target="tpu_custom_call" | custom-call | flops 1 | bytes 1 | tf_op jit(solution)/shard_map/gate_pass/pallas_call | solution.py:841
  439.7 8.4 turn_pass.3.refs_3_.refs_5_.refs_6_.refs_8_.refs_10_.refs_11_
  494.3 23.3 %down_pass.1 = (f32[512,2304]{1,0:T(8,128)}, bf16[512,2304]{1,0:T(8,128)(2,1)}) custom-call(bf16[1024,1024]{1,0:T(8,128)(2,1)} %get-tuple-element.191.refs_2_.refs_0_.refs_1_, bf16[1024,1024]{1,0:T(8,128)(2,1)} %get-tuple-element.191.refs_2_.refs_0_.refs_1_, bf16[1024,1024]{1,0:T(8,128)(2,1)} %get-tuple-element.192.refs_2_.refs_3_, ...), custom_call_target="tpu_custom_call" | custom-call | flops 1 | bytes 1 | tf_op jit(solution)/shard_map/down_pass/pallas_call | solution.py:903
  557.0 14.1 %attend_back_pass.1 = (f32[512,2048]{1,0:T(8,128)}, bf16[512,2048]{1,0:T(8,128)(2,1)}, bf16[512,512]{1,0:T(8,128)(2,1)S(1)}, bf16[512,256]{1,0:T(8,128)(2,1)S(1)...) custom-call(s32[6]{0:T(128)S(1)} %copy-done.56, ...), custom_call_target="tpu_custom_call" | custom-call | flops 100000000376832 | bytes 1 | tf_op jit(solution)/shard_map/attend_back_pass/pallas_call | solution.py:497
  574.1 37.0 %all-reduce.14.cloned.1.call-done = bf16[256,2560]{1,0:T(8,128)(2,1)} async-done(((bf16[256,2560]{1,0:T(8,128)(2,1)}), bf16[256,2560]{1,0:T(8,128)(2,1)}) %all-reduce.14.cloned.1.call-update) | async-done | bytes 1310736 | tf_op jit(solution)/shard_map/psum | solution.py:1339
  611.1 23.8 %reduce-scatter.2.cloned.1.call-done = bf16[1,512,128]{2,1,0:T(8,128)(2,1)} async-done(((bf16[4,512,128]{2,1,0:T(8,128)(2,1)}), bf16[1,512,128]{2,1,0:T(8,128)(2,1)}) %reduce-scatter.2.cloned.1.call-update) | async-done | bytes 131088 | tf_op jit(solution)/shard_map/reduce_scatter | solution.py:1365
  668.4 10.7 %shares_pass.1 = (bf16[4,576,512]{2,1,0:T(8,128)(2,1)}, bf16[4,576,512]{2,1,0:T(8,128)(2,1)}, bf16[400,512]{1,0:T(8,128)(2,1)S(1)}, bf16[400,512]{1,0:T(8,128)(2...) custom-call(s32[6]{0:T(128)S(1)} %copy-done.56, bf16[512,2048]{1,0:T(8,128)(2,1)} %get-tuple-element.228.normed, ...), custom_call_target="tpu_custom_call" | custom-call | flops 1 | bytes 1 | tf_op jit(solution)/shard_map/shares_pass/pallas_call | solution.py:497
  681.4 9.0 collective-permute-done.23.refs_1_
  704.5 82.8 %all-reduce.16.cloned.1.call-done = (bf16[256,2048]{1,0:T(8,128)(2,1)}, bf16[512,2816]{1,0:T(8,128)(2,1)}) async-done(((bf16[256,2048]{1,0:T(8,128)(2,1)}, bf16[512,2816]{1,0:T(8,128)(2,1)}), (bf16[256,2048]{1,0:T(8,128)(2,1)}, bf16[512,2816]{1,0:T(8,128)(2,1)})) %all-reduce.16.cloned.1.call-update) | async-done | bytes 3932176 | tf_op jit(solution)/shard_map/psum | solution.py:1379
  787.3 8.4 first_back_pass.1
  811.5 7.9 sum_pass.9
  826.6 8.7 collective-permute-done.38.refs_1_
  867.7 12.5 %finish_pass.1 = (f32[2,256,4096]{2,1,0:T(8,128)}, f32[4096,256]{1,0:T(8,128)}, f32[1,2,64,4096]{3,2,1,0:T(8,128)}, f32[1,64,4096]{2,1,0:T(8,128)}) custom-call(s32[1]{0:T(128)} %bitcast.3.core, bf16[3840,512]{1,0:T(8,128)(2,1)S(1)} %copy-done.5, bf16[7680,512]{1,0:T(8,128)(2,1)} %collective-permute-done.21.refs_1_, ...), custom_call_target="tpu_custom_call" | custom-call | flops 1 | bytes 1 | tf_op jit(solution)/shard_map/finish_pass/pallas_call | solution.py:1121
  (372 shorter events, 326.3 us)
Async XLA Ops:
  7.2 176.9 %all-gather.6.cloned.1.call-start = ((), (), s32[]{:S(2)}) async-start(), calls=%async_computation.5 | async-start | bytes 5242880 | tf_op jit(solution)/shard_map/all_gather | solution.py:1215
  20.7 50.7 %collective-permute-start.1 = (bf16[688,768]{1,0:T(8,128)(2,1)}, bf16[688,768]{1,0:T(8,128)(2,1)}, u32[]{:S(2)}, u32[]{:S(2)}) collective-permute-start(bf16[688,768]{1,0:T(8,128)(2,1)} %get-tuple-element.139.refs_0_), channel_id=1, source_target_pairs={{0,8},{8,0},{16,24},{24,16},{1,9},{9,1},{17,25},{25,17},{2,10},{10... | collective-permute-start | bytes 3170312 | tf_op jit(solution)/shard_map/ppermute | solution.py:93
  95.5 185.8 %all-reduce.10.cloned.1.call-start = ((), (), s32[]{:S(2)}) async-start(), calls=%async_computation.1 | async-start | bytes 4718592 | tf_op jit(solution)/shard_map/psum | solution.py:1254
  95.6 192.7 %collective-permute-start.13 = (bf16[7680,512]{1,0:T(8,128)(2,1)}, bf16[7680,512]{1,0:T(8,128)(2,1)}, u32[]{:S(2)}, u32[]{:S(2)}) collective-permute-start(bf16[7680,512]{1,0:T(8,128)(2,1)} %bitcast.106), channel_id=1, source_target_pairs={{0,16},{8,24},{16,0},{24,8},{1,17},{9,25},{17,1},{25,9},{2,18},{10... | collective-permute-start | bytes 23592968 | tf_op jit(solution)/shard_map/ppermute | solution.py:93
  96.2 197.2 %collective-permute-start.12 = (bf16[7680,512]{1,0:T(8,128)(2,1)}, bf16[7680,512]{1,0:T(8,128)(2,1)}, u32[]{:S(2)}, u32[]{:S(2)}) collective-permute-start(bf16[7680,512]{1,0:T(8,128)(2,1)} %bitcast.107), channel_id=1, source_target_pairs={{0,8},{8,0},{16,24},{24,16},{1,9},{9,1},{17,25},{25,17},{2,10},{10... | collective-permute-start | bytes 23592968 | tf_op jit(solution)/shard_map/ppermute | solution.py:93
  195.9 103.4 %collective-permute-start.10 = (bf16[512,2304]{1,0:T(8,128)(2,1)}, bf16[512,2304]{1,0:T(8,128)(2,1)}, u32[]{:S(2)}, u32[]{:S(2)}) collective-permute-start(bf16[512,2304]{1,0:T(8,128)(2,1)} %grad_pass.1.own.refs_2_), channel_id=1, source_target_pairs={{0,4},{4,0},{1,5},{5,1},{2,6},{6,2},{3,7},{7,3},{8,12},{12,8},{9,1... | collective-permute-start | bytes 7077896 | tf_op jit(solution)/shard_map/ppermute | solution.py:93
  288.2 54.6 %collective-permute-start.11 = (bf16[512,2560]{1,0:T(8,128)(2,1)}, bf16[512,2560]{1,0:T(8,128)(2,1)S(1)}, u32[]{:S(2)}, u32[]{:S(2)}) collective-permute-start(bf16[512,2560]{1,0:T(8,128)(2,1)} %get-tuple-element.171.refs_0_.own.refs_2_), channel_id=1, source_target_pairs={{0,4},{4,0},{1,5},{5,1},{2,6},{6,2},{3,7},{7,3},{8,12},{12,8},{9,1... | collective-permute-start | bytes 7864328 | tf_op jit(solution)/shard_map/ppermute | solution.py:93
  297.1 45.8 %collective-permute-start.15 = (bf16[1920,512]{1,0:T(8,128)(2,1)S(1)}, bf16[1920,512]{1,0:T(8,128)(2,1)}, u32[]{:S(2)}, u32[]{:S(2)}) collective-permute-start(bf16[1920,512]{1,0:T(8,128)(2,1)S(1)} %get-tuple-element.328), channel_id=1, source_target_pairs={{0,16},{8,24},{16,0},{24,8},{1,17},{9,25},{17,1},{25,9},{2,18},{10... | collective-permute-start | bytes 5898248 | tf_op jit(solution)/shard_map/ppermute | solution.py:93
  298.6 83.3 %collective-permute-start.16 = (bf16[1920,512]{1,0:T(8,128)(2,1)}, bf16[1920,512]{1,0:T(8,128)(2,1)}, u32[]{:S(2)}, u32[]{:S(2)}) collective-permute-start(bf16[1920,512]{1,0:T(8,128)(2,1)} %get-tuple-element.329), channel_id=1, source_target_pairs={{0,8},{8,0},{16,24},{24,16},{1,9},{9,1},{17,25},{25,17},{2,10},{10... | collective-permute-start | bytes 5898248 | tf_op jit(solution)/shard_map/ppermute | solution.py:93
  299.3 85.0 %collective-permute-start.17 = (bf16[1920,512]{1,0:T(8,128)(2,1)}, bf16[1920,512]{1,0:T(8,128)(2,1)}, u32[]{:S(2)}, u32[]{:S(2)}) collective-permute-start(bf16[1920,512]{1,0:T(8,128)(2,1)} %get-tuple-element.327), channel_id=1, source_target_pairs={{0,16},{8,24},{16,0},{24,8},{1,17},{9,25},{17,1},{25,9},{2,18},{10... | collective-permute-start | bytes 5898248 | tf_op jit(solution)/shard_map/ppermute | solution.py:93
  436.8 116.0 %all-reduce.12.cloned.1.call-start = ((), (), s32[]{:S(2)}) async-start(), calls=%async_computation.2 | async-start | bytes 5242880 | tf_op jit(solution)/shard_map/psum | solution.py:1291
  437.5 173.5 %all-reduce.14.cloned.1.call-start = ((), (), s32[]{:S(2)}) async-start(), calls=%async_computation.3 | async-start | bytes 2621440 | tf_op jit(solution)/shard_map/psum | solution.py:1339
  518.0 172.4 %collective-permute-start.23 = (bf16[7680,512]{1,0:T(8,128)(2,1)}, bf16[7680,512]{1,0:T(8,128)(2,1)}, u32[]{:S(2)}, u32[]{:S(2)}) collective-permute-start(bf16[7680,512]{1,0:T(8,128)(2,1)} %get-tuple-element.190), channel_id=1, source_target_pairs={{0,16},{8,24},{16,0},{24,8},{1,17},{9,25},{17,1},{25,9},{2,18},{10... | collective-permute-start | bytes 23592968 | tf_op jit(solution)/shard_map/ppermute | solution.py:93
  519.5 177.3 %collective-permute-start.21 = (bf16[7680,512]{1,0:T(8,128)(2,1)}, bf16[7680,512]{1,0:T(8,128)(2,1)}, u32[]{:S(2)}, u32[]{:S(2)}) collective-permute-start(bf16[7680,512]{1,0:T(8,128)(2,1)} %get-tuple-element.189), channel_id=1, source_target_pairs={{0,8},{8,0},{16,24},{24,16},{1,9},{9,1},{17,25},{25,17},{2,10},{10... | collective-permute-start | bytes 23592968 | tf_op jit(solution)/shard_map/ppermute | solution.py:93
  552.8 82.1 %reduce-scatter.2.cloned.1.call-start = ((), (), s32[]{:S(2)}) async-start(), calls=%async_computation.4 | async-start | bytes 655360 | tf_op jit(solution)/shard_map/reduce_scatter | solution.py:1365
  611.1 176.2 %all-reduce.16.cloned.1.call-start = ((), (), s32[]{:S(2)}) async-start(), calls=%async_computation.7 | async-start | bytes 7864320 | tf_op jit(solution)/shard_map/psum | solution.py:1379
  641.8 221.0 %all-gather.8.cloned.1.call-start = ((), (), s32[]{:S(2)}) async-start(), calls=%async_computation.6 | async-start | bytes 1310720 | tf_op jit(solution)/shard_map/all_gather | solution.py:1481
  679.9 141.2 %collective-permute-start.37 = (bf16[400,512]{1,0:T(8,128)(2,1)}, bf16[400,512]{1,0:T(8,128)(2,1)}, u32[]{:S(2)}, u32[]{:S(2)}) collective-permute-start(bf16[400,512]{1,0:T(8,128)(2,1)} %get-tuple-element.255), channel_id=1, source_target_pairs={{0,16},{8,24},{16,0},{24,8},{1,17},{9,25},{17,1},{25,9},{2,18},{10... | collective-permute-start | bytes 1228808 | tf_op jit(solution)/shard_map/ppermute | solution.py:93
  681.4 118.7 %collective-permute-start.25 = (bf16[4,576,512]{2,1,0:T(8,128)(2,1)}, bf16[4,576,512]{2,1,0:T(8,128)(2,1)}, u32[]{:S(2)}, u32[]{:S(2)}) collective-permute-start(bf16[4,576,512]{2,1,0:T(8,128)(2,1)} %get-tuple-element.235), channel_id=1, source_target_pairs={{0,4},{4,0},{1,5},{5,1},{2,6},{6,2},{3,7},{7,3},{8,12},{12,8},{9,1... | collective-permute-start | bytes 7077896 | tf_op jit(solution)/shard_map/ppermute | solution.py:93
  696.2 115.3 %collective-permute-start.24 = (bf16[3840,512]{1,0:T(8,128)(2,1)}, bf16[3840,512]{1,0:T(8,128)(2,1)}, u32[]{:S(2)}, u32[]{:S(2)}) collective-permute-start(bf16[3840,512]{1,0:T(8,128)(2,1)} %sum_pass.8), channel_id=1, source_target_pairs={{0,8},{8,0},{16,24},{24,16},{1,9},{9,1},{17,25},{25,17},{2,10},{10... | collective-permute-start | bytes 11796488 | tf_op jit(solution)/shard_map/ppermute | solution.py:93
  703.0 108.5 %collective-permute-start.22 = (bf16[3840,512]{1,0:T(8,128)(2,1)}, bf16[3840,512]{1,0:T(8,128)(2,1)}, u32[]{:S(2)}, u32[]{:S(2)}) collective-permute-start(bf16[3840,512]{1,0:T(8,128)(2,1)} %sum_pass.7), channel_id=1, source_target_pairs={{0,16},{8,24},{16,0},{24,8},{1,17},{9,25},{17,1},{25,9},{2,18},{10... | collective-permute-start | bytes 11796488 | tf_op jit(solution)/shard_map/ppermute | solution.py:93
  798.6 50.3 %collective-permute-start.34 = (bf16[264,768]{1,0:T(8,128)(2,1)}, bf16[264,768]{1,0:T(8,128)(2,1)}, u32[]{:S(2)}, u32[]{:S(2)}) collective-permute-start(bf16[264,768]{1,0:T(8,128)(2,1)} %get-tuple-element.336), channel_id=1, source_target_pairs={{0,8},{8,0},{16,24},{24,16},{1,9},{9,1},{17,25},{25,17},{2,10},{10... | collective-permute-start | bytes 1216520 | tf_op jit(solution)/shard_map/ppermute | solution.py:93
  802.2 49.4 %collective-permute-start.30 = (bf16[576,512]{1,0:T(8,128)(2,1)}, bf16[576,512]{1,0:T(8,128)(2,1)}, u32[]{:S(2)}, u32[]{:S(2)}) collective-permute-start(bf16[576,512]{1,0:T(8,128)(2,1)} %add_pass.6), channel_id=1, source_target_pairs={{0,8},{8,0},{16,24},{24,16},{1,9},{9,1},{17,25},{25,17},{2,10},{10... | collective-permute-start | bytes 1769480 | tf_op jit(solution)/shard_map/ppermute | solution.py:93
  819.4 46.4 %collective-permute-start.26 = (bf16[3840,512]{1,0:T(8,128)(2,1)}, bf16[3840,512]{1,0:T(8,128)(2,1)}, u32[]{:S(2)}, u32[]{:S(2)}) collective-permute-start(bf16[3840,512]{1,0:T(8,128)(2,1)} %sum_pass.9), channel_id=1, source_target_pairs={{0,4},{4,0},{1,5},{5,1},{2,6},{6,2},{3,7},{7,3},{8,12},{12,8},{9,1... | collective-permute-start | bytes 11796488 | tf_op jit(solution)/shard_map/ppermute | solution.py:93
  (108 other events, 1580.0 us)
Sparse Core Ops, SparseCore 0:
  95.7 88.4 all-gather.5
  187.1 94.1 all-reduce.9
  440.0 102.3 all-reduce.11
  552.9 58.0 all-reduce.13
  613.7 21.1 reduce-scatter.1
  641.9 145.2 all-reduce.15
  836.9 25.9 all-gather.7

commit v4 on v3

--- a/solution.py
+++ b/solution.py
@@ -138,6 +138,7 @@
 
 def gather_far(near, hold, height):
     chunks = [[((b, c), (b, CHUNKS + c)) for b in near] for c in range(CHUNKS)]
+    cut = []
     if lax.axis_size("dp") == 4:
         size = CHUNKS // GROUPS
         for group in range(GROUPS):
@@ -146,10 +147,11 @@
             two = lax.slice_in_dim(
                 after(near[1], hold), *[CHUNKS * height + r for r in rows], axis=0
             )
+            cut += [one, two]
             one, two = trade(one, "dp", 1), trade(two, "dp", 2)
             for n in range(size):
                 chunks[group * size + n].append(((one, n), (two, n)))
-    return chunks
+    return chunks, cut
 
 
 def scatter_dp(parts, *last):
@@ -1250,8 +1252,9 @@
             ((row_count, model_width + rank), BF16),
         ],
     )
-    chunks = gather_far(near, flat_heads, height)
+    chunks, cut = gather_far(near, flat_heads, height)
     branch_sum = lax.psum(branch_part, "mp")
+    branch_sum = after(branch_sum, *cut)
     rank_out = branch_sum[:, model_width:]
 
     hidden_state, normed_own = simple_pass(

time: 911 us -> 904 us (level)
    psum x1, waiting for transfers between devices: 85.4 us -> 5.91 us  [local(): branch_sum = lax.psum(branch_part, 'mp')]
    ppermute x40, waiting for transfers between devices: 106 us -> 177 us  [trade(): return lax.ppermute(block, axis, [(i, i ^ mask) for i in range(count)])]
    unnamed x173 -> x179, local copies, waits for them, and re-layouts: 38.9 us -> 39.8 us
  transfers between devices with their start and end apart: 47 -> 47, of which waited for: 18 -> 21; matrix products, arithmetic and copies ran while one was open for 7% -> 7% of each run, Pallas kernels for 34% -> 34%
where the time goes in v4:
time: 904 us; the launch traced here: 894 us
  waiting for transfers between devices  367 us (41%)
  Pallas kernels  354 us (39%)
  local copies, waits for them, and re-layouts  62 us (7%)
  other arithmetic  36.4 us (4%)
  starting transfers between devices  29.2 us (3%)
  blocking collectives  23 us (3%)
  between operations  16.4 us (2%)
    ppermute x40, waiting for transfers between devices, trade(): return lax.ppermute(block, axis, [(i, i ^ mask) for i in range(count)])  177 us
    pallas_call x16, Pallas kernels, weight_pass(): pl.pallas_call(functools.partial(weight_kernel, part, rank_part, tuple((i...  91.7 us
    psum x1, waiting for transfers between devices, local(): grad_norm_one, ffn_last = lax.psum((grad_norm_part, ffn_last), 'mp')  82.9 us
    pallas_call x2, Pallas kernels, gate_pass(): pl.pallas_call(functools.partial(gate_kernel, len(chunks[0]), width, rank...  77.1 us
    pallas_call x9, Pallas kernels, simple_pass(): pl.pallas_call(kernel, grid=(1,), in_specs=specs, out_specs=[whole_spec(s...  66.4 us
    unnamed x179, local copies, waits for them, and re-layouts  39.8 us
    psum x1, waiting for transfers between devices, local(): ffn_first = lax.psum(ffn_first, 'mp')  37.1 us
    all_gather x1, waiting for transfers between devices, local(): lax.all_gather(late, 'mp', axis=0, tiled=False)  34.9 us
  transfers between devices with their start and end apart: 47, of which 21 were waited for; matrix products, arithmetic and copies ran while one was open for 7% of the time, Pallas kernels for 34%

profile of v4, /device:TPU:0, one launch (start us, length us, event | category | flops | bytes accessed | tf_op | source)
XLA Modules:
  0.0 893.9 jit_solution(18357292359223840160)
XLA Ops:
  40.4 6.7 bundle_pass.1
  49.1 16.2 %collective-permute-done.2.refs_3_ = bf16[656,640]{1,0:T(8,128)(2,1)} collective-permute-done((bf16[656,640]{1,0:T(8,128)(2,1)}, bf16[656,640]{1,0:T(8,128)(2,1)}, u32[]{:S(2)}, u32[]{:S(2)}) %collective-permute-start.2) | collective-permute-done | bytes 839712 | tf_op jit(solution)/shard_map/ppermute | solution.py:93
  70.3 17.3 %collective-permute-done.8.refs_7_ = bf16[656,640]{1,0:T(8,128)(2,1)S(1)} collective-permute-done((bf16[656,640]{1,0:T(8,128)(2,1)}, bf16[656,640]{1,0:T(8,128)(2,1)S(1)}, u32[]{:S(2)}, u32[]{:S(2)}) %collective-permute-start.8) | collective-permute-done | bytes 839712 | tf_op jit(solution)/shard_map/ppermute | solution.py:93
  107.1 10.2 %project_pass.1 = (bf16[512,2048]{1,0:T(8,128)(2,1)}, bf16[512,768]{1,0:T(8,128)(2,1)S(1)}, bf16[512,512]{1,0:T(8,128)(2,1)S(1)}, bf16[512,128]{1,0:T(8,128)(2,1)S(1)}) custom-call(s32[6]{0:T(128)S(1)} %stack.65.place, bf16[512,2048]{1,0:T(8,128)(2,1)} %maximum_select_fusion.1.rows, bf16[16,2048]{1,0:T(8,128)(2,1)S(1)} %get-tuple-element.144.gains, ...), custom_call_target="tpu_custom_call" | custom-call | flops 1 | bytes 1 | tf_op jit(solution)/shard_map/project_pass/pallas_call | solution.py:499
  118.2 23.0 %all-gather = bf16[2048,128]{1,0:T(8,128)(2,1)S(1)} all-gather(bf16[512,128]{1,0:T(8,128)(2,1)S(1)} %get-tuple-element.149), channel_id=2, replica_groups=mesh['dp'=4,'depth'=2,'mp'=4] {'mp'}, dimensions={0}, use_global_device_ids=true | all-gather | bytes 655360 | tf_op jit(solution)/shard_map/all_gather | solution.py:1243
  148.1 34.9 %all-gather.6.cloned.1.call-done = bf16[16,512,256]{2,1,0:T(8,128)(2,1)} async-done(((bf16[4,512,256]{2,1,0:T(8,128)(2,1)}), bf16[16,512,256]{2,1,0:T(8,128)(2,1)}) %all-gather.6.cloned.1.call-update) | async-done | bytes 4194320 | tf_op jit(solution)/shard_map/all_gather | solution.py:1217
  194.7 70.7 %collective-permute-done.11.refs_6_.refs_7_.refs_14_.refs_15_.refs_22_.refs_23_.refs_30_.refs_31_ = bf16[7680,512]{1,0:T(8,128)(2,1)} collective-permute-done((bf16[7680,512]{1,0:T(8,128)(2,1)}, bf16[7680,512]{1,0:T(8,128)(2,1)}, u32[]{:S(2)}, u32[]{:S(2)}) %collective-permute-start.11) | collective-permute-done | bytes 7864352 | tf_op jit(solution)/shard_map/ppermute | solution.py:93
  281.8 7.1 second_pass.1
  293.0 7.5 turn_pass.2.refs_4_.refs_7_.refs_9_.refs_12_
  300.4 34.2 %collective-permute-done.15.refs_11_.refs_19_ = bf16[1920,512]{1,0:T(8,128)(2,1)} collective-permute-done((bf16[1920,512]{1,0:T(8,128)(2,1)S(1)}, bf16[1920,512]{1,0:T(8,128)(2,1)}, u32[]{:S(2)}, u32[]{:S(2)}) %collective-permute-start.15) | collective-permute-done | bytes 1966112 | tf_op jit(solution)/shard_map/ppermute | solution.py:93
  337.7 37.5 %gate_pass.2 = (bf16[1024,1024]{1,0:T(8,128)(2,1)}, bf16[1024,1024]{1,0:T(8,128)(2,1)}, bf16[1024,1024]{1,0:T(8,128)(2,1)}, bf16[512,2560]{1,0:T(8,128)(2,1)}, bf16[512,2560]{1,0:T(8,128)(2,1)}) custom-call(bf16[512,2560]{1,0:T(8,128)(2,1)} %get-tuple-element.173.refs_0_.own.refs_2_, bf16[512,2560]{1,0:T(8,128)(2,1)} %copy-done.63, ...), custom_call_target="tpu_custom_call" | custom-call | flops 1 | bytes 1 | tf_op jit(solution)/shard_map/gate_pass/pallas_call | solution.py:843
  377.5 39.6 %gate_pass.3 = (bf16[1024,1024]{1,0:T(8,128)(2,1)}, bf16[1024,1024]{1,0:T(8,128)(2,1)}, bf16[1024,1024]{1,0:T(8,128)(2,1)}, f32[512,2560]{1,0:T(8,128)}, bf16[512,2560]{1,0:T(8,128)(2,1)}) custom-call(bf16[512,2560]{1,0:T(8,128)(2,1)} %get-tuple-element.173.refs_0_.own.refs_2_, bf16[512,2560]{1,0:T(8,128)(2,1)} %copy-done.63, ...), custom_call_target="tpu_custom_call" | custom-call | flops 1 | bytes 1 | tf_op jit(solution)/shard_map/gate_pass/pallas_call | solution.py:843
  432.8 8.4 turn_pass.3.refs_3_.refs_5_.refs_6_.refs_8_.refs_10_.refs_11_
  487.1 23.3 %down_pass.1 = (f32[512,2304]{1,0:T(8,128)}, bf16[512,2304]{1,0:T(8,128)(2,1)}) custom-call(bf16[1024,1024]{1,0:T(8,128)(2,1)} %get-tuple-element.193.refs_2_.refs_0_.refs_1_, bf16[1024,1024]{1,0:T(8,128)(2,1)} %get-tuple-element.193.refs_2_.refs_0_.refs_1_, bf16[1024,1024]{1,0:T(8,128)(2,1)} %get-tuple-element.194.refs_2_.refs_3_, ...), custom_call_target="tpu_custom_call" | custom-call | flops 1 | bytes 1 | tf_op jit(solution)/shard_map/down_pass/pallas_call | solution.py:905
  549.7 14.1 %attend_back_pass.1 = (f32[512,2048]{1,0:T(8,128)}, bf16[512,2048]{1,0:T(8,128)(2,1)}, bf16[512,512]{1,0:T(8,128)(2,1)S(1)}, bf16[512,256]{1,0:T(8,128)(2,1)S(1)...) custom-call(s32[6]{0:T(128)S(1)} %copy-done.57, ...), custom_call_target="tpu_custom_call" | custom-call | flops 100000000376832 | bytes 1 | tf_op jit(solution)/shard_map/attend_back_pass/pallas_call | solution.py:499
  566.8 37.1 %all-reduce.14.cloned.1.call-done = bf16[256,2560]{1,0:T(8,128)(2,1)} async-done(((bf16[256,2560]{1,0:T(8,128)(2,1)}), bf16[256,2560]{1,0:T(8,128)(2,1)}) %all-reduce.14.cloned.1.call-update) | async-done | bytes 1310736 | tf_op jit(solution)/shard_map/psum | solution.py:1342
  603.9 23.8 %reduce-scatter.2.cloned.1.call-done = bf16[1,512,128]{2,1,0:T(8,128)(2,1)} async-done(((bf16[4,512,128]{2,1,0:T(8,128)(2,1)}), bf16[1,512,128]{2,1,0:T(8,128)(2,1)}) %reduce-scatter.2.cloned.1.call-update) | async-done | bytes 131088 | tf_op jit(solution)/shard_map/reduce_scatter | solution.py:1368
  661.3 10.7 %shares_pass.1 = (bf16[4,576,512]{2,1,0:T(8,128)(2,1)}, bf16[4,576,512]{2,1,0:T(8,128)(2,1)}, bf16[400,512]{1,0:T(8,128)(2,1)S(1)}, bf16[400,512]{1,0:T(8,128)(2...) custom-call(s32[6]{0:T(128)S(1)} %copy-done.57, bf16[512,2048]{1,0:T(8,128)(2,1)} %get-tuple-element.230.normed, ...), custom_call_target="tpu_custom_call" | custom-call | flops 1 | bytes 1 | tf_op jit(solution)/shard_map/shares_pass/pallas_call | solution.py:499
  674.2 9.0 %collective-permute-done.23.refs_1_ = bf16[7680,512]{1,0:T(8,128)(2,1)} collective-permute-done((bf16[7680,512]{1,0:T(8,128)(2,1)}, bf16[7680,512]{1,0:T(8,128)(2,1)}, u32[]{:S(2)}, u32[]{:S(2)}) %collective-permute-start.23) | collective-permute-done | bytes 7864352 | tf_op jit(solution)/shard_map/ppermute | solution.py:93
  697.2 82.9 %all-reduce.16.cloned.1.call-done = (bf16[256,2048]{1,0:T(8,128)(2,1)}, bf16[512,2816]{1,0:T(8,128)(2,1)}) async-done(((bf16[256,2048]{1,0:T(8,128)(2,1)}, bf16[512,2816]{1,0:T(8,128)(2,1)}), (bf16[256,2048]{1,0:T(8,128)(2,1)}, bf16[512,2816]{1,0:T(8,128)(2,1)})) %all-reduce.16.cloned.1.call-update) | async-done | bytes 3932176 | tf_op jit(solution)/shard_map/psum | solution.py:1382
  780.1 8.4 first_back_pass.1
  804.3 7.9 sum_pass.9
  819.4 8.7 collective-permute-done.38.refs_1_
  860.5 12.5 %finish_pass.1 = (f32[2,256,4096]{2,1,0:T(8,128)}, f32[4096,256]{1,0:T(8,128)}, f32[1,2,64,4096]{3,2,1,0:T(8,128)}, f32[1,64,4096]{2,1,0:T(8,128)}) custom-call(s32[1]{0:T(128)} %bitcast.3.core, bf16[3840,512]{1,0:T(8,128)(2,1)S(1)} %copy-done.5, bf16[7680,512]{1,0:T(8,128)(2,1)} %collective-permute-done.21.refs_1_, ...), custom_call_target="tpu_custom_call" | custom-call | flops 1 | bytes 1 | tf_op jit(solution)/shard_map/finish_pass/pallas_call | solution.py:1123
  (378 shorter events, 326.1 us)
Async XLA Ops:
  7.2 175.8 %all-gather.6.cloned.1.call-start = ((), (), s32[]{:S(2)}) async-start(), calls=%async_computation.5 | async-start | bytes 5242880 | tf_op jit(solution)/shard_map/all_gather | solution.py:1217
  20.7 49.6 %collective-permute-start.1 = (bf16[688,768]{1,0:T(8,128)(2,1)}, bf16[688,768]{1,0:T(8,128)(2,1)}, u32[]{:S(2)}, u32[]{:S(2)}) collective-permute-start(bf16[688,768]{1,0:T(8,128)(2,1)} %get-tuple-element.140.refs_0_), channel_id=1, source_target_pairs={{0,8},{8,0},{16,24},{24,16},{1,9},{9,1},{17,25},{25,17},{2,10},{10... | collective-permute-start | bytes 3170312 | tf_op jit(solution)/shard_map/ppermute | solution.py:93
  94.4 185.8 %all-reduce.10.cloned.1.call-start = ((), (), s32[]{:S(2)}) async-start(), calls=%async_computation.1 | async-start | bytes 4718592 | tf_op jit(solution)/shard_map/psum | solution.py:1256
  94.5 170.9 %collective-permute-start.11 = (bf16[7680,512]{1,0:T(8,128)(2,1)}, bf16[7680,512]{1,0:T(8,128)(2,1)}, u32[]{:S(2)}, u32[]{:S(2)}) collective-permute-start(bf16[7680,512]{1,0:T(8,128)(2,1)} %bitcast.106), channel_id=1, source_target_pairs={{0,8},{8,0},{16,24},{24,16},{1,9},{9,1},{17,25},{25,17},{2,10},{10... | collective-permute-start | bytes 23592968 | tf_op jit(solution)/shard_map/ppermute | solution.py:93
  95.1 170.5 %collective-permute-start.10 = (bf16[7680,512]{1,0:T(8,128)(2,1)}, bf16[7680,512]{1,0:T(8,128)(2,1)}, u32[]{:S(2)}, u32[]{:S(2)}) collective-permute-start(bf16[7680,512]{1,0:T(8,128)(2,1)} %bitcast.107), channel_id=1, source_target_pairs={{0,16},{8,24},{16,0},{24,8},{1,17},{9,25},{17,1},{25,9},{2,18},{10... | collective-permute-start | bytes 23592968 | tf_op jit(solution)/shard_map/ppermute | solution.py:93
  194.7 97.8 %collective-permute-start.12 = (bf16[512,2304]{1,0:T(8,128)(2,1)}, bf16[512,2304]{1,0:T(8,128)(2,1)}, u32[]{:S(2)}, u32[]{:S(2)}) collective-permute-start(bf16[512,2304]{1,0:T(8,128)(2,1)} %grad_pass.1.own.refs_2_), channel_id=1, source_target_pairs={{0,4},{4,0},{1,5},{5,1},{2,6},{6,2},{3,7},{7,3},{8,12},{12,8},{9,1... | collective-permute-start | bytes 7077896 | tf_op jit(solution)/shard_map/ppermute | solution.py:93
  288.9 47.3 %collective-permute-start.13 = (bf16[512,2560]{1,0:T(8,128)(2,1)}, bf16[512,2560]{1,0:T(8,128)(2,1)S(1)}, u32[]{:S(2)}, u32[]{:S(2)}) collective-permute-start(bf16[512,2560]{1,0:T(8,128)(2,1)} %get-tuple-element.173.refs_0_.own.refs_2_), channel_id=1, source_target_pairs={{0,4},{4,0},{1,5},{5,1},{2,6},{6,2},{3,7},{7,3},{8,12},{12,8},{9,1... | collective-permute-start | bytes 7864328 | tf_op jit(solution)/shard_map/ppermute | solution.py:93
  288.9 45.8 %collective-permute-start.15 = (bf16[1920,512]{1,0:T(8,128)(2,1)S(1)}, bf16[1920,512]{1,0:T(8,128)(2,1)}, u32[]{:S(2)}, u32[]{:S(2)}) collective-permute-start(bf16[1920,512]{1,0:T(8,128)(2,1)S(1)} %copy-done.77), channel_id=1, source_target_pairs={{0,16},{8,24},{16,0},{24,8},{1,17},{9,25},{17,1},{25,9},{2,18},{10... | collective-permute-start | bytes 5898248 | tf_op jit(solution)/shard_map/ppermute | solution.py:93
  291.9 84.5 %collective-permute-start.17 = (bf16[1920,512]{1,0:T(8,128)(2,1)}, bf16[1920,512]{1,0:T(8,128)(2,1)}, u32[]{:S(2)}, u32[]{:S(2)}) collective-permute-start(bf16[1920,512]{1,0:T(8,128)(2,1)} %get-tuple-element.329), channel_id=1, source_target_pairs={{0,16},{8,24},{16,0},{24,8},{1,17},{9,25},{17,1},{25,9},{2,18},{10... | collective-permute-start | bytes 5898248 | tf_op jit(solution)/shard_map/ppermute | solution.py:93
  292.4 85.1 %collective-permute-start.16 = (bf16[1920,512]{1,0:T(8,128)(2,1)}, bf16[1920,512]{1,0:T(8,128)(2,1)}, u32[]{:S(2)}, u32[]{:S(2)}) collective-permute-start(bf16[1920,512]{1,0:T(8,128)(2,1)} %get-tuple-element.331), channel_id=1, source_target_pairs={{0,8},{8,0},{16,24},{24,16},{1,9},{9,1},{17,25},{25,17},{2,10},{10... | collective-permute-start | bytes 5898248 | tf_op jit(solution)/shard_map/ppermute | solution.py:93
  430.0 115.5 %all-reduce.12.cloned.1.call-start = ((), (), s32[]{:S(2)}) async-start(), calls=%async_computation.2 | async-start | bytes 5242880 | tf_op jit(solution)/shard_map/psum | solution.py:1294
  430.7 173.1 %all-reduce.14.cloned.1.call-start = ((), (), s32[]{:S(2)}) async-start(), calls=%async_computation.3 | async-start | bytes 2621440 | tf_op jit(solution)/shard_map/psum | solution.py:1342
  510.9 172.4 %collective-permute-start.23 = (bf16[7680,512]{1,0:T(8,128)(2,1)}, bf16[7680,512]{1,0:T(8,128)(2,1)}, u32[]{:S(2)}, u32[]{:S(2)}) collective-permute-start(bf16[7680,512]{1,0:T(8,128)(2,1)} %get-tuple-element.192), channel_id=1, source_target_pairs={{0,16},{8,24},{16,0},{24,8},{1,17},{9,25},{17,1},{25,9},{2,18},{10... | collective-permute-start | bytes 23592968 | tf_op jit(solution)/shard_map/ppermute | solution.py:93
  511.4 179.1 %collective-permute-start.21 = (bf16[7680,512]{1,0:T(8,128)(2,1)}, bf16[7680,512]{1,0:T(8,128)(2,1)}, u32[]{:S(2)}, u32[]{:S(2)}) collective-permute-start(bf16[7680,512]{1,0:T(8,128)(2,1)} %get-tuple-element.191), channel_id=1, source_target_pairs={{0,8},{8,0},{16,24},{24,16},{1,9},{9,1},{17,25},{25,17},{2,10},{10... | collective-permute-start | bytes 23592968 | tf_op jit(solution)/shard_map/ppermute | solution.py:93
  545.5 82.2 %reduce-scatter.2.cloned.1.call-start = ((), (), s32[]{:S(2)}) async-start(), calls=%async_computation.4 | async-start | bytes 655360 | tf_op jit(solution)/shard_map/reduce_scatter | solution.py:1368
  603.9 176.2 %all-reduce.16.cloned.1.call-start = ((), (), s32[]{:S(2)}) async-start(), calls=%async_computation.7 | async-start | bytes 7864320 | tf_op jit(solution)/shard_map/psum | solution.py:1382
  634.6 221.1 %all-gather.8.cloned.1.call-start = ((), (), s32[]{:S(2)}) async-start(), calls=%async_computation.6 | async-start | bytes 1310720 | tf_op jit(solution)/shard_map/all_gather | solution.py:1484
  672.7 141.2 %collective-permute-start.37 = (bf16[400,512]{1,0:T(8,128)(2,1)}, bf16[400,512]{1,0:T(8,128)(2,1)}, u32[]{:S(2)}, u32[]{:S(2)}) collective-permute-start(bf16[400,512]{1,0:T(8,128)(2,1)} %get-tuple-element.257), channel_id=1, source_target_pairs={{0,16},{8,24},{16,0},{24,8},{1,17},{9,25},{17,1},{25,9},{2,18},{10... | collective-permute-start | bytes 1228808 | tf_op jit(solution)/shard_map/ppermute | solution.py:93
  674.2 118.7 %collective-permute-start.25 = (bf16[4,576,512]{2,1,0:T(8,128)(2,1)}, bf16[4,576,512]{2,1,0:T(8,128)(2,1)}, u32[]{:S(2)}, u32[]{:S(2)}) collective-permute-start(bf16[4,576,512]{2,1,0:T(8,128)(2,1)} %get-tuple-element.237), channel_id=1, source_target_pairs={{0,4},{4,0},{1,5},{5,1},{2,6},{6,2},{3,7},{7,3},{8,12},{12,8},{9,1... | collective-permute-start | bytes 7077896 | tf_op jit(solution)/shard_map/ppermute | solution.py:93
  689.0 115.2 %collective-permute-start.24 = (bf16[3840,512]{1,0:T(8,128)(2,1)}, bf16[3840,512]{1,0:T(8,128)(2,1)}, u32[]{:S(2)}, u32[]{:S(2)}) collective-permute-start(bf16[3840,512]{1,0:T(8,128)(2,1)} %sum_pass.8), channel_id=1, source_target_pairs={{0,8},{8,0},{16,24},{24,16},{1,9},{9,1},{17,25},{25,17},{2,10},{10... | collective-permute-start | bytes 11796488 | tf_op jit(solution)/shard_map/ppermute | solution.py:93
  696.7 107.6 %collective-permute-start.22 = (bf16[3840,512]{1,0:T(8,128)(2,1)}, bf16[3840,512]{1,0:T(8,128)(2,1)}, u32[]{:S(2)}, u32[]{:S(2)}) collective-permute-start(bf16[3840,512]{1,0:T(8,128)(2,1)} %sum_pass.7), channel_id=1, source_target_pairs={{0,16},{8,24},{16,0},{24,8},{1,17},{9,25},{17,1},{25,9},{2,18},{10... | collective-permute-start | bytes 11796488 | tf_op jit(solution)/shard_map/ppermute | solution.py:93
  791.4 50.3 %collective-permute-start.34 = (bf16[264,768]{1,0:T(8,128)(2,1)}, bf16[264,768]{1,0:T(8,128)(2,1)}, u32[]{:S(2)}, u32[]{:S(2)}) collective-permute-start(bf16[264,768]{1,0:T(8,128)(2,1)} %get-tuple-element.338), channel_id=1, source_target_pairs={{0,8},{8,0},{16,24},{24,16},{1,9},{9,1},{17,25},{25,17},{2,10},{10... | collective-permute-start | bytes 1216520 | tf_op jit(solution)/shard_map/ppermute | solution.py:93
  795.0 49.4 %collective-permute-start.30 = (bf16[576,512]{1,0:T(8,128)(2,1)}, bf16[576,512]{1,0:T(8,128)(2,1)}, u32[]{:S(2)}, u32[]{:S(2)}) collective-permute-start(bf16[576,512]{1,0:T(8,128)(2,1)} %add_pass.6), channel_id=1, source_target_pairs={{0,8},{8,0},{16,24},{24,16},{1,9},{9,1},{17,25},{25,17},{2,10},{10... | collective-permute-start | bytes 1769480 | tf_op jit(solution)/shard_map/ppermute | solution.py:93
  812.2 46.4 %collective-permute-start.26 = (bf16[3840,512]{1,0:T(8,128)(2,1)}, bf16[3840,512]{1,0:T(8,128)(2,1)}, u32[]{:S(2)}, u32[]{:S(2)}) collective-permute-start(bf16[3840,512]{1,0:T(8,128)(2,1)} %sum_pass.9), channel_id=1, source_target_pairs={{0,4},{4,0},{1,5},{5,1},{2,6},{6,2},{3,7},{7,3},{8,12},{12,8},{9,1... | collective-permute-start | bytes 11796488 | tf_op jit(solution)/shard_map/ppermute | solution.py:93
  (111 other events, 1694.4 us)
Sparse Core Ops, SparseCore 0:
  94.5 88.4 all-gather.5
  186.0 94.1 all-reduce.9
  433.2 102.2 all-reduce.11
  545.7 58.1 all-reduce.13
  606.5 21.1 reduce-scatter.1
  634.7 145.2 all-reduce.15
  829.7 25.9 all-gather.7
